TPU v7x, 32 devices: a whole 2x2x4 slice. The times are simulated.
32 devices in a mesh: ctx: 8 (over z, x), tp: 4 (over y, core).
Axes of the slice: x: 2, y: 2, z: 4, core: 2. Of those that a mesh axis runs over, the one named last changes fastest.
Arguments:
- tokens: bfloat16 [2048, 8192], P('ctx'), may hold values from -6 to 6
- select_index: int32 [256], P('ctx'), may hold values from 0 to 255, as said below
- valid_count: int32 [8], replicated, may hold values from 4 to 32, as said below
- queries: bfloat16 [256, 4096], P('ctx', 'tp'), may hold values from -160 to 160
- key_matrix: bfloat16 [8192, 512], P('ctx', 'tp'), may hold values from -0.0625 to 0.0625
- value_matrix: bfloat16 [8192, 512], P('ctx', 'tp'), may hold values from -0.0625 to 0.0625
- out_grad: bfloat16 [256, 4096], P('ctx', 'tp'), may hold values from -6 to 6
Outputs:
- attended: bfloat16 [256, 4096], P('ctx', 'tp')
- query_gradient: bfloat16 [256, 4096], P('ctx', 'tp')
- token_grad: bfloat16 [2048, 8192], P('ctx', 'tp')
- key_weight_grad: bfloat16 [8192, 512], P('ctx', 'tp')
- value_weight_grad: bfloat16 [8192, 512], P('ctx', 'tp')
Inputs may be any that keep to these rules, and one draw needn't show every extreme that they name: `select_index`: within one shard the offsets of all 32 slots are distinct, and those of the first valid_count slots rise. `valid_count`: some shard holds exactly 32 live slots.
All inputs are finite; a program needn't handle non-finite values.
Results may differ from a plain program's by a relative error of at most 0.023.
The roundings to bfloat16 on the way count: a program that leaves them out, or rounds other values in their place, can miss the bound.
Values may be sent and summed in bfloat16 or wider, within the bound.
No kernel may reach another device: no remote copies, remote signals or barrier semaphores. Data moves between devices by JAX's collectives and lax.ppermute only.
A program may use at most 64 MiB of HBM per device.

v0:
```python
import math

import jax
import jax.numpy as jnp
from jax import lax
from jax.sharding import PartitionSpec as P

HEAD_WIDTH = 128


neg_large = -1e30


def local(tokens, select_index, valid_count, queries, key_matrix, value_matrix, out_grad):
    shard_len = tokens.shape[0]
    capacity = select_index.shape[0]
    key_value_width = key_matrix.shape[1]
    kv_local = key_value_width // HEAD_WIDTH
    per_group = queries.shape[1] // key_value_width
    ctx_size = lax.axis_size("ctx")
    own_shard = lax.axis_index("ctx")
    all_keys = ctx_size * capacity
    block_len = min(512, all_keys)
    num_blocks = all_keys // block_len
    score_scale = 1.0 / math.sqrt(HEAD_WIDTH)
    slot_ids = jnp.arange(capacity, dtype=jnp.int32)
    own_count = jnp.sum(
        jnp.where(jnp.arange(ctx_size, dtype=jnp.int32) == own_shard, valid_count, 0)
    )
    live_query = slot_ids < own_count
    query_pos = jnp.where(live_query, select_index, shard_len)
    key_shard = jnp.arange(all_keys, dtype=jnp.int32) // capacity
    key_live = (slot_ids[None, :] < valid_count[:, None]).reshape(all_keys)
    key_pos = jnp.tile(select_index, ctx_size)
    picked = jnp.take(tokens, select_index, axis=0)
    weight_key, weight_value = (
        lax.all_gather(key_matrix, "ctx", axis=0, tiled=True),
        lax.all_gather(value_matrix, "ctx", axis=0, tiled=True),
    )
    both_weights = jnp.concatenate([weight_key, weight_value], axis=1)
    projected = jnp.dot(picked, both_weights, preferred_element_type=jnp.float32).astype(
        jnp.bfloat16
    )
    kv_rows = lax.all_gather(projected, "ctx", axis=0, tiled=True)
    heads_of_query = queries.reshape(capacity, kv_local, per_group, HEAD_WIDTH)
    gradient_rows = jnp.where(live_query[:, None], out_grad, jnp.zeros_like(out_grad))
    gradient_heads = gradient_rows.reshape(capacity, kv_local, per_group, HEAD_WIDTH)
    stat_shape = (kv_local, per_group, capacity)

    def block_data(blk_id):
        leading_item = blk_id * block_len
        kv_blk = lax.dynamic_slice_in_dim(kv_rows, leading_item, block_len, 0)
        key_block = kv_blk[:, :key_value_width].reshape(block_len, kv_local, HEAD_WIDTH)
        value_block = kv_blk[:, key_value_width:].reshape(block_len, kv_local, HEAD_WIDTH)
        live_blk = lax.dynamic_slice_in_dim(key_live, leading_item, block_len, 0)
        shard_blk = lax.dynamic_slice_in_dim(key_shard, leading_item, block_len, 0)
        pos_blk = lax.dynamic_slice_in_dim(key_pos, leading_item, block_len, 0)
        same_shard = (shard_blk[None, :] == own_shard) & (pos_blk[None, :] <= query_pos[:, None])
        visible = live_blk[None, :] & ((shard_blk[None, :] < own_shard) | same_shard)
        active = leading_item // capacity <= own_shard
        return (key_block, value_block, visible, active)

    def block_scores(key_block, visible):
        scores = (
            jnp.einsum(
                "toul,iol->outi", heads_of_query, key_block, preferred_element_type=jnp.float32
            )
            * score_scale
        )
        return jnp.where(visible[None, None], scores, neg_large)

    def max_step(carried, blk_id):
        row_max, row_sum = carried
        key_block, value_block, visible, active = block_data(blk_id)

        def max_visit():
            scores = block_scores(key_block, visible)
            new_max = jnp.maximum(row_max, jnp.max(scores, axis=-1))
            terms = jnp.where(visible[None, None], jnp.exp(scores - new_max[..., None]), 0.0)
            new_sum = row_sum * jnp.exp(row_max - new_max) + jnp.sum(terms, axis=-1)
            return ((new_max, new_sum), scores)

        def max_ignore():
            return ((row_max, row_sum), jnp.full(stat_shape + (block_len,), neg_large, jnp.float32))

        stats, scores = lax.cond(active, max_visit, max_ignore)
        return (stats, None)

    start_stats = (jnp.full(stat_shape, neg_large, jnp.float32), jnp.zeros(stat_shape, jnp.float32))
    block_ids = jnp.arange(num_blocks, dtype=jnp.int32)
    (row_max, row_sum), stored = lax.scan(max_step, start_stats, block_ids)
    log_total = row_max + jnp.log(row_sum)

    def get_scores(key_block, visible):
        return block_scores(key_block, visible)

    def out_step(output_acc, blk_id):
        key_block, value_block, visible, active = block_data(blk_id)

        def out_visit():
            probs = jnp.exp(get_scores(key_block, visible) - log_total[..., None])
            weight_matrices = probs.astype(jnp.bfloat16)
            return output_acc + jnp.einsum(
                "ljvo,olf->vljf", weight_matrices, value_block, preferred_element_type=jnp.float32
            )

        def out_ignore():
            return output_acc

        return (lax.cond(active, out_visit, out_ignore), None)

    head_shape = (capacity, kv_local, per_group, HEAD_WIDTH)
    output_acc, unused = lax.scan(out_step, jnp.zeros(head_shape, jnp.float32), block_ids)
    attended = jnp.where(live_query[:, None, None, None], output_acc, 0.0).astype(jnp.bfloat16)
    out_dot = jnp.transpose(
        jnp.sum(gradient_heads.astype(jnp.float32) * attended.astype(jnp.float32), axis=-1),
        (1, 2, 0),
    )

    def grad_step(query_acc, blk_id):
        key_block, value_block, visible, active = block_data(blk_id)

        def grad_visit():
            probs = jnp.exp(get_scores(key_block, visible) - log_total[..., None])
            weight_matrices = probs.astype(jnp.bfloat16)
            grad_probs = jnp.einsum(
                "toul,iol->outi", gradient_heads, value_block, preferred_element_type=jnp.float32
            )
            score_gradient = (probs * (grad_probs - out_dot[..., None]) * score_scale).astype(
                jnp.bfloat16
            )
            new_acc = query_acc + jnp.einsum(
                "ljvo,olf->vljf", score_gradient, key_block, preferred_element_type=jnp.float32
            )
            key_part = jnp.einsum(
                "cifh,fcij->hcj", score_gradient, heads_of_query, preferred_element_type=jnp.float32
            )
            value_part = jnp.einsum(
                "cifh,fcij->hcj",
                weight_matrices,
                gradient_heads,
                preferred_element_type=jnp.float32,
            )
            return (
                new_acc,
                jnp.concatenate(
                    [
                        key_part.reshape(block_len, key_value_width),
                        value_part.reshape(block_len, key_value_width),
                    ],
                    axis=1,
                ),
            )

        def grad_ignore():
            return (query_acc, jnp.zeros((block_len, 2 * key_value_width), jnp.float32))

        return lax.cond(active, grad_visit, grad_ignore)

    query_acc, kv_terms = lax.scan(grad_step, jnp.zeros(head_shape, jnp.float32), block_ids)
    query_gradient = query_acc.astype(jnp.bfloat16).reshape(
        capacity, kv_local * per_group * HEAD_WIDTH
    )
    kv_terms = kv_terms.reshape(all_keys, 2 * key_value_width)
    own_grads = lax.psum_scatter(kv_terms, "ctx", scatter_dimension=0, tiled=True).astype(
        jnp.bfloat16
    )
    owned_columns = lax.all_to_all(picked, "ctx", split_axis=1, concat_axis=0, tiled=True)
    weight_grad = lax.dot_general(
        owned_columns,
        lax.all_gather(own_grads, "ctx", axis=0, tiled=True),
        (((0,), (0,)), ((), ())),
        preferred_element_type=jnp.float32,
    )
    key_weight_grad = weight_grad[:, :key_value_width].astype(jnp.bfloat16)
    value_weight_grad = weight_grad[:, key_value_width:].astype(jnp.bfloat16)
    row_grad = lax.dot_general(
        own_grads, both_weights, (((1,), (1,)), ((), ())), preferred_element_type=jnp.float32
    )
    summed = lax.psum_scatter(row_grad, "tp", scatter_dimension=1, tiled=True)
    summed = jnp.where(live_query[:, None], summed, 0.0)
    token_grad = (
        jnp.zeros((shard_len, summed.shape[1]), jnp.float32)
        .at[select_index]
        .set(summed)
        .astype(jnp.bfloat16)
    )
    return (
        attended.reshape(capacity, kv_local * per_group * HEAD_WIDTH),
        query_gradient,
        token_grad,
        key_weight_grad,
        value_weight_grad,
    )


def solution(mesh):
    in_specs = (
        P("ctx", None),
        P("ctx"),
        P(),
        P("ctx", "tp"),
        P("ctx", "tp"),
        P("ctx", "tp"),
        P("ctx", "tp"),
    )
    out_specs = (P("ctx", "tp"), P("ctx", "tp"), P("ctx", "tp"), P("ctx", "tp"), P("ctx", "tp"))
    return jax.shard_map(local, mesh=mesh, in_specs=in_specs, out_specs=out_specs, check_vma=False)
```

profile of v0, /device:TPU:4, one launch (start us, length us, event | category | flops | bytes accessed | tf_op | source)
XLA Modules:
  0.0 266.7 jit_solution(6403213478916528648)
XLA Ops:
  8.0 0.7 all-gather.5.cloned.1.call-update
  8.7 1.3 fusion.56
  10.7 0.9 select_bitcast_fusion
  12.3 0.7 iota_compare_fusion
  13.2 0.9 copy.44
  14.0 1.3 compare_select_fusion
  15.3 4.1 %gather_fusion = bf16[32,8192]{1,0:T(8,128)(2,1)S(1)} fusion(bf16[256,8192]{1,0:T(8,128)(2,1)} %param.13, s32[1024]{0:T(1024)S(1)} %pad_clamp_fusion), kind=kCustom, calls=%fused_computation | custom fusion | bytes 1048704 | tf_op jit(solution)/shard_map/jit(_take)/gather | solution.py:35
  19.6 41.1 %all-gather.3.cloned.1.call-done = bf16[8192,128]{1,0:T(8,128)(2,1)} async-done(((bf16[1024,128]{1,0:T(8,128)(2,1)}), bf16[8192,128]{1,0:T(8,128)(2,1)}) %all-gather.3.cloned.1.call-update) | async-done | bytes 2097168 | tf_op jit(solution)/shard_map/all_gather | solution.py:37
  60.7 3.1 %constant_dynamic-update-slice_fusion.1 = bf16[8192,256]{1,0:T(8,128)(2,1)} fusion(bf16[8192,128]{1,0:T(8,128)(2,1)} %all-gather.3.cloned.1.call-done), kind=kLoop, calls=%fused_computation.80 | loop fusion | bytes 4194304
  63.8 46.8 %all-gather.5.cloned.1.call-done = bf16[8192,128]{1,0:T(8,128)(2,1)} async-done(((bf16[1024,128]{1,0:T(8,128)(2,1)}), bf16[8192,128]{1,0:T(8,128)(2,1)}) %all-gather.5.cloned.1.call-update) | async-done | bytes 2097168 | tf_op jit(solution)/shard_map/all_gather | solution.py:38
  110.6 3.1 %constant_dynamic-update-slice_fusion = bf16[8192,256]{1,0:T(8,128)(2,1)} fusion(bf16[8192,256]{1,0:T(8,128)(2,1)} %constant_dynamic-update-slice_fusion.1, bf16[8192,128]{1,0:T(8,128)(2,1)} %all-gather.5.cloned.1.call-done), kind=kLoop, calls=%fused_computation.79 | loop fusion | bytes 4194304 | tf_op jit(solution)/shard_map/concatenate | solution.py:40
  113.7 3.0 %convolution_convert_fusion.1 = bf16[32,256]{1,0:T(8,128)(2,1)S(1)} fusion(bf16[8192,256]{1,0:T(8,128)(2,1)} %constant_dynamic-update-slice_fusion, bf16[32,8192]{1,0:T(8,128)(2,1)S(1)} %gather_fusion, pred[32]{0:T(512)(128)(4,1)S(1)} %compare_and_fusion), kind=kOutput, calls=%fused_computation.60 | convolution fusion | flops 134488064 | bytes 4735008 | tf_op jit(solution)/shard_map/dot_general | solution.py:41
  116.7 30.5 %all_gather.14 = bf16[256,256]{1,0:T(8,128)(2,1)S(1)} all-gather(bf16[32,256]{1,0:T(8,128)(2,1)S(1)} %convolution_convert_fusion.1), channel_id=1, replica_groups=mesh['ctx'=8,'tp'=4] {'ctx'}, dimensions={0}, use_global_device_ids=true | all-gather | bytes 147456 | tf_op jit(solution)/shard_map/all_gather | solution.py:44
  148.4 1.1 conditional.5
  149.6 0.8 copy.38
  150.5 59.8 %reduce-scatter.7.cloned.1.call-done = f32[32,256]{1,0:T(8,128)} async-done(((f32[256,256]{1,0:T(8,128)}), f32[32,256]{1,0:T(8,128)}) %reduce-scatter.7.cloned.1.call-update) | async-done | bytes 32784
  210.3 0.9 copy.39
  211.1 4.5 %fusion.60 = f32[32,8192]{1,0:T(8,128)} fusion(bf16[32,256]{0,1:T(8,128)(2,1)S(1)} %copy.39, bf16[8192,256]{1,0:T(8,128)(2,1)} %constant_dynamic-update-slice_fusion), kind=kOutput, calls=%fused_computation.98 | convolution fusion | flops 134217728 | bytes 5259264 | tf_op jit(solution)/shard_map/dot_general | solution.py:177
  215.7 0.9 bitcast_select_fusion
  216.6 3.7 %all-to-all-start = ((bf16[32,8,1024]{2,0,1:T(8,128)(2,1)}), bf16[32,8,1024]{2,0,1:T(8,128)(2,1)S(1)}, u32[]{:S(2)}, u32[]{:S(2)}) async-start(bf16[32,8,1024]{2,0,1:T(8,128)(2,1)} %bitcast_select_fusion), calls=%async_computation.1 | async-start | bytes 1048576 | tf_op jit(solution)/shard_map/all_to_all | solution.py:168
  221.6 34.4 %all_gather.15 = bf16[256,256]{1,0:T(8,128)(2,1)S(1)} all-gather(bf16[32,256]{1,0:T(8,128)(2,1)S(1)} %copy.37), channel_id=1, replica_groups=mesh['ctx'=8,'tp'=4] {'ctx'}, dimensions={0}, use_global_device_ids=true | all-gather | bytes 147456 | tf_op jit(solution)/shard_map/all_gather | solution.py:171
  256.5 0.8 fusion.59
  257.3 1.8 scatter_custom_fusion
  259.1 1.1 convert_element_type.55
  (48 shorter events, 7.3 us)
Async XLA Ops:
  7.2 12.3 %copy-start = (s32[32]{0:T(128)S(1)}, s32[32]{0:T(128)}, u32[]{:S(2)}) copy-start(s32[32]{0:T(128)} %param.14) | copy-start | bytes 388
  7.2 53.5 %all-gather.3.cloned.1.call-start = ((), (), s32[]{:S(2)}) async-start(), calls=%async_computation.3 | async-start | bytes 2359296 | tf_op jit(solution)/shard_map/all_gather | solution.py:37
  7.9 102.7 %all-gather.5.cloned.1.call-start = ((), (), s32[]{:S(2)}) async-start(), calls=%async_computation.4 | async-start | bytes 2359296 | tf_op jit(solution)/shard_map/all_gather | solution.py:38
  8.7 201.6 %reduce-scatter.7.cloned.1.call-start = ((), (), s32[]{:S(2)}) async-start(), calls=%async_computation.6 | async-start | bytes 294912
  150.4 106.9 %reduce-scatter.5.cloned.1.call-start = ((), (), s32[]{:S(2)}) async-start(), calls=%async_computation.5 | async-start | bytes 1310720 | tf_op jit(solution)/shard_map/reduce_scatter | solution.py:180
  216.6 39.5 %all-to-all-start = ((bf16[32,8,1024]{2,0,1:T(8,128)(2,1)}), bf16[32,8,1024]{2,0,1:T(8,128)(2,1)S(1)}, u32[]{:S(2)}, u32[]{:S(2)}) async-start(bf16[32,8,1024]{2,0,1:T(8,128)(2,1)} %bitcast_select_fusion), calls=%async_computation.1 | async-start | bytes 1048576 | tf_op jit(solution)/shard_map/all_to_all | solution.py:168
Sparse Core Ops, SparseCore 0:
  10.1 50.4 all-gather.2
  62.8 47.7 all-gather.4
  150.5 59.6 reduce-scatter.6
  215.8 22.7 reduce-scatter.4
where the time goes:
time: 269 us; the launch traced here: 267 us
  waiting for transfers between devices  149 us (55%)
  blocking collectives  65 us (24%)
  local copies, waits for them, and re-layouts  16 us (6%)
  between operations  13.9 us (5%)
  matrix products  9.53 us (4%)
  other arithmetic  9.21 us (3%)
  starting transfers between devices  3.82 us (1%)
    unnamed x5, waiting for transfers between devices  61.2 us
    all_gather x1, waiting for transfers between devices, local(): lax.all_gather(value_matrix, 'ctx', axis=0, tiled=True)  46.8 us
    all_gather x1, waiting for transfers between devices, local(): lax.all_gather(key_matrix, 'ctx', axis=0, tiled=True)  41.1 us
    all_gather x1, blocking collectives, local(): lax.all_gather(own_grads, 'ctx', axis=0, tiled=True)  34.4 us
    all_gather x1, blocking collectives, local(): kv_rows = lax.all_gather(projected, 'ctx', axis=0, tiled=True)  30.5 us
    unnamed x9, local copies, waits for them, and re-layouts  7 us
  transfers between devices with their start and end apart: 5, of which 3 were waited for; matrix products, arithmetic and copies ran while one was open for 7% of the time, Pallas kernels for 0%

commit v1 on v0

v1 whole, which is shorter than its diff:
```python
import functools
import math

import jax
import jax.numpy as jnp
from jax import lax
from jax.experimental import pallas as pl
from jax.experimental.pallas import tpu as pltpu
from jax.sharding import PartitionSpec as P

HEAD = 128
NEG = -1e30
HIDDEN = 1 << 30
F32 = jnp.float32
BF16 = jnp.bfloat16


VMEM = pl.BlockSpec(memory_space=pltpu.VMEM)
SMEM = pl.BlockSpec(memory_space=pltpu.SMEM)
HBM = pl.BlockSpec(memory_space=pltpu.HBM)


def dot(x, y, cx, cy):
    return lax.dot_general(x, y, (((cx,), (cy,)), ((), ())), preferred_element_type=F32)


def place(inner):
    ctx = lax.axis_index("ctx")
    return ctx // inner, lax.rem(ctx, inner), lax.axis_index("tp")


def call(body, outs, in_specs, out_specs, scratch=(), cost=None, name=None):
    return pl.pallas_call(
        body,
        out_shape=outs,
        in_specs=in_specs,
        out_specs=out_specs,
        scratch_shapes=list(scratch),
        compiler_params=pltpu.CompilerParams(vmem_limit_bytes=48 * 2**20),
        cost_estimate=cost,
        name=name,
    )


def cost(flops, nbytes):
    return pl.CostEstimate(flops=int(flops), bytes_accessed=int(nbytes), transcendentals=0)


def one_hot(select_ref, limit, rows, width):
    at = lax.broadcasted_iota(jnp.int32, (rows, width), 0)
    wanted = jnp.full((rows, width), -1, jnp.int32)
    for j in range(rows):
        wanted = jnp.where((at == j) & (j < limit), select_ref[j], wanted)
    column = lax.broadcasted_iota(jnp.int32, (rows, width), 1)
    return jnp.where(column == wanted, 1.0, 0.0).astype(BF16)


def pick_body(
    size, inner, half, select_hbm, count_hbm, tokens_ref, q_ref, og_ref, k_ref, v_ref, *rest
):
    pairs = size // 2 - 1
    outs, (qd_ref, w_ref, hot_ref) = rest[: pairs + 2], rest[pairs + 2 : pairs + 5]
    select_ref, count_ref, buf, sems, side = rest[pairs + 5 :]
    a, b, t = place(inner)
    cap, rows = outs[0].shape[0], tokens_ref.shape[0]
    width = q_ref.shape[1]
    core = lax.rem(t, 2)
    first = [
        pltpu.make_async_copy(select_hbm, select_ref, side.at[0]),
        pltpu.make_async_copy(count_hbm, count_ref, side.at[1]),
    ]
    for c in first:
        c.start()
    starts = [(a ^ (2 * i + 1 + core)) * (2 * half) for i in range(pairs)]
    starts += [(a ^ (size - 1)) * (2 * half) + core * half, a * (2 * half)]
    copies = []
    for i, at in enumerate(starts):
        wide = outs[i].shape[1]
        copies.append(
            pltpu.make_async_copy(
                tokens_ref.at[:, pl.ds(pl.multiple_of(at, 128), wide)],
                buf.at[:, 2 * half * i : 2 * half * i + wide],
                sems.at[i],
            )
        )
        copies[i].start()
    others = [
        pltpu.make_async_copy(q_ref, qd_ref.at[:, :width], side.at[2]),
        pltpu.make_async_copy(og_ref, qd_ref.at[:, width:], side.at[3]),
        pltpu.make_async_copy(k_ref, w_ref.at[:, : k_ref.shape[1]], side.at[4]),
        pltpu.make_async_copy(v_ref, w_ref.at[:, k_ref.shape[1] :], side.at[5]),
    ]
    for c in others:
        c.start()
    for c in first:
        c.wait()
    hot = one_hot(select_ref, cap, cap, rows)
    slot = lax.broadcasted_iota(jnp.int32, (cap, rows), 0)
    live = slot < count_ref[a * inner + b]
    hot_ref[...] = jnp.where(live, hot.astype(F32), 0.0).astype(BF16)
    for i in range(len(starts)):
        copies[i].wait()
        wide = outs[i].shape[1]
        outs[i][...] = dot(hot, buf[:, 2 * half * i : 2 * half * i + wide], 1, 0).astype(BF16)
    for c in others:
        c.wait()


def project_body(size, inner, half, *refs):
    pairs = size // 2 - 1
    got, other_ref, own_ref, w_ref = refs[: pairs + 1], refs[pairs + 1], refs[pairs + 2], refs[pairs + 3]
    kv_refs = refs[pairs + 4 : pairs + 2 * inner + 2]
    outs = refs[pairs + 2 * inner + 2 :]
    part_ref, cols, ws, rows_ref = outs[0], outs[1 : inner + 1], outs[inner + 1 : 2 * inner], outs[-1]
    a, b, t = place(inner)
    cap = own_ref.shape[0]
    core = lax.rem(t, 2)

    def to(z):
        return pl.ds(pl.multiple_of(z * cap, cap), cap)

    def side(k):
        return pl.ds(pl.multiple_of(k * half, 128), half)

    rows_ref[to(a), :] = own_ref[...]
    for i in range(pairs):
        rows_ref[to(a ^ (2 * i + 1 + core)), :] = got[i][...]
        rows_ref[to(a ^ (2 * i + 2 - core)), :] = other_ref[:, 2 * half * i : 2 * half * (i + 1)]
    rows_ref[to(a ^ (size - 1)), side(core)] = got[pairs][...]
    rows_ref[to(a ^ (size - 1)), side(1 - core)] = other_ref[:, 2 * half * pairs :]
    depth, kv_width = w_ref.shape[0], w_ref.shape[1] // 2
    total = None
    for s in range(inner):
        part = rows_ref[:, pl.ds(pl.multiple_of((b ^ s) * depth, 128), depth)]
        cols[s][...] = part
        if s:
            ws[s - 1][:, :kv_width] = kv_refs[2 * s - 2][...]
            ws[s - 1][:, kv_width:] = kv_refs[2 * s - 1][...]
        term = dot(part, (ws[s - 1] if s else w_ref)[...], 1, 0)
        total = term if total is None else total + term
    part_ref[...] = total.astype(BF16)


def attend_body(size, inner, cap, group, count_ref, *refs):
    qds, kvs = refs[:size], refs[size : size + inner]
    att_ref, dq_ref = refs[size + inner : size + inner + 2]
    kept_ref = refs[size + inner + 2]
    sent = refs[size + inner + 3 : size + 2 * inner + 2]
    q_all, do_all = refs[size + 2 * inner + 2 :]
    a, b, t = place(inner)
    width = group * HEAD
    block = group * cap
    scale = 1.0 / math.sqrt(HEAD)
    slot = lax.broadcasted_iota(jnp.int32, (cap, HEAD), 0)
    for s in range(size):
        count = count_ref[(a ^ s) * inner + b]
        for g in range(group):
            to = slice(s * block + g * cap, s * block + (g + 1) * cap)
            q_all[to, :] = qds[s][:, g * HEAD : (g + 1) * HEAD]
            rows = qds[s][:, width + g * HEAD : width + (g + 1) * HEAD]
            do_all[to, :] = jnp.where(slot < count, rows.astype(F32), 0.0).astype(BF16)
    kv = jnp.concatenate([r[...] for r in kvs], axis=0)
    keys, values = kv[:, :HEAD], kv[:, HEAD:]
    keys_t = keys.astype(F32).T.astype(BF16)
    values_t = values.astype(F32).T.astype(BF16)
    row = lax.broadcasted_iota(jnp.int32, (cap, block), 0)
    pieces = []
    for s in range(inner):
        for z in range(size):
            shard = z * inner + (b ^ s)
            pieces.append(jnp.where(row < count_ref[shard], shard * cap + row, HIDDEN))
    key_at = jnp.concatenate(pieces, axis=0)
    column = lax.rem(lax.broadcasted_iota(jnp.int32, (1, block), 1), cap)
    dk = dv = None
    for s in range(size):
        shard = (a ^ s) * inner + b
        live = column < count_ref[shard]
        q = q_all[s * block : (s + 1) * block, :]
        do = do_all[s * block : (s + 1) * block, :]
        scores = dot(keys, q, 1, 1) * scale
        scores = jnp.where(key_at <= shard * cap + column, scores, NEG)
        terms = jnp.exp(scores - jnp.max(scores, axis=0, keepdims=True))
        probs = terms * (1.0 / jnp.sum(terms, axis=0, keepdims=True))
        weights = probs.astype(BF16)
        att = jnp.where(live, dot(values_t, weights, 1, 0), 0.0).astype(BF16).astype(F32)
        do_t = do.astype(F32).T
        out_dot = jnp.sum(do_t * att, axis=0, keepdims=True)
        grad_probs = dot(values, do, 1, 1)
        grad_scores = (probs * (grad_probs - out_dot) * scale).astype(BF16)
        k_term, v_term = dot(grad_scores, q, 1, 0), dot(weights, do, 1, 0)
        dk = k_term if dk is None else dk + k_term
        dv = v_term if dv is None else dv + v_term
        if s == 0:
            att_rows = att.T.astype(BF16)
            dq_rows = dot(keys_t, grad_scores, 1, 0).T.astype(BF16)
            for g in range(group):
                att_ref[:, g * HEAD : (g + 1) * HEAD] = att_rows[g * cap : (g + 1) * cap, :]
                dq_ref[:, g * HEAD : (g + 1) * HEAD] = dq_rows[g * cap : (g + 1) * cap, :]
    rows = size * cap
    kept_ref[:, :HEAD] = dk[:rows, :]
    kept_ref[:, HEAD:] = dv[:rows, :]
    for s in range(1, inner):
        sent[s - 1][:, :HEAD] = dk[s * rows : (s + 1) * rows, :].astype(BF16)
        sent[s - 1][:, HEAD:] = dv[s * rows : (s + 1) * rows, :].astype(BF16)


def total_body(inner, *refs):
    terms, grads_ref = refs[:inner], refs[inner]
    total = terms[0][...]
    for r in terms[1:]:
        total = total + r[...].astype(F32)
    grads_ref[...] = total.astype(BF16)


def total_pieces_body(size, inner, cap, *refs):
    total_body(inner, *refs[: inner + 1])
    grads_ref, low_ref, high_ref = refs[inner:]
    t = lax.axis_index("tp")
    for s in range(size):
        u = t ^ s
        at = lax.rem(u, 2) * (size // 2) + u // 2
        piece = grads_ref[pl.ds(pl.multiple_of(at * cap, cap), cap), :]
        out_ref, j = (low_ref, s) if s < size // 2 else (high_ref, s - size // 2)
        out_ref[j * cap : (j + 1) * cap, :] = piece


def weight_body(inner, *refs):
    cols, grads, (k_ref, v_ref) = refs[:inner], refs[inner : 2 * inner], refs[2 * inner :]
    total = None
    for c, g in zip(cols, grads):
        term = dot(c[...], g[...], 0, 0)
        total = term if total is None else total + term
    width = k_ref.shape[1]
    k_ref[...] = total[:, :width].astype(BF16)
    v_ref[...] = total[:, width:].astype(BF16)


def rows_body(size, inner, *refs):
    grads, weights, out_ref = refs[:size], refs[size : size + size * inner], refs[-1]
    a, b, t = place(inner)
    depth = weights[0].shape[0]
    for j in range(inner):
        total = None
        for s in range(size):
            term = dot(grads[s][...], weights[s * inner + j][...], 1, 1)
            total = term if total is None else total + term
        out_ref[:, pl.ds(pl.multiple_of((b ^ j) * depth, 128), depth)] = total.astype(BF16)


def scatter_body(hot_ref, rows_ref, out_ref):
    out_ref[...] = dot(hot_ref[...], rows_ref[...], 0, 0).astype(BF16)


def after(x, *others):
    return lax.optimization_barrier((x, *others))[0]


def local(tokens, select_index, valid_count, queries, key_matrix, value_matrix, out_grad):
    size, ctx = lax.axis_size("tp"), lax.axis_size("ctx")
    inner = ctx // size
    cap = select_index.shape[0]
    rows, model = tokens.shape
    depth, kv_width = key_matrix.shape
    width = queries.shape[1]
    group = width // kv_width
    half = inner * depth // 2
    slots = size * cap
    pairs = size // 2 - 1
    shape = jax.ShapeDtypeStruct

    def a_swap(x, s):
        return lax.ppermute(x, "ctx", [(j, (j // inner ^ s) * inner + j % inner) for j in range(ctx)])

    def b_swap(x, s):
        return lax.ppermute(x, "ctx", [(j, j // inner * inner + (j % inner ^ s)) for j in range(ctx)])

    def t_swap(x, s):
        return lax.ppermute(x, "tp", [(j, j ^ s) for j in range(size)])

    def move(x, target):
        index = [(a, b, t) for a in range(size) for b in range(inner) for t in range(size)]
        flat = lambda a, b, t: (a * inner + b) * size + t
        return lax.ppermute(x, ("ctx", "tp"), [(flat(*i), flat(*target(*i))) for i in index])

    kv_swapped = [b_swap(x, s) for s in range(1, inner) for x in (key_matrix, value_matrix)]

    *picked, own, qd, weights, hot = call(
        functools.partial(pick_body, size, inner, half),
        [shape((cap, 2 * half), BF16)] * pairs
        + [shape((cap, half), BF16), shape((cap, 2 * half), BF16)]
        + [shape((cap, 2 * width), BF16), shape((depth, 2 * kv_width), BF16)]
        + [shape((cap, rows), BF16)],
        [HBM] * 7,
        [VMEM] * (pairs + 5),
        [
            pltpu.SMEM((cap,), jnp.int32),
            pltpu.SMEM((ctx,), jnp.int32),
            pltpu.VMEM((rows, 2 * half * (pairs + 2)), BF16),
            pltpu.SemaphoreType.DMA((pairs + 2,)),
            pltpu.SemaphoreType.DMA((6,)),
        ],
        cost(2 * cap * rows * model // 2, rows * model),
        "pick",
    )(select_index, valid_count, tokens, queries, out_grad, key_matrix, value_matrix)
    got = [
        move(picked[i], lambda a, b, t, i=i: (a ^ (2 * i + 1 + t % 2), b, t)) for i in range(pairs)
    ] + [a_swap(picked[pairs], size - 1)]
    other = t_swap(jnp.concatenate(got, axis=1), 1)
    qds = [qd] + [a_swap(qd, s) for s in range(1, size)]

    part, *cols = call(
        functools.partial(project_body, size, inner, half),
        [shape((slots, 2 * kv_width), BF16)]
        + [shape((slots, depth), BF16)] * inner
        + [shape((depth, 2 * kv_width), BF16)] * (inner - 1),
        [VMEM] * (pairs + 2 * inner + 2),
        [VMEM] * (2 * inner),
        [pltpu.VMEM((slots, 2 * half), BF16)],
        cost(4 * slots * half * 2 * kv_width, 4 * half * (slots + 2 * kv_width)),
        "project",
    )(*got, other, own, weights, *kv_swapped)
    cols, w_own = cols[:inner], [weights] + cols[inner:]
    parts = [part] + [a_swap(part, s) for s in range(1, size)]
    cols = cols[:1] + [b_swap(after(x, parts[1]), s + 1) for s, x in enumerate(cols[1:])]
    while len(parts) > 1:
        parts = [x.astype(F32) + y.astype(F32) for x, y in zip(parts[::2], parts[1::2])]
    kv = parts[0].astype(BF16)
    kvs = [kv] + [b_swap(kv, s) for s in range(1, inner)]

    block = shape((slots, 2 * kv_width), BF16)
    attended, query_gradient, kept, *sent = call(
        functools.partial(attend_body, size, inner, cap, group),
        [shape((cap, width), BF16)] * 2
        + [shape((slots, 2 * kv_width), F32)]
        + [block] * (inner - 1),
        [SMEM] + [VMEM] * (size + inner),
        [VMEM] * (2 + inner),
        [pltpu.VMEM((slots * group, HEAD), BF16)] * 2,
        cost(12 * slots * group * slots * inner * HEAD, 4 * slots * width),
        "attend",
    )(valid_count, *qds, *kvs)

    terms = [kept] + [b_swap(x, s + 1) for s, x in enumerate(sent)]
    piece = shape((size // 2 * cap, 2 * kv_width), BF16)
    grads, low, high = call(
        functools.partial(total_pieces_body, size, inner, cap),
        [block, piece, piece],
        [VMEM] * inner,
        [VMEM] * 3,
        (),
        cost(slots * kv_width * 4, 16 * slots * kv_width),
        "grads_total",
    )(*terms)

    held, heads, step = [low], [0], size // 2
    out = [high]
    while step:
        out = out[0] if len(out) == 1 else jnp.concatenate(out, axis=0)
        back = t_swap(out, step)
        count = step * cap
        held += [back[i * count : (i + 1) * count] for i in range(len(heads))]
        heads += [h ^ step for h in heads]
        step //= 2
        out = [x[step * cap :] for x in held]
        held = [x[: step * cap] if step else x for x in held]
    head_grads = [held[heads.index(s)] for s in range(size)]

    w_heads, order, step = [w_own], [0], size // 2
    while step:
        w_heads = w_heads + [[t_swap(x, step) for x in ws] for ws in w_heads]
        order = order + [o ^ step for o in order]
        step //= 2
    w_heads = [w_heads[order.index(s)] for s in range(size)]

    row_grad = call(
        functools.partial(rows_body, size, inner),
        shape((cap, 2 * half), BF16),
        [VMEM] * (size + size * inner),
        VMEM,
        (),
        cost(4 * cap * size * 2 * kv_width * half, 8 * size * kv_width * half),
        "row_grad",
    )(*head_grads, *[x for ws in w_heads for x in ws])
    swapped = move(row_grad, lambda a, b, t: (t % 2 * (size // 2) + t // 2, b, a))

    ready = after(grads, row_grad)
    all_grads = [grads] + [b_swap(ready, s) for s in range(1, inner)]
    key_weight_grad, value_weight_grad = call(
        functools.partial(weight_body, inner),
        [shape((depth, kv_width), BF16)] * 2,
        [VMEM] * (2 * inner),
        [VMEM] * 2,
        (),
        cost(4 * slots * half * 2 * kv_width, 16 * half * kv_width),
        "weight_grads",
    )(*cols, *all_grads)

    token_grad = pl.pallas_call(
        scatter_body,
        out_shape=shape((rows, 2 * half), BF16),
        grid=(4,),
        in_specs=[
            pl.BlockSpec((cap, rows), lambda i: (0, 0)),
            pl.BlockSpec((cap, half // 2), lambda i: (0, i)),
        ],
        out_specs=pl.BlockSpec((rows, half // 2), lambda i: (0, i)),
        cost_estimate=cost(4 * rows * cap * half, 4 * rows * half),
        name="scatter",
    )(hot, swapped)
    return attended, query_gradient, token_grad, key_weight_grad, value_weight_grad


def solution(mesh):
    split = P("ctx", "tp")
    in_specs = (P("ctx", None), P("ctx"), P(), split, split, split, split)
    return jax.shard_map(
        local, mesh=mesh, in_specs=in_specs, out_specs=(split,) * 5, check_vma=False
    )
```

time: 269 us -> 81.1 us (0.30)
  waiting for transfers between devices: 149 us -> 35 us
  blocking collectives: 65 us -> 0 us
  starting transfers between devices: 3.82 us -> 25.5 us
  between operations: 13.9 us -> 0.76 us
  Pallas kernels: 0 us -> 11.5 us
  matrix products: 9.53 us -> 0 us
  other arithmetic: 9.21 us -> 0.05 us
  local copies, waits for them, and re-layouts: 16 us -> 7.73 us
    all_gather x2 -> x0, waiting for transfers between devices: 87.9 us -> none  [the longest x1 46.8 us: local(): lax.all_gather(value_matrix, 'ctx', axis=0, tiled=True)]
    all_gather x2 -> x0, blocking collectives: 65 us -> none  [the longest x1 34.4 us: local(): lax.all_gather(own_grads, 'ctx', axis=0, tiled=True)]
    unnamed x5 -> x0, waiting for transfers between devices: 61.2 us -> none
    ppermute x0 -> x24, waiting for transfers between devices: none -> 35 us  [the longest x6 15 us: b_swap(): lax.ppermute(x, 'ctx', [(j, j // inner * inner + (j % inner ^ s)) for j i...]
    ppermute x0 -> x24, starting transfers between devices: none -> 25.5 us  [the longest x7 11.3 us: a_swap(): lax.ppermute(x, 'ctx', [(j, (j // inner ^ s) * inner + j % inner) for j i...]
    pallas_call x0 -> x7, Pallas kernels: none -> 11.5 us  [the longest x1 3.6 us: local(): call(functools.partial(attend_body, size, inner, cap, group), [shape((cap...]
    dot_general x10 -> x0, matrix products: 9.53 us -> none  [the longest x1 4.51 us: local(): lax.dot_general(own_grads, both_weights, (((1,), (1,)), ((), ())), prefer...]
    gather x1 -> x0, local copies, waits for them, and re-layouts: 4.07 us -> none  [local(): picked = jnp.take(tokens, select_index, axis=0)]
  transfers between devices with their start and end apart: 5 -> 24, of which waited for: 3 -> 12; matrix products, arithmetic and copies ran while one was open for 7% -> 0% of each run, Pallas kernels for 0% -> 8%
where the time goes in v1:
time: 81.1 us; the launch traced here: 80.5 us
  waiting for transfers between devices  35 us (43%)
  starting transfers between devices  25.5 us (31%)
  Pallas kernels  11.5 us (14%)
  local copies, waits for them, and re-layouts  7.73 us (10%)
    ppermute x6, waiting for transfers between devices, b_swap(): lax.ppermute(x, 'ctx', [(j, j // inner * inner + (j % inner ^ s)) for j i...  15 us
    ppermute x7, starting transfers between devices, a_swap(): lax.ppermute(x, 'ctx', [(j, (j // inner ^ s) * inner + j % inner) for j i...  11.3 us
    ppermute x7, waiting for transfers between devices, a_swap(): lax.ppermute(x, 'ctx', [(j, (j // inner ^ s) * inner + j % inner) for j i...  9.65 us
    ppermute x9, waiting for transfers between devices, t_swap(): return lax.ppermute(x, 'tp', [(j, j ^ s) for j in range(size)])  8.51 us
    unnamed x20, local copies, waits for them, and re-layouts  7.72 us
    ppermute x6, starting transfers between devices, b_swap(): lax.ppermute(x, 'ctx', [(j, j // inner * inner + (j % inner ^ s)) for j i...  7.18 us
    pallas_call x1, Pallas kernels, local(): call(functools.partial(attend_body, size, inner, cap, group), [shape((cap...  3.6 us
    ppermute x2, starting transfers between devices, move(): lax.ppermute(x, ('ctx', 'tp'), [(flat(*i), flat(*target(*i))) for i in in...  3.58 us
  transfers between devices with their start and end apart: 24, of which 12 were waited for; matrix products, arithmetic and copies ran while one was open for 0% of the time, Pallas kernels for 8%

profile of v1, /device:TPU:4, one launch (start us, length us, event | category | flops | bytes accessed | tf_op | source)
XLA Modules:
  0.0 80.5 jit_solution(10753474877336992021)
XLA Ops:
  0.6 2.2 %copy-done = bf16[256,8192]{1,0:T(8,128)(2,1)S(1)} copy-done((bf16[256,8192]{1,0:T(8,128)(2,1)S(1)}, bf16[256,8192]{1,0:T(8,128)(2,1)}, u32[]{:S(2)}) %copy-start) | copy-done | bytes 4194328
  9.2 1.6 %collective-permute-start.3 = (bf16[32,2048]{1,0:T(8,128)(2,1)S(1)}, bf16[32,2048]{1,0:T(8,128)(2,1)S(1)}, u32[]{:S(2)}, u32[]{:S(2)}) collective-permute-start(bf16[32,2048]{1,0:T(8,128)(2,1)S(1)} %get-tuple-element.27), channel_id=1, source_target_pairs={{0,8},{1,17},{2,10},{3,19},{4,12},{5,21},{6,14},{7,23},{8,0},{9,25... | collective-permute-start | bytes 393224 | tf_op jit(solution)/shard_map/ppermute | solution.py:283
  10.8 2.5 %collective-permute-start.4 = (bf16[32,1024]{1,0:T(8,128)(2,1)S(1)}, bf16[32,1024]{1,0:T(8,128)(2,1)S(1)}, u32[]{:S(2)}, u32[]{:S(2)}) collective-permute-start(bf16[32,1024]{1,0:T(8,128)(2,1)S(1)} %get-tuple-element.28), channel_id=1, source_target_pairs={{0,24},{4,28},{8,16},{12,20},{16,8},{20,12},{24,0},{28,4},{1,25},{... | collective-permute-start | bytes 196616 | tf_op jit(solution)/shard_map/ppermute | solution.py:272
  13.3 1.5 %collective-permute-start.6 = (bf16[1024,128]{1,0:T(8,128)(2,1)S(1)}, bf16[1024,128]{1,0:T(8,128)(2,1)S(1)}, u32[]{:S(2)}, u32[]{:S(2)}) collective-permute-start(bf16[1024,128]{1,0:T(8,128)(2,1)S(1)} %copy-done.1), channel_id=1, source_target_pairs={{0,4},{4,0},{8,12},{12,8},{16,20},{20,16},{24,28},{28,24},{1,5},{5... | collective-permute-start | bytes 786440 | tf_op jit(solution)/shard_map/ppermute | solution.py:275
  15.3 2.6 %collective-permute-done.4.refs_1_ = bf16[32,1024]{1,0:T(8,128)(2,1)S(1)} collective-permute-done((bf16[32,1024]{1,0:T(8,128)(2,1)S(1)}, bf16[32,1024]{1,0:T(8,128)(2,1)S(1)}, u32[]{:S(2)}, u32[]{:S(2)}) %collective-permute-start.4) | collective-permute-done | bytes 65568 | tf_op jit(solution)/shard_map/ppermute | solution.py:272
  18.0 4.5 %collective-permute-done.6.refs_5_ = bf16[1024,128]{1,0:T(8,128)(2,1)S(1)} collective-permute-done((bf16[1024,128]{1,0:T(8,128)(2,1)S(1)}, bf16[1024,128]{1,0:T(8,128)(2,1)S(1)}, u32[]{:S(2)}, u32[]{:S(2)}) %collective-permute-start.6) | collective-permute-done | bytes 262176 | tf_op jit(solution)/shard_map/ppermute | solution.py:275
  22.5 3.8 %collective-permute-done.7.refs_6_ = bf16[1024,128]{1,0:T(8,128)(2,1)S(1)} collective-permute-done((bf16[1024,128]{1,0:T(8,128)(2,1)S(1)}, bf16[1024,128]{1,0:T(8,128)(2,1)S(1)}, u32[]{:S(2)}, u32[]{:S(2)}) %collective-permute-start.7) | collective-permute-done | bytes 262176 | tf_op jit(solution)/shard_map/ppermute | solution.py:275
  26.7 2.5 %collective-permute-start.10 = (bf16[128,256]{1,0:T(8,128)(2,1)S(1)}, bf16[128,256]{1,0:T(8,128)(2,1)S(1)}, u32[]{:S(2)}, u32[]{:S(2)}) collective-permute-start(bf16[128,256]{1,0:T(8,128)(2,1)S(1)} %get-tuple-element.31), channel_id=1, source_target_pairs={{0,24},{4,28},{8,16},{12,20},{16,8},{20,12},{24,0},{28,4},{1,25},{... | collective-permute-start | bytes 196616 | tf_op jit(solution)/shard_map/ppermute | solution.py:272
  29.3 1.9 %collective-permute-start.8 = (bf16[128,256]{1,0:T(8,128)(2,1)S(1)}, bf16[128,256]{1,0:T(8,128)(2,1)S(1)}, u32[]{:S(2)}, u32[]{:S(2)}) collective-permute-start(bf16[128,256]{1,0:T(8,128)(2,1)S(1)} %get-tuple-element.31), channel_id=1, source_target_pairs={{0,8},{4,12},{8,0},{12,4},{16,24},{20,28},{24,16},{28,20},{1,9},{5... | collective-permute-start | bytes 196616 | tf_op jit(solution)/shard_map/ppermute | solution.py:272
  31.2 2.5 %collective-permute-start.2 = (bf16[32,2048]{1,0:T(8,128)(2,1)S(1)}, bf16[32,2048]{1,0:T(8,128)(2,1)S(1)}, u32[]{:S(2)}, u32[]{:S(2)}) collective-permute-start(bf16[32,2048]{1,0:T(8,128)(2,1)S(1)} %get-tuple-element.26.refs_0_), channel_id=1, source_target_pairs={{0,24},{4,28},{8,16},{12,20},{16,8},{20,12},{24,0},{28,4},{1,25},{... | collective-permute-start | bytes 393224 | tf_op jit(solution)/shard_map/ppermute | solution.py:272
  33.7 1.9 %collective-permute-start = (bf16[32,2048]{1,0:T(8,128)(2,1)S(1)}, bf16[32,2048]{1,0:T(8,128)(2,1)S(1)}, u32[]{:S(2)}, u32[]{:S(2)}) collective-permute-start(bf16[32,2048]{1,0:T(8,128)(2,1)S(1)} %get-tuple-element.26.refs_0_), channel_id=1, source_target_pairs={{0,8},{4,12},{8,0},{12,4},{16,24},{20,28},{24,16},{28,20},{1,9},{5... | collective-permute-start | bytes 393224 | tf_op jit(solution)/shard_map/ppermute | solution.py:272
  35.6 4.1 %collective-permute-done.9 = bf16[128,256]{1,0:T(8,128)(2,1)S(1)} collective-permute-done((bf16[128,256]{1,0:T(8,128)(2,1)S(1)}, bf16[128,256]{1,0:T(8,128)(2,1)S(1)}, u32[]{:S(2)}, u32[]{:S(2)}) %collective-permute-start.9) | collective-permute-done | bytes 65568 | tf_op jit(solution)/shard_map/ppermute | solution.py:272
  40.2 1.5 %collective-permute-start.18 = (bf16[1024,256]{1,0:T(8,128)(2,1)S(1)}, bf16[1024,256]{1,0:T(8,128)(2,1)S(1)}, u32[]{:S(2)}, u32[]{:S(2)}) collective-permute-start(bf16[1024,256]{1,0:T(8,128)(2,1)S(1)} %get-tuple-element.39.refs_5_), channel_id=1, source_target_pairs={{0,2},{1,3},{2,0},{3,1},{4,6},{5,7},{6,4},{7,5},{8,10},{9,11},{10,... | collective-permute-start | bytes 1572872 | tf_op jit(solution)/shard_map/ppermute | solution.py:278
  41.8 1.6 %collective-permute-start.11 = (bf16[128,256]{1,0:T(8,128)(2,1)S(1)}, bf16[128,256]{1,0:T(8,128)(2,1)S(1)}, u32[]{:S(2)}, u32[]{:S(2)}) collective-permute-start(bf16[128,256]{1,0:T(8,128)(2,1)S(1)} %add_convert_fusion.refs_4_), channel_id=1, source_target_pairs={{0,4},{4,0},{8,12},{12,8},{16,20},{20,16},{24,28},{28,24},{1,5},{5... | collective-permute-start | bytes 196616 | tf_op jit(solution)/shard_map/ppermute | solution.py:275
  43.3 3.0 %collective-permute-done.1.refs_2_ = bf16[32,2048]{1,0:T(8,128)(2,1)S(1)} collective-permute-done((bf16[32,2048]{1,0:T(8,128)(2,1)S(1)}, bf16[32,2048]{1,0:T(8,128)(2,1)S(1)}, u32[]{:S(2)}, u32[]{:S(2)}) %collective-permute-start.1) | collective-permute-done | bytes 131104 | tf_op jit(solution)/shard_map/ppermute | solution.py:272
  46.3 3.6 %attend.1 = (bf16[32,1024]{1,0:T(8,128)(2,1)}, bf16[32,1024]{1,0:T(8,128)(2,1)}, f32[128,256]{1,0:T(8,128)S(1)}, bf16[128,256]{1,0:T(8,128)(2,1)S(1)}) custom-call(s32[8]{0:T(128)S(1)} %copy-done.8, bf16[32,2048]{1,0:T(8,128)(2,1)S(1)} %get-tuple-element.26.refs_0_, bf16[32,2048]{1,0:T(8,128)(2,1)S(1)} %collective-permute-done.refs_1_, ...), custom_call_target="tpu_custom_call" | custom-call | flops 402653184 | bytes 524288 | tf_op jit(solution)/shard_map/attend/pallas_call | solution.py:331
  49.9 1.5 %collective-permute-start.12 = (bf16[128,256]{1,0:T(8,128)(2,1)S(1)}, bf16[128,256]{1,0:T(8,128)(2,1)S(1)}, u32[]{:S(2)}, u32[]{:S(2)}) collective-permute-start(bf16[128,256]{1,0:T(8,128)(2,1)S(1)} %get-tuple-element.36), channel_id=1, source_target_pairs={{0,4},{4,0},{8,12},{12,8},{16,20},{20,16},{24,28},{28,24},{1,5},{5... | collective-permute-start | bytes 196616 | tf_op jit(solution)/shard_map/ppermute | solution.py:275
  51.9 2.3 %collective-permute-done.12.refs_1_ = bf16[128,256]{1,0:T(8,128)(2,1)S(1)} collective-permute-done((bf16[128,256]{1,0:T(8,128)(2,1)S(1)}, bf16[128,256]{1,0:T(8,128)(2,1)S(1)}, u32[]{:S(2)}, u32[]{:S(2)}) %collective-permute-start.12) | collective-permute-done | bytes 65568 | tf_op jit(solution)/shard_map/ppermute | solution.py:275
  54.8 6.8 %collective-permute-done.18.refs_9_ = bf16[1024,256]{1,0:T(8,128)(2,1)S(1)} collective-permute-done((bf16[1024,256]{1,0:T(8,128)(2,1)S(1)}, bf16[1024,256]{1,0:T(8,128)(2,1)S(1)}, u32[]{:S(2)}, u32[]{:S(2)}) %collective-permute-start.18) | collective-permute-done | bytes 524320 | tf_op jit(solution)/shard_map/ppermute | solution.py:278
  63.6 1.5 %collective-permute-start.22 = (bf16[128,1024]{1,0:T(8,128)(2,1)S(1)}, bf16[128,1024]{1,0:T(8,128)(2,1)S(1)}, u32[]{:S(2)}, u32[]{:S(2)}) collective-permute-start(bf16[128,1024]{1,0:T(8,128)(2,1)S(1)} %get-tuple-element.42), channel_id=1, source_target_pairs={{0,4},{4,0},{8,12},{12,8},{16,20},{20,16},{24,28},{28,24},{1,5},{5... | collective-permute-start | bytes 786440 | tf_op jit(solution)/shard_map/ppermute | solution.py:275
  66.4 1.9 %collective-permute-start.21 = (bf16[32,2048]{1,0:T(8,128)(2,1)S(1)}, bf16[32,2048]{1,0:T(8,128)(2,1)S(1)}, u32[]{:S(2)}, u32[]{:S(2)}) collective-permute-start(bf16[32,2048]{1,0:T(8,128)(2,1)S(1)} %row_grad.1), channel_id=1, source_target_pairs={{0,0},{1,16},{2,8},{3,24},{4,4},{5,20},{6,12},{7,28},{8,1},{9,17},... | collective-permute-start | bytes 393224 | tf_op jit(solution)/shard_map/ppermute | solution.py:283
  68.9 3.7 %collective-permute-done.22.refs_1_ = bf16[128,1024]{1,0:T(8,128)(2,1)S(1)} collective-permute-done((bf16[128,1024]{1,0:T(8,128)(2,1)S(1)}, bf16[128,1024]{1,0:T(8,128)(2,1)S(1)}, u32[]{:S(2)}, u32[]{:S(2)}) %collective-permute-start.22) | collective-permute-done | bytes 262176 | tf_op jit(solution)/shard_map/ppermute | solution.py:275
  74.6 1.9 %collective-permute-done.21.rows_ref = bf16[32,2048]{1,0:T(8,128)(2,1)S(1)} collective-permute-done((bf16[32,2048]{1,0:T(8,128)(2,1)S(1)}, bf16[32,2048]{1,0:T(8,128)(2,1)S(1)}, u32[]{:S(2)}, u32[]{:S(2)}) %collective-permute-start.21) | collective-permute-done | bytes 131104 | tf_op jit(solution)/shard_map/ppermute | solution.py:283
  77.1 3.4 %scatter.1 = bf16[256,2048]{1,0:T(8,128)(2,1)} custom-call(bf16[32,256]{1,0:T(8,128)(2,1)} %copy-done.5, bf16[32,2048]{1,0:T(8,128)(2,1)} %copy-done.9), custom_call_target="tpu_custom_call" | custom-call | flops 33554432 | bytes 1048576 | tf_op jit(solution)/shard_map/scatter/pallas_call | solution.py:398
  (57 shorter events, 15.6 us)
Async XLA Ops:
  9.2 8.7 %collective-permute-start.3 = (bf16[32,2048]{1,0:T(8,128)(2,1)S(1)}, bf16[32,2048]{1,0:T(8,128)(2,1)S(1)}, u32[]{:S(2)}, u32[]{:S(2)}) collective-permute-start(bf16[32,2048]{1,0:T(8,128)(2,1)S(1)} %get-tuple-element.27), channel_id=1, source_target_pairs={{0,8},{1,17},{2,10},{3,19},{4,12},{5,21},{6,14},{7,23},{8,0},{9,25... | collective-permute-start | bytes 393224 | tf_op jit(solution)/shard_map/ppermute | solution.py:283
  10.8 7.1 %collective-permute-start.4 = (bf16[32,1024]{1,0:T(8,128)(2,1)S(1)}, bf16[32,1024]{1,0:T(8,128)(2,1)S(1)}, u32[]{:S(2)}, u32[]{:S(2)}) collective-permute-start(bf16[32,1024]{1,0:T(8,128)(2,1)S(1)} %get-tuple-element.28), channel_id=1, source_target_pairs={{0,24},{4,28},{8,16},{12,20},{16,8},{20,12},{24,0},{28,4},{1,25},{... | collective-permute-start | bytes 196616 | tf_op jit(solution)/shard_map/ppermute | solution.py:272
  13.3 9.2 %collective-permute-start.6 = (bf16[1024,128]{1,0:T(8,128)(2,1)S(1)}, bf16[1024,128]{1,0:T(8,128)(2,1)S(1)}, u32[]{:S(2)}, u32[]{:S(2)}) collective-permute-start(bf16[1024,128]{1,0:T(8,128)(2,1)S(1)} %copy-done.1), channel_id=1, source_target_pairs={{0,4},{4,0},{8,12},{12,8},{16,20},{20,16},{24,28},{28,24},{1,5},{5... | collective-permute-start | bytes 786440 | tf_op jit(solution)/shard_map/ppermute | solution.py:275
  14.8 11.5 %collective-permute-start.7 = (bf16[1024,128]{1,0:T(8,128)(2,1)S(1)}, bf16[1024,128]{1,0:T(8,128)(2,1)S(1)}, u32[]{:S(2)}, u32[]{:S(2)}) collective-permute-start(bf16[1024,128]{1,0:T(8,128)(2,1)S(1)} %copy-done.2), channel_id=1, source_target_pairs={{0,4},{4,0},{8,12},{12,8},{16,20},{20,16},{24,28},{28,24},{1,5},{5... | collective-permute-start | bytes 786440 | tf_op jit(solution)/shard_map/ppermute | solution.py:275
  17.9 8.4 %collective-permute-start.5 = (bf16[32,3072]{1,0:T(8,128)(2,1)S(1)}, bf16[32,3072]{1,0:T(8,128)(2,1)S(1)}, u32[]{:S(2)}, u32[]{:S(2)}) collective-permute-start(bf16[32,3072]{1,0:T(8,128)(2,1)S(1)} %pad_maximum_fusion), channel_id=1, source_target_pairs={{0,1},{1,0},{2,3},{3,2},{4,5},{5,4},{6,7},{7,6},{8,9},{9,8},{10,11... | collective-permute-start | bytes 589832 | tf_op jit(solution)/shard_map/ppermute | solution.py:278
  26.7 6.9 %collective-permute-start.10 = (bf16[128,256]{1,0:T(8,128)(2,1)S(1)}, bf16[128,256]{1,0:T(8,128)(2,1)S(1)}, u32[]{:S(2)}, u32[]{:S(2)}) collective-permute-start(bf16[128,256]{1,0:T(8,128)(2,1)S(1)} %get-tuple-element.31), channel_id=1, source_target_pairs={{0,24},{4,28},{8,16},{12,20},{16,8},{20,12},{24,0},{28,4},{1,25},{... | collective-permute-start | bytes 196616 | tf_op jit(solution)/shard_map/ppermute | solution.py:272
  29.3 10.4 %collective-permute-start.9 = (bf16[128,256]{1,0:T(8,128)(2,1)S(1)}, bf16[128,256]{1,0:T(8,128)(2,1)S(1)}, u32[]{:S(2)}, u32[]{:S(2)}) collective-permute-start(bf16[128,256]{1,0:T(8,128)(2,1)S(1)} %get-tuple-element.31), channel_id=1, source_target_pairs={{0,16},{4,20},{8,24},{12,28},{16,0},{20,4},{24,8},{28,12},{1,17},{... | collective-permute-start | bytes 196616 | tf_op jit(solution)/shard_map/ppermute | solution.py:272
  29.3 10.9 %collective-permute-start.8 = (bf16[128,256]{1,0:T(8,128)(2,1)S(1)}, bf16[128,256]{1,0:T(8,128)(2,1)S(1)}, u32[]{:S(2)}, u32[]{:S(2)}) collective-permute-start(bf16[128,256]{1,0:T(8,128)(2,1)S(1)} %get-tuple-element.31), channel_id=1, source_target_pairs={{0,8},{4,12},{8,0},{12,4},{16,24},{20,28},{24,16},{28,20},{1,9},{5... | collective-permute-start | bytes 196616 | tf_op jit(solution)/shard_map/ppermute | solution.py:272
  31.2 10.6 %collective-permute-start.2 = (bf16[32,2048]{1,0:T(8,128)(2,1)S(1)}, bf16[32,2048]{1,0:T(8,128)(2,1)S(1)}, u32[]{:S(2)}, u32[]{:S(2)}) collective-permute-start(bf16[32,2048]{1,0:T(8,128)(2,1)S(1)} %get-tuple-element.26.refs_0_), channel_id=1, source_target_pairs={{0,24},{4,28},{8,16},{12,20},{16,8},{20,12},{24,0},{28,4},{1,25},{... | collective-permute-start | bytes 393224 | tf_op jit(solution)/shard_map/ppermute | solution.py:272
  33.6 12.7 %collective-permute-start.1 = (bf16[32,2048]{1,0:T(8,128)(2,1)S(1)}, bf16[32,2048]{1,0:T(8,128)(2,1)S(1)}, u32[]{:S(2)}, u32[]{:S(2)}) collective-permute-start(bf16[32,2048]{1,0:T(8,128)(2,1)S(1)} %get-tuple-element.26.refs_0_), channel_id=1, source_target_pairs={{0,16},{4,20},{8,24},{12,28},{16,0},{20,4},{24,8},{28,12},{1,17},{... | collective-permute-start | bytes 393224 | tf_op jit(solution)/shard_map/ppermute | solution.py:272
  33.7 12.7 %collective-permute-start = (bf16[32,2048]{1,0:T(8,128)(2,1)S(1)}, bf16[32,2048]{1,0:T(8,128)(2,1)S(1)}, u32[]{:S(2)}, u32[]{:S(2)}) collective-permute-start(bf16[32,2048]{1,0:T(8,128)(2,1)S(1)} %get-tuple-element.26.refs_0_), channel_id=1, source_target_pairs={{0,8},{4,12},{8,0},{12,4},{16,24},{20,28},{24,16},{28,20},{1,9},{5... | collective-permute-start | bytes 393224 | tf_op jit(solution)/shard_map/ppermute | solution.py:272
  39.7 15.1 %collective-permute-start.17 = (bf16[1024,256]{1,0:T(8,128)(2,1)S(1)}, bf16[1024,256]{1,0:T(8,128)(2,1)S(1)}, u32[]{:S(2)}, u32[]{:S(2)}) collective-permute-start(bf16[1024,256]{1,0:T(8,128)(2,1)S(1)} %get-tuple-element.30.refs_4_), channel_id=1, source_target_pairs={{0,2},{1,3},{2,0},{3,1},{4,6},{5,7},{6,4},{7,5},{8,10},{9,11},{10,... | collective-permute-start | bytes 1572872 | tf_op jit(solution)/shard_map/ppermute | solution.py:278
  40.2 21.4 %collective-permute-start.18 = (bf16[1024,256]{1,0:T(8,128)(2,1)S(1)}, bf16[1024,256]{1,0:T(8,128)(2,1)S(1)}, u32[]{:S(2)}, u32[]{:S(2)}) collective-permute-start(bf16[1024,256]{1,0:T(8,128)(2,1)S(1)} %get-tuple-element.39.refs_5_), channel_id=1, source_target_pairs={{0,2},{1,3},{2,0},{3,1},{4,6},{5,7},{6,4},{7,5},{8,10},{9,11},{10,... | collective-permute-start | bytes 1572872 | tf_op jit(solution)/shard_map/ppermute | solution.py:278
  41.8 4.6 %collective-permute-start.11 = (bf16[128,256]{1,0:T(8,128)(2,1)S(1)}, bf16[128,256]{1,0:T(8,128)(2,1)S(1)}, u32[]{:S(2)}, u32[]{:S(2)}) collective-permute-start(bf16[128,256]{1,0:T(8,128)(2,1)S(1)} %add_convert_fusion.refs_4_), channel_id=1, source_target_pairs={{0,4},{4,0},{8,12},{12,8},{16,20},{20,16},{24,28},{28,24},{1,5},{5... | collective-permute-start | bytes 196616 | tf_op jit(solution)/shard_map/ppermute | solution.py:275
  49.9 4.3 %collective-permute-start.12 = (bf16[128,256]{1,0:T(8,128)(2,1)S(1)}, bf16[128,256]{1,0:T(8,128)(2,1)S(1)}, u32[]{:S(2)}, u32[]{:S(2)}) collective-permute-start(bf16[128,256]{1,0:T(8,128)(2,1)S(1)} %get-tuple-element.36), channel_id=1, source_target_pairs={{0,4},{4,0},{8,12},{12,8},{16,20},{20,16},{24,28},{28,24},{1,5},{5... | collective-permute-start | bytes 196616 | tf_op jit(solution)/shard_map/ppermute | solution.py:275
  51.4 13.6 %collective-permute-start.15 = (bf16[1024,256]{1,0:T(8,128)(2,1)S(1)}, bf16[1024,256]{1,0:T(8,128)(2,1)S(1)}, u32[]{:S(2)}, u32[]{:S(2)}) collective-permute-start(bf16[1024,256]{1,0:T(8,128)(2,1)S(1)} %get-tuple-element.30.refs_4_), channel_id=1, source_target_pairs={{0,1},{1,0},{2,3},{3,2},{4,5},{5,4},{6,7},{7,6},{8,9},{9,8},{10,11... | collective-permute-start | bytes 1572872 | tf_op jit(solution)/shard_map/ppermute | solution.py:278
  51.4 13.6 %collective-permute-start.16 = (bf16[1024,256]{1,0:T(8,128)(2,1)S(1)}, bf16[1024,256]{1,0:T(8,128)(2,1)S(1)}, u32[]{:S(2)}, u32[]{:S(2)}) collective-permute-start(bf16[1024,256]{1,0:T(8,128)(2,1)S(1)} %get-tuple-element.39.refs_5_), channel_id=1, source_target_pairs={{0,1},{1,0},{2,3},{3,2},{4,5},{5,4},{6,7},{7,6},{8,9},{9,8},{10,11... | collective-permute-start | bytes 1572872 | tf_op jit(solution)/shard_map/ppermute | solution.py:278
  54.2 7.7 %collective-permute-start.13 = (bf16[64,256]{1,0:T(8,128)(2,1)S(1)}, bf16[64,256]{1,0:T(8,128)(2,1)S(1)}, u32[]{:S(2)}, u32[]{:S(2)}) collective-permute-start(bf16[64,256]{1,0:T(8,128)(2,1)S(1)} %get-tuple-element.38), channel_id=1, source_target_pairs={{0,2},{1,3},{2,0},{3,1},{4,6},{5,7},{6,4},{7,5},{8,10},{9,11},{10,... | collective-permute-start | bytes 98312 | tf_op jit(solution)/shard_map/ppermute | solution.py:278
  54.8 10.2 %collective-permute-start.19 = (bf16[1024,256]{1,0:T(8,128)(2,1)S(1)}, bf16[1024,256]{1,0:T(8,128)(2,1)S(1)}, u32[]{:S(2)}, u32[]{:S(2)}) collective-permute-start(bf16[1024,256]{1,0:T(8,128)(2,1)S(1)} %collective-permute-done.17.refs_8_), channel_id=1, source_target_pairs={{0,1},{1,0},{2,3},{3,2},{4,5},{5,4},{6,7},{7,6},{8,9},{9,8},{10,11... | collective-permute-start | bytes 1572872 | tf_op jit(solution)/shard_map/ppermute | solution.py:278
  61.6 3.5 %collective-permute-start.20 = (bf16[1024,256]{1,0:T(8,128)(2,1)S(1)}, bf16[1024,256]{1,0:T(8,128)(2,1)S(1)}, u32[]{:S(2)}, u32[]{:S(2)}) collective-permute-start(bf16[1024,256]{1,0:T(8,128)(2,1)S(1)} %collective-permute-done.18.refs_9_), channel_id=1, source_target_pairs={{0,1},{1,0},{2,3},{3,2},{4,5},{5,4},{6,7},{7,6},{8,9},{9,8},{10,11... | collective-permute-start | bytes 1572872 | tf_op jit(solution)/shard_map/ppermute | solution.py:278
  62.0 1.6 %collective-permute-start.14 = (bf16[64,256]{1,0:T(8,128)(2,1)S(1)}, bf16[64,256]{1,0:T(8,128)(2,1)S(1)}, u32[]{:S(2)}, u32[]{:S(2)}) collective-permute-start(bf16[64,256]{1,0:T(8,128)(2,1)S(1)} %pad_maximum_fusion.1), channel_id=1, source_target_pairs={{0,1},{1,0},{2,3},{3,2},{4,5},{5,4},{6,7},{7,6},{8,9},{9,8},{10,11... | collective-permute-start | bytes 98312 | tf_op jit(solution)/shard_map/ppermute | solution.py:278
  63.6 9.1 %collective-permute-start.22 = (bf16[128,1024]{1,0:T(8,128)(2,1)S(1)}, bf16[128,1024]{1,0:T(8,128)(2,1)S(1)}, u32[]{:S(2)}, u32[]{:S(2)}) collective-permute-start(bf16[128,1024]{1,0:T(8,128)(2,1)S(1)} %get-tuple-element.42), channel_id=1, source_target_pairs={{0,4},{4,0},{8,12},{12,8},{16,20},{20,16},{24,28},{28,24},{1,5},{5... | collective-permute-start | bytes 786440 | tf_op jit(solution)/shard_map/ppermute | solution.py:275
  66.4 10.1 %collective-permute-start.21 = (bf16[32,2048]{1,0:T(8,128)(2,1)S(1)}, bf16[32,2048]{1,0:T(8,128)(2,1)S(1)}, u32[]{:S(2)}, u32[]{:S(2)}) collective-permute-start(bf16[32,2048]{1,0:T(8,128)(2,1)S(1)} %row_grad.1), channel_id=1, source_target_pairs={{0,0},{1,16},{2,8},{3,24},{4,4},{5,20},{6,12},{7,28},{8,1},{9,17},... | collective-permute-start | bytes 393224 | tf_op jit(solution)/shard_map/ppermute | solution.py:283
  68.3 5.0 %collective-permute-start.23 = (bf16[128,256]{1,0:T(8,128)(2,1)S(1)}, bf16[128,256]{1,0:T(8,128)(2,1)S(1)}, u32[]{:S(2)}, u32[]{:S(2)}) collective-permute-start(bf16[128,256]{1,0:T(8,128)(2,1)S(1)} %get-tuple-element.44.refs_2_), channel_id=1, source_target_pairs={{0,4},{4,0},{8,12},{12,8},{16,20},{20,16},{24,28},{28,24},{1,5},{5... | collective-permute-start | bytes 196616 | tf_op jit(solution)/shard_map/ppermute | solution.py:275
  (10 other events, 72.7 us)

commit v2 on v1

--- a/solution.py
+++ b/solution.py
@@ -11,6 +11,7 @@
 HEAD = 128
 NEG = -1e30
 HIDDEN = 1 << 30
+HINT = 2 * 10**10
 F32 = jnp.float32
 BF16 = jnp.bfloat16
 
@@ -108,10 +109,9 @@
 
 def project_body(size, inner, half, *refs):
     pairs = size // 2 - 1
-    got, other_ref, own_ref, w_ref = refs[: pairs + 1], refs[pairs + 1], refs[pairs + 2], refs[pairs + 3]
-    kv_refs = refs[pairs + 4 : pairs + 2 * inner + 2]
-    outs = refs[pairs + 2 * inner + 2 :]
-    part_ref, cols, ws, rows_ref = outs[0], outs[1 : inner + 1], outs[inner + 1 : 2 * inner], outs[-1]
+    got, other_ref, own_ref = refs[: pairs + 1], refs[pairs + 1], refs[pairs + 2]
+    w_refs, outs = refs[pairs + 3 : pairs + 3 + inner], refs[pairs + 3 + inner :]
+    part_ref, cols, rows_ref = outs[0], outs[1 : inner + 1], outs[-1]
     a, b, t = place(inner)
     cap = own_ref.shape[0]
     core = lax.rem(t, 2)
@@ -128,36 +128,39 @@
         rows_ref[to(a ^ (2 * i + 2 - core)), :] = other_ref[:, 2 * half * i : 2 * half * (i + 1)]
     rows_ref[to(a ^ (size - 1)), side(core)] = got[pairs][...]
     rows_ref[to(a ^ (size - 1)), side(1 - core)] = other_ref[:, 2 * half * pairs :]
-    depth, kv_width = w_ref.shape[0], w_ref.shape[1] // 2
+    depth = w_refs[0].shape[0]
     total = None
     for s in range(inner):
         part = rows_ref[:, pl.ds(pl.multiple_of((b ^ s) * depth, 128), depth)]
         cols[s][...] = part
-        if s:
-            ws[s - 1][:, :kv_width] = kv_refs[2 * s - 2][...]
-            ws[s - 1][:, kv_width:] = kv_refs[2 * s - 1][...]
-        term = dot(part, (ws[s - 1] if s else w_ref)[...], 1, 0)
+        term = dot(part, w_refs[s][...], 1, 0)
         total = term if total is None else total + term
     part_ref[...] = total.astype(BF16)
 
 
 def attend_body(size, inner, cap, group, count_ref, *refs):
     qds, kvs = refs[:size], refs[size : size + inner]
-    att_ref, dq_ref = refs[size + inner : size + inner + 2]
-    kept_ref = refs[size + inner + 2]
-    sent = refs[size + inner + 3 : size + 2 * inner + 2]
-    q_all, do_all = refs[size + 2 * inner + 2 :]
+    att_ref, dq_ref, kept_ref, sent_ref, q_all, do_all = refs[size + inner :]
     a, b, t = place(inner)
     width = group * HEAD
     block = group * cap
     scale = 1.0 / math.sqrt(HEAD)
     slot = lax.broadcasted_iota(jnp.int32, (cap, HEAD), 0)
+    far, far_other = qds[2][...], qds[3][...]
+    swapped = jnp.concatenate([far_other[cap:], far_other[:cap]], axis=0)
+    odd = lax.rem(a, 2) == 1
+    far_q, far_do = jnp.where(odd, swapped, far), jnp.where(odd, far, swapped)
     for s in range(size):
         count = count_ref[(a ^ s) * inner + b]
+        if s < 2:
+            q_rows, do_rows = qds[s][:, :width], qds[s][:, width:]
+        else:
+            far_rows = slice((s - 2) * cap, (s - 1) * cap)
+            q_rows, do_rows = far_q[far_rows], far_do[far_rows]
         for g in range(group):
             to = slice(s * block + g * cap, s * block + (g + 1) * cap)
-            q_all[to, :] = qds[s][:, g * HEAD : (g + 1) * HEAD]
-            rows = qds[s][:, width + g * HEAD : width + (g + 1) * HEAD]
+            q_all[to, :] = q_rows[:, g * HEAD : (g + 1) * HEAD]
+            rows = do_rows[:, g * HEAD : (g + 1) * HEAD]
             do_all[to, :] = jnp.where(slot < count, rows.astype(F32), 0.0).astype(BF16)
     kv = jnp.concatenate([r[...] for r in kvs], axis=0)
     keys, values = kv[:, :HEAD], kv[:, HEAD:]
@@ -196,59 +199,68 @@
             for g in range(group):
                 att_ref[:, g * HEAD : (g + 1) * HEAD] = att_rows[g * cap : (g + 1) * cap, :]
                 dq_ref[:, g * HEAD : (g + 1) * HEAD] = dq_rows[g * cap : (g + 1) * cap, :]
-    rows = size * cap
-    kept_ref[:, :HEAD] = dk[:rows, :]
-    kept_ref[:, HEAD:] = dv[:rows, :]
-    for s in range(1, inner):
-        sent[s - 1][:, :HEAD] = dk[s * rows : (s + 1) * rows, :].astype(BF16)
-        sent[s - 1][:, HEAD:] = dv[s * rows : (s + 1) * rows, :].astype(BF16)
-
-
-def total_body(inner, *refs):
-    terms, grads_ref = refs[:inner], refs[inner]
-    total = terms[0][...]
-    for r in terms[1:]:
-        total = total + r[...].astype(F32)
-    grads_ref[...] = total.astype(BF16)
-
-
-def total_pieces_body(size, inner, cap, *refs):
-    total_body(inner, *refs[: inner + 1])
-    grads_ref, low_ref, high_ref = refs[inner:]
-    t = lax.axis_index("tp")
-    for s in range(size):
-        u = t ^ s
-        at = lax.rem(u, 2) * (size // 2) + u // 2
-        piece = grads_ref[pl.ds(pl.multiple_of(at * cap, cap), cap), :]
-        out_ref, j = (low_ref, s) if s < size // 2 else (high_ref, s - size // 2)
-        out_ref[j * cap : (j + 1) * cap, :] = piece
+    for ref in (kept_ref, sent_ref):
+        ref[:, :HEAD] = dk.astype(ref.dtype)
+        ref[:, HEAD:] = dv.astype(ref.dtype)
+
+
+def total_body(size, inner, cap, *refs):
+    terms, (grads_ref, keep_ref, send_ref) = refs[:inner], refs[inner:]
+    slots = size * cap
+    for s in range(inner):
+        total = None
+        for j in range(inner):
+            term = terms[j][(s ^ j) * slots : ((s ^ j) + 1) * slots, :].astype(F32)
+            total = term if total is None else total + term
+        grads_ref[s * slots : (s + 1) * slots, :] = total.astype(BF16)
+    rows = slots // 2
+    core = lax.rem(lax.axis_index("tp"), 2)
+    keep_ref[...] = grads_ref[pl.ds(pl.multiple_of(core * rows, rows), rows), :]
+    send_ref[...] = grads_ref[pl.ds(pl.multiple_of((1 - core) * rows, rows), rows), :]
 
 
 def weight_body(inner, *refs):
-    cols, grads, (k_ref, v_ref) = refs[:inner], refs[inner : 2 * inner], refs[2 * inner :]
+    cols, (grads_ref, k_ref, v_ref) = refs[:inner], refs[inner:]
+    slots = cols[0].shape[0]
     total = None
-    for c, g in zip(cols, grads):
-        term = dot(c[...], g[...], 0, 0)
+    for s in range(inner):
+        term = dot(cols[s][...], grads_ref[s * slots : (s + 1) * slots, :], 0, 0)
         total = term if total is None else total + term
     width = k_ref.shape[1]
     k_ref[...] = total[:, :width].astype(BF16)
     v_ref[...] = total[:, width:].astype(BF16)
 
 
-def rows_body(size, inner, *refs):
-    grads, weights, out_ref = refs[:size], refs[size : size + size * inner], refs[-1]
+def rows_body(size, inner, cap, *refs):
+    own, pair, weights, outs = refs[0], refs[1], refs[2 : 2 + 2 * inner], refs[2 + 2 * inner :]
+    outs, total_ref = outs[:-1], outs[-1]
     a, b, t = place(inner)
     depth = weights[0].shape[0]
     for j in range(inner):
+        total = dot(own[...], weights[j][...], 1, 1) + dot(pair[...], weights[inner + j][...], 1, 1)
+        total_ref[:, pl.ds(pl.multiple_of((b ^ j) * depth, 128), depth)] = total.astype(BF16)
+    for m in range(len(outs)):
+        at = (t // 2) ^ m
+        outs[m][...] = total_ref[pl.ds(pl.multiple_of(at * cap, cap), cap), :]
+
+
+def scatter_body(parts, hot_ref, *refs):
+    rows_refs, out_ref, buf, sems = refs[:parts], refs[parts], refs[parts + 1], refs[parts + 2]
+    count = sems.shape[0]
+    wide = out_ref.shape[1] // count
+    hot = hot_ref[...]
+    copies = []
+    for i in range(count):
+        cols = slice(i * wide, (i + 1) * wide)
         total = None
-        for s in range(size):
-            term = dot(grads[s][...], weights[s * inner + j][...], 1, 1)
+        for r in rows_refs:
+            term = dot(hot, r[:, cols], 0, 0)
             total = term if total is None else total + term
-        out_ref[:, pl.ds(pl.multiple_of((b ^ j) * depth, 128), depth)] = total.astype(BF16)
-
-
-def scatter_body(hot_ref, rows_ref, out_ref):
-    out_ref[...] = dot(hot_ref[...], rows_ref[...], 0, 0).astype(BF16)
+        buf[:, cols] = total.astype(BF16)
+        copies.append(pltpu.make_async_copy(buf.at[:, cols], out_ref.at[:, cols], sems.at[i]))
+        copies[i].start()
+    for c in copies:
+        c.wait()
 
 
 def after(x, *others):
@@ -282,8 +294,7 @@
         flat = lambda a, b, t: (a * inner + b) * size + t
         return lax.ppermute(x, ("ctx", "tp"), [(flat(*i), flat(*target(*i))) for i in index])
 
-    kv_swapped = [b_swap(x, s) for s in range(1, inner) for x in (key_matrix, value_matrix)]
-
+    inputs = (select_index, valid_count, tokens, queries, out_grad, key_matrix, value_matrix)
     *picked, own, qd, weights, hot = call(
         functools.partial(pick_body, size, inner, half),
         [shape((cap, 2 * half), BF16)] * pairs
@@ -299,114 +310,101 @@
             pltpu.SemaphoreType.DMA((pairs + 2,)),
             pltpu.SemaphoreType.DMA((6,)),
         ],
-        cost(2 * cap * rows * model // 2, rows * model),
+        cost(HINT, rows * model),
         "pick",
-    )(select_index, valid_count, tokens, queries, out_grad, key_matrix, value_matrix)
+    )(*[pltpu.with_memory_space_constraint(x, pltpu.HBM) for x in inputs])
     got = [
         move(picked[i], lambda a, b, t, i=i: (a ^ (2 * i + 1 + t % 2), b, t)) for i in range(pairs)
     ] + [a_swap(picked[pairs], size - 1)]
+    k_far = [b_swap(key_matrix, s) for s in range(1, inner)]
+    v_far = [b_swap(value_matrix, s) for s in range(1, inner)]
+    w_own = [weights] + [jnp.concatenate(x, axis=1) for x in zip(k_far, v_far)]
+    k_pair = [t_swap(x, 1) for x in k_far]
     other = t_swap(jnp.concatenate(got, axis=1), 1)
-    qds = [qd] + [a_swap(qd, s) for s in range(1, size)]
+    near = a_swap(qd, 1)
+    both = jnp.concatenate([qd, near], axis=0)
+    odd = lax.rem(lax.axis_index("ctx") // inner, 2) == 1
+    far = a_swap(jnp.where(odd, both[:, width:], both[:, :width]), 2)
+    far_other = a_swap(far, 1)
+    qds = [qd, near, far, far_other]
 
     part, *cols = call(
         functools.partial(project_body, size, inner, half),
         [shape((slots, 2 * kv_width), BF16)]
-        + [shape((slots, depth), BF16)] * inner
-        + [shape((depth, 2 * kv_width), BF16)] * (inner - 1),
-        [VMEM] * (pairs + 2 * inner + 2),
-        [VMEM] * (2 * inner),
+        + [shape((slots, depth), BF16)] * inner,
+        [VMEM] * (pairs + inner + 3),
+        [VMEM] * (inner + 1),
         [pltpu.VMEM((slots, 2 * half), BF16)],
-        cost(4 * slots * half * 2 * kv_width, 4 * half * (slots + 2 * kv_width)),
+        cost(HINT, 4 * half * (slots + 2 * kv_width)),
         "project",
-    )(*got, other, own, weights, *kv_swapped)
-    cols, w_own = cols[:inner], [weights] + cols[inner:]
+    )(*got, other, own, *w_own)
     parts = [part] + [a_swap(part, s) for s in range(1, size)]
-    cols = cols[:1] + [b_swap(after(x, parts[1]), s + 1) for s, x in enumerate(cols[1:])]
+    first = parts[1]
+    cols = cols[:1] + [b_swap(after(x, first), s + 1) for s, x in enumerate(cols[1:])]
     while len(parts) > 1:
         parts = [x.astype(F32) + y.astype(F32) for x, y in zip(parts[::2], parts[1::2])]
     kv = parts[0].astype(BF16)
     kvs = [kv] + [b_swap(kv, s) for s in range(1, inner)]
 
-    block = shape((slots, 2 * kv_width), BF16)
-    attended, query_gradient, kept, *sent = call(
+    terms = (slots * inner, 2 * kv_width)
+    attended, query_gradient, kept, sent = call(
         functools.partial(attend_body, size, inner, cap, group),
-        [shape((cap, width), BF16)] * 2
-        + [shape((slots, 2 * kv_width), F32)]
-        + [block] * (inner - 1),
+        [shape((cap, width), BF16)] * 2 + [shape(terms, F32), shape(terms, BF16)],
         [SMEM] + [VMEM] * (size + inner),
-        [VMEM] * (2 + inner),
+        [VMEM] * 4,
         [pltpu.VMEM((slots * group, HEAD), BF16)] * 2,
         cost(12 * slots * group * slots * inner * HEAD, 4 * slots * width),
         "attend",
-    )(valid_count, *qds, *kvs)
-
-    terms = [kept] + [b_swap(x, s + 1) for s, x in enumerate(sent)]
+    )(valid_count, *qds, after(kvs[0], cols[1]), *kvs[1:])
+
     piece = shape((size // 2 * cap, 2 * kv_width), BF16)
-    grads, low, high = call(
-        functools.partial(total_pieces_body, size, inner, cap),
-        [block, piece, piece],
+    grads, keep, send = call(
+        functools.partial(total_body, size, inner, cap),
+        [shape(terms, BF16), piece, piece],
         [VMEM] * inner,
         [VMEM] * 3,
         (),
-        cost(slots * kv_width * 4, 16 * slots * kv_width),
+        cost(slots * inner * kv_width * 4, 16 * slots * inner * kv_width),
         "grads_total",
-    )(*terms)
-
-    held, heads, step = [low], [0], size // 2
-    out = [high]
-    while step:
-        out = out[0] if len(out) == 1 else jnp.concatenate(out, axis=0)
-        back = t_swap(out, step)
-        count = step * cap
-        held += [back[i * count : (i + 1) * count] for i in range(len(heads))]
-        heads += [h ^ step for h in heads]
-        step //= 2
-        out = [x[step * cap :] for x in held]
-        held = [x[: step * cap] if step else x for x in held]
-    head_grads = [held[heads.index(s)] for s in range(size)]
-
-    w_heads, order, step = [w_own], [0], size // 2
-    while step:
-        w_heads = w_heads + [[t_swap(x, step) for x in ws] for ws in w_heads]
-        order = order + [o ^ step for o in order]
-        step //= 2
-    w_heads = [w_heads[order.index(s)] for s in range(size)]
-
-    row_grad = call(
-        functools.partial(rows_body, size, inner),
-        shape((cap, 2 * half), BF16),
-        [VMEM] * (size + size * inner),
-        VMEM,
-        (),
+    )(kept, *[b_swap(sent, s) for s in range(1, inner)])
+    pair_grads = t_swap(send, 1)
+    w_pair = [t_swap(after(weights, first), 1)] + [
+        jnp.concatenate([k, t_swap(after(v, first), 1)], axis=1) for k, v in zip(k_pair, v_far)
+    ]
+
+    row_grads = call(
+        functools.partial(rows_body, size, inner, cap),
+        [shape((cap, 2 * half), BF16)] * (size // 2),
+        [VMEM] * (2 + 2 * inner),
+        [VMEM] * (size // 2),
+        [pltpu.VMEM((size // 2 * cap, 2 * half), BF16)],
         cost(4 * cap * size * 2 * kv_width * half, 8 * size * kv_width * half),
         "row_grad",
-    )(*head_grads, *[x for ws in w_heads for x in ws])
-    swapped = move(row_grad, lambda a, b, t: (t % 2 * (size // 2) + t // 2, b, a))
-
-    ready = after(grads, row_grad)
-    all_grads = [grads] + [b_swap(ready, s) for s in range(1, inner)]
+    )(keep, pair_grads, *w_own, *w_pair)
+    swapped = [
+        move(x, lambda a, b, t, m=m: (t % 2 * (size // 2) + (t // 2 ^ m), b, a))
+        for m, x in enumerate(row_grads)
+    ]
     key_weight_grad, value_weight_grad = call(
         functools.partial(weight_body, inner),
         [shape((depth, kv_width), BF16)] * 2,
-        [VMEM] * (2 * inner),
+        [VMEM] * (inner + 1),
         [VMEM] * 2,
         (),
         cost(4 * slots * half * 2 * kv_width, 16 * half * kv_width),
         "weight_grads",
-    )(*cols, *all_grads)
-
-    token_grad = pl.pallas_call(
-        scatter_body,
-        out_shape=shape((rows, 2 * half), BF16),
-        grid=(4,),
-        in_specs=[
-            pl.BlockSpec((cap, rows), lambda i: (0, 0)),
-            pl.BlockSpec((cap, half // 2), lambda i: (0, i)),
-        ],
-        out_specs=pl.BlockSpec((rows, half // 2), lambda i: (0, i)),
-        cost_estimate=cost(4 * rows * cap * half, 4 * rows * half),
-        name="scatter",
-    )(hot, swapped)
+    )(*cols, after(grads, row_grads[0]))
+
+    chunks = 4
+    token_grad = call(
+        functools.partial(scatter_body, size // 2),
+        shape((rows, 2 * half), BF16),
+        [VMEM] * (1 + size // 2),
+        HBM,
+        [pltpu.VMEM((rows, 2 * half), BF16), pltpu.SemaphoreType.DMA((chunks,))],
+        cost(4 * rows * cap * half, 4 * rows * half),
+        "scatter",
+    )(hot, *swapped)
     return attended, query_gradient, token_grad, key_weight_grad, value_weight_grad
 
 

time: 81.1 us -> 59.4 us (0.73)
  local copies, waits for them, and re-layouts: 7.73 us -> 0.14 us
  waiting for transfers between devices: 35 us -> 28 us
  starting transfers between devices: 25.5 us -> 19.5 us
  Pallas kernels: 11.5 us -> 9.69 us
    ppermute x6 -> x5, waiting for transfers between devices: 15 us -> 5.54 us  [b_swap(): lax.ppermute(x, 'ctx', [(j, j // inner * inner + (j % inner ^ s)) for j i...]
    ppermute x2 -> x3, waiting for transfers between devices: 1.88 us -> 10.2 us  [move(): lax.ppermute(x, ('ctx', 'tp'), [(flat(*i), flat(*target(*i))) for i in in...]
    unnamed x20 -> x4, local copies, waits for them, and re-layouts: 7.72 us -> 0.06 us
    ppermute x9 -> x5, waiting for transfers between devices: 8.51 us -> 1.12 us  [t_swap(): return lax.ppermute(x, 'tp', [(j, j ^ s) for j in range(size)])]
    ppermute x9 -> x5, starting transfers between devices: 3.42 us -> 0.15 us  [t_swap(): return lax.ppermute(x, 'tp', [(j, j ^ s) for j in range(size)])]
    pallas_call x3, Pallas kernels: 4.75 us -> 2.26 us  [the longest x1 1.47 us: local(): call(functools.partial(scatter_body, size // 2), shape((rows, 2 * half),...]
    ppermute x7, waiting for transfers between devices: 9.65 us -> 11.2 us  [a_swap(): lax.ppermute(x, 'ctx', [(j, (j // inner ^ s) * inner + j % inner) for j i...]
    ppermute x2 -> x3, starting transfers between devices: 3.58 us -> 2.48 us  [move(): lax.ppermute(x, ('ctx', 'tp'), [(flat(*i), flat(*target(*i))) for i in in...]
  transfers between devices with their start and end apart: 24 -> 20, of which waited for: 12 -> 12; matrix products, arithmetic and copies ran while one was open for 0% -> 0% of each run, Pallas kernels for 8% -> 13%
where the time goes in v2:
time: 59.4 us; the launch traced here: 58.3 us
  waiting for transfers between devices  28 us (47%)
  starting transfers between devices  19.5 us (33%)
  Pallas kernels  9.69 us (16%)
  between operations  0.82 us (1%)
    ppermute x7, waiting for transfers between devices, a_swap(): lax.ppermute(x, 'ctx', [(j, (j // inner ^ s) * inner + j % inner) for j i...  11.2 us
    ppermute x3, waiting for transfers between devices, move(): lax.ppermute(x, ('ctx', 'tp'), [(flat(*i), flat(*target(*i))) for i in in...  10.2 us
    ppermute x7, starting transfers between devices, a_swap(): lax.ppermute(x, 'ctx', [(j, (j // inner ^ s) * inner + j % inner) for j i...  10.2 us
    ppermute x5, starting transfers between devices, b_swap(): lax.ppermute(x, 'ctx', [(j, j // inner * inner + (j % inner ^ s)) for j i...  6.63 us
    ppermute x5, waiting for transfers between devices, b_swap(): lax.ppermute(x, 'ctx', [(j, j // inner * inner + (j % inner ^ s)) for j i...  5.54 us
    pallas_call x1, Pallas kernels, local(): call(functools.partial(attend_body, size, inner, cap, group), [shape((cap...  3.59 us
    ppermute x3, starting transfers between devices, move(): lax.ppermute(x, ('ctx', 'tp'), [(flat(*i), flat(*target(*i))) for i in in...  2.48 us
    pallas_call x1, Pallas kernels, local(): call(functools.partial(pick_body, size, inner, half), [shape((cap, 2 * ha...  2.23 us
  transfers between devices with their start and end apart: 20, of which 12 were waited for; matrix products, arithmetic and copies ran while one was open for 0% of the time, Pallas kernels for 13%

profile of v2, /device:TPU:4, one launch (start us, length us, event | category | flops | bytes accessed | tf_op | source)
XLA Modules:
  0.0 58.3 jit_solution(14705286385178031918)
XLA Ops:
  0.6 1.6 %collective-permute-start.6 = (bf16[1024,128]{1,0:T(8,128)(2,1)}, bf16[1024,128]{1,0:T(8,128)(2,1)S(1)}, u32[]{:S(2)}, u32[]{:S(2)}) collective-permute-start(bf16[1024,128]{1,0:T(8,128)(2,1)} %k_ref.1), channel_id=1, source_target_pairs={{0,4},{4,0},{8,12},{12,8},{16,20},{20,16},{24,28},{28,24},{1,5},{5... | collective-permute-start | bytes 786440 | tf_op jit(solution)/shard_map/ppermute | solution.py:287
  2.7 2.2 %pick.1 = (bf16[32,2048]{1,0:T(8,128)(2,1)S(1)}, bf16[32,1024]{1,0:T(8,128)(2,1)S(1)}, bf16[32,2048]{1,0:T(8,128)(2,1)S(1)}, bf16[32,2048]{1,0:T(8,128)(2,1)S(1)...) custom-call(s32[32]{0:T(128)} %select_hbm.1, s32[8]{0:T(128)} %count_ref.1, bf16[256,8192]{1,0:T(8,128)(2,1)} %tokens_ref.1, ...), custom_call_target="tpu_custom_call" | custom-call | flops 20000000000 | bytes 2097152 | tf_op jit(solution)/shard_map/pick/pallas_call | solution.py:298
  5.0 3.7 %collective-permute-start.4 = (bf16[32,1024]{1,0:T(8,128)(2,1)S(1)}, bf16[32,1024]{1,0:T(8,128)(2,1)S(1)}, u32[]{:S(2)}, u32[]{:S(2)}) collective-permute-start(bf16[32,1024]{1,0:T(8,128)(2,1)S(1)} %get-tuple-element.32), channel_id=1, source_target_pairs={{0,24},{4,28},{8,16},{12,20},{16,8},{20,12},{24,0},{28,4},{1,25},{... | collective-permute-start | bytes 196616 | tf_op jit(solution)/shard_map/ppermute | solution.py:284
  8.6 2.0 %collective-permute-start = (bf16[32,2048]{1,0:T(8,128)(2,1)S(1)}, bf16[32,2048]{1,0:T(8,128)(2,1)S(1)}, u32[]{:S(2)}, u32[]{:S(2)}) collective-permute-start(bf16[32,2048]{1,0:T(8,128)(2,1)S(1)} %get-tuple-element.30.refs_0_), channel_id=1, source_target_pairs={{0,8},{4,12},{8,0},{12,4},{16,24},{20,28},{24,16},{28,20},{1,9},{5... | collective-permute-start | bytes 393224 | tf_op jit(solution)/shard_map/ppermute | solution.py:284
  10.7 1.2 %collective-permute-done.4.refs_1_ = bf16[32,1024]{1,0:T(8,128)(2,1)S(1)} collective-permute-done((bf16[32,1024]{1,0:T(8,128)(2,1)S(1)}, bf16[32,1024]{1,0:T(8,128)(2,1)S(1)}, u32[]{:S(2)}, u32[]{:S(2)}) %collective-permute-start.4) | collective-permute-done | bytes 65568 | tf_op jit(solution)/shard_map/ppermute | solution.py:284
  11.9 3.2 %collective-permute-done.3.refs_0_ = bf16[32,2048]{1,0:T(8,128)(2,1)S(1)} collective-permute-done((bf16[32,2048]{1,0:T(8,128)(2,1)S(1)}, bf16[32,2048]{1,0:T(8,128)(2,1)S(1)}, u32[]{:S(2)}, u32[]{:S(2)}) %collective-permute-start.3) | collective-permute-done | bytes 131104 | tf_op jit(solution)/shard_map/ppermute | solution.py:295
  15.2 1.3 %collective-permute-done.refs_1_ = bf16[32,2048]{1,0:T(8,128)(2,1)S(1)} collective-permute-done((bf16[32,2048]{1,0:T(8,128)(2,1)S(1)}, bf16[32,2048]{1,0:T(8,128)(2,1)S(1)}, u32[]{:S(2)}, u32[]{:S(2)}) %collective-permute-start) | collective-permute-done | bytes 131104 | tf_op jit(solution)/shard_map/ppermute | solution.py:284
  17.6 2.3 %collective-permute-start.8 = (bf16[128,256]{1,0:T(8,128)(2,1)S(1)}, bf16[128,256]{1,0:T(8,128)(2,1)S(1)}, u32[]{:S(2)}, u32[]{:S(2)}) collective-permute-start(bf16[128,256]{1,0:T(8,128)(2,1)S(1)} %get-tuple-element.35), channel_id=1, source_target_pairs={{0,8},{4,12},{8,0},{12,4},{16,24},{20,28},{24,16},{28,20},{1,9},{5... | collective-permute-start | bytes 196616 | tf_op jit(solution)/shard_map/ppermute | solution.py:284
  19.9 1.7 %collective-permute-start.10 = (bf16[128,256]{1,0:T(8,128)(2,1)S(1)}, bf16[128,256]{1,0:T(8,128)(2,1)S(1)}, u32[]{:S(2)}, u32[]{:S(2)}) collective-permute-start(bf16[128,256]{1,0:T(8,128)(2,1)S(1)} %get-tuple-element.35), channel_id=1, source_target_pairs={{0,24},{4,28},{8,16},{12,20},{16,8},{20,12},{24,0},{28,4},{1,25},{... | collective-permute-start | bytes 196616 | tf_op jit(solution)/shard_map/ppermute | solution.py:284
  22.7 1.5 %collective-permute-start.11 = (bf16[128,1024]{1,0:T(8,128)(2,1)S(1)}, bf16[128,1024]{1,0:T(8,128)(2,1)S(1)}, u32[]{:S(2)}, u32[]{:S(2)}) collective-permute-start(bf16[128,1024]{1,0:T(8,128)(2,1)S(1)} %get-tuple-element.37), channel_id=1, source_target_pairs={{0,4},{4,0},{8,12},{12,8},{16,20},{20,16},{24,28},{28,24},{1,5},{5... | collective-permute-start | bytes 786440 | tf_op jit(solution)/shard_map/ppermute | solution.py:287
  24.1 4.2 %collective-permute-done.1.refs_2_ = bf16[64,1024]{1,0:T(8,128)(2,1)S(1)} collective-permute-done((bf16[64,1024]{1,0:T(8,128)(2,1)S(1)}, bf16[64,1024]{1,0:T(8,128)(2,1)S(1)}, u32[]{:S(2)}, u32[]{:S(2)}) %collective-permute-start.1) | collective-permute-done | bytes 131104 | tf_op jit(solution)/shard_map/ppermute | solution.py:284
  28.4 2.2 %collective-permute-done.9 = bf16[128,256]{1,0:T(8,128)(2,1)S(1)} collective-permute-done((bf16[128,256]{1,0:T(8,128)(2,1)S(1)}, bf16[128,256]{1,0:T(8,128)(2,1)S(1)}, u32[]{:S(2)}, u32[]{:S(2)}) %collective-permute-start.9) | collective-permute-done | bytes 65568 | tf_op jit(solution)/shard_map/ppermute | solution.py:284
  30.7 1.6 %collective-permute-start.12 = (bf16[128,256]{1,0:T(8,128)(2,1)S(1)}, bf16[128,256]{1,0:T(8,128)(2,1)S(1)}, u32[]{:S(2)}, u32[]{:S(2)}) collective-permute-start(bf16[128,256]{1,0:T(8,128)(2,1)S(1)} %add_convert_fusion.refs_4_), channel_id=1, source_target_pairs={{0,4},{4,0},{8,12},{12,8},{16,20},{20,16},{24,28},{28,24},{1,5},{5... | collective-permute-start | bytes 196616 | tf_op jit(solution)/shard_map/ppermute | solution.py:287
  32.3 1.1 %collective-permute-done.2.refs_3_ = bf16[64,1024]{1,0:T(8,128)(2,1)S(1)} collective-permute-done((bf16[64,1024]{1,0:T(8,128)(2,1)S(1)}, bf16[64,1024]{1,0:T(8,128)(2,1)S(1)}, u32[]{:S(2)}, u32[]{:S(2)}) %collective-permute-start.2) | collective-permute-done | bytes 131104 | tf_op jit(solution)/shard_map/ppermute | solution.py:284
  33.4 1.9 %collective-permute-done.12.refs_5_ = bf16[128,256]{1,0:T(8,128)(2,1)S(1)} collective-permute-done((bf16[128,256]{1,0:T(8,128)(2,1)S(1)}, bf16[128,256]{1,0:T(8,128)(2,1)S(1)}, u32[]{:S(2)}, u32[]{:S(2)}) %collective-permute-start.12) | collective-permute-done | bytes 65568 | tf_op jit(solution)/shard_map/ppermute | solution.py:287
  35.3 3.6 %attend.1 = (bf16[32,1024]{1,0:T(8,128)(2,1)}, bf16[32,1024]{1,0:T(8,128)(2,1)}, f32[256,256]{1,0:T(8,128)S(1)}, bf16[256,256]{1,0:T(8,128)(2,1)S(1)}) custom-call(s32[8]{0:T(128)S(1)} %copy-done, bf16[32,2048]{1,0:T(8,128)(2,1)S(1)} %get-tuple-element.30.refs_0_, bf16[32,2048]{1,0:T(8,128)(2,1)S(1)} %collective-permute-done.refs_1_, ...), custom_call_target="tpu_custom_call" | custom-call | flops 402653184 | bytes 524288 | tf_op jit(solution)/shard_map/attend/pallas_call | solution.py:350
  38.9 1.5 %collective-permute-start.13 = (bf16[256,256]{1,0:T(8,128)(2,1)S(1)}, bf16[256,256]{1,0:T(8,128)(2,1)S(1)}, u32[]{:S(2)}, u32[]{:S(2)}) collective-permute-start(bf16[256,256]{1,0:T(8,128)(2,1)S(1)} %get-tuple-element.43), channel_id=1, source_target_pairs={{0,4},{4,0},{8,12},{12,8},{16,20},{20,16},{24,28},{28,24},{1,5},{5... | collective-permute-start | bytes 393224 | tf_op jit(solution)/shard_map/ppermute | solution.py:287
  40.4 3.6 %collective-permute-done.13.refs_1_ = bf16[256,256]{1,0:T(8,128)(2,1)S(1)} collective-permute-done((bf16[256,256]{1,0:T(8,128)(2,1)S(1)}, bf16[256,256]{1,0:T(8,128)(2,1)S(1)}, u32[]{:S(2)}, u32[]{:S(2)}) %collective-permute-start.13) | collective-permute-done | bytes 131104 | tf_op jit(solution)/shard_map/ppermute | solution.py:287
  44.2 1.1 %collective-permute-done.14.refs_1_ = bf16[64,256]{1,0:T(8,128)(2,1)S(1)} collective-permute-done((bf16[64,256]{1,0:T(8,128)(2,1)S(1)}, bf16[64,256]{1,0:T(8,128)(2,1)S(1)}, u32[]{:S(2)}, u32[]{:S(2)}) %collective-permute-start.14) | collective-permute-done | bytes 32800 | tf_op jit(solution)/shard_map/ppermute | solution.py:290
  46.6 1.9 %collective-permute-start.18 = (bf16[32,2048]{1,0:T(8,128)(2,1)S(1)}, bf16[32,2048]{1,0:T(8,128)(2,1)S(1)}, u32[]{:S(2)}, u32[]{:S(2)}) collective-permute-start(bf16[32,2048]{1,0:T(8,128)(2,1)S(1)} %get-tuple-element.48), channel_id=1, source_target_pairs={{0,0},{1,16},{2,8},{3,24},{4,4},{5,20},{6,12},{7,28},{8,1},{9,17},... | collective-permute-start | bytes 393224 | tf_op jit(solution)/shard_map/ppermute | solution.py:295
  48.6 1.3 %weight_grads.1 = (bf16[1024,128]{1,0:T(8,128)(2,1)}, bf16[1024,128]{1,0:T(8,128)(2,1)}) custom-call(bf16[128,1024]{1,0:T(8,128)(2,1)S(1)} %get-tuple-element.50.refs_0_, bf16[128,1024]{1,0:T(8,128)(2,1)S(1)} %collective-permute-done.11.refs_1_, bf16[256,256]{1,0:T(8,128)(2,1)S(1)} %get-tuple-element.52.refs_2_), custom_call_target="tpu_custom_call" | custom-call | flops 134217728 | bytes 2097152 | tf_op jit(solution)/shard_map/weight_grads/pallas_call | solution.py:388
  49.8 5.0 %collective-permute-done.19.refs_1_ = bf16[32,2048]{1,0:T(8,128)(2,1)S(1)} collective-permute-done((bf16[32,2048]{1,0:T(8,128)(2,1)S(1)}, bf16[32,2048]{1,0:T(8,128)(2,1)S(1)}, u32[]{:S(2)}, u32[]{:S(2)}) %collective-permute-start.19) | collective-permute-done | bytes 131104 | tf_op jit(solution)/shard_map/ppermute | solution.py:295
  54.9 1.9 %collective-permute-done.18.refs_0_ = bf16[32,2048]{1,0:T(8,128)(2,1)S(1)} collective-permute-done((bf16[32,2048]{1,0:T(8,128)(2,1)S(1)}, bf16[32,2048]{1,0:T(8,128)(2,1)S(1)}, u32[]{:S(2)}, u32[]{:S(2)}) %collective-permute-start.18) | collective-permute-done | bytes 131104 | tf_op jit(solution)/shard_map/ppermute | solution.py:295
  56.8 1.5 %scatter.1 = bf16[256,2048]{1,0:T(8,128)(2,1)} custom-call(bf16[32,256]{1,0:T(8,128)(2,1)S(1)} %get-tuple-element.41.hot_ref, bf16[32,2048]{1,0:T(8,128)(2,1)S(1)} %collective-permute-done.18.refs_0_, bf16[32,2048]{1,0:T(8,128)(2,1)S(1)} %collective-permute-done.19.refs_1_), custom_call_target="tpu_custom_call" | custom-call | flops 33554432 | bytes 1048576 | tf_op jit(solution)/shard_map/scatter/pallas_call | solution.py:399
  (33 shorter events, 4.3 us)
Async XLA Ops:
  0.6 16.5 %collective-permute-start.6 = (bf16[1024,128]{1,0:T(8,128)(2,1)}, bf16[1024,128]{1,0:T(8,128)(2,1)S(1)}, u32[]{:S(2)}, u32[]{:S(2)}) collective-permute-start(bf16[1024,128]{1,0:T(8,128)(2,1)} %k_ref.1), channel_id=1, source_target_pairs={{0,4},{4,0},{8,12},{12,8},{16,20},{20,16},{24,28},{28,24},{1,5},{5... | collective-permute-start | bytes 786440 | tf_op jit(solution)/shard_map/ppermute | solution.py:287
  2.2 15.0 %collective-permute-start.7 = (bf16[1024,128]{1,0:T(8,128)(2,1)}, bf16[1024,128]{1,0:T(8,128)(2,1)S(1)}, u32[]{:S(2)}, u32[]{:S(2)}) collective-permute-start(bf16[1024,128]{1,0:T(8,128)(2,1)} %v_ref.1), channel_id=1, source_target_pairs={{0,4},{4,0},{8,12},{12,8},{16,20},{20,16},{24,28},{28,24},{1,5},{5... | collective-permute-start | bytes 786440 | tf_op jit(solution)/shard_map/ppermute | solution.py:287
  5.0 6.9 %collective-permute-start.4 = (bf16[32,1024]{1,0:T(8,128)(2,1)S(1)}, bf16[32,1024]{1,0:T(8,128)(2,1)S(1)}, u32[]{:S(2)}, u32[]{:S(2)}) collective-permute-start(bf16[32,1024]{1,0:T(8,128)(2,1)S(1)} %get-tuple-element.32), channel_id=1, source_target_pairs={{0,24},{4,28},{8,16},{12,20},{16,8},{20,12},{24,0},{28,4},{1,25},{... | collective-permute-start | bytes 196616 | tf_op jit(solution)/shard_map/ppermute | solution.py:284
  8.6 6.5 %collective-permute-start.3 = (bf16[32,2048]{1,0:T(8,128)(2,1)S(1)}, bf16[32,2048]{1,0:T(8,128)(2,1)S(1)}, u32[]{:S(2)}, u32[]{:S(2)}) collective-permute-start(bf16[32,2048]{1,0:T(8,128)(2,1)S(1)} %get-tuple-element.31), channel_id=1, source_target_pairs={{0,8},{1,17},{2,10},{3,19},{4,12},{5,21},{6,14},{7,23},{8,0},{9,25... | collective-permute-start | bytes 393224 | tf_op jit(solution)/shard_map/ppermute | solution.py:295
  8.6 7.9 %collective-permute-start = (bf16[32,2048]{1,0:T(8,128)(2,1)S(1)}, bf16[32,2048]{1,0:T(8,128)(2,1)S(1)}, u32[]{:S(2)}, u32[]{:S(2)}) collective-permute-start(bf16[32,2048]{1,0:T(8,128)(2,1)S(1)} %get-tuple-element.30.refs_0_), channel_id=1, source_target_pairs={{0,8},{4,12},{8,0},{12,4},{16,24},{20,28},{24,16},{28,20},{1,9},{5... | collective-permute-start | bytes 393224 | tf_op jit(solution)/shard_map/ppermute | solution.py:284
  15.2 2.1 %collective-permute-start.5 = (bf16[32,3072]{1,0:T(8,128)(2,1)S(1)}, bf16[32,3072]{1,0:T(8,128)(2,1)S(1)}, u32[]{:S(2)}, u32[]{:S(2)}) collective-permute-start(bf16[32,3072]{1,0:T(8,128)(2,1)S(1)} %pad_maximum_fusion.1), channel_id=1, source_target_pairs={{0,1},{1,0},{2,3},{3,2},{4,5},{5,4},{6,7},{7,6},{8,9},{9,8},{10,11... | collective-permute-start | bytes 589832 | tf_op jit(solution)/shard_map/ppermute | solution.py:290
  16.6 11.8 %collective-permute-start.1 = (bf16[64,1024]{1,0:T(8,128)(2,1)S(1)}, bf16[64,1024]{1,0:T(8,128)(2,1)S(1)}, u32[]{:S(2)}, u32[]{:S(2)}) collective-permute-start(bf16[64,1024]{1,0:T(8,128)(2,1)S(1)} %slice_select_fusion), channel_id=1, source_target_pairs={{0,16},{4,20},{8,24},{12,28},{16,0},{20,4},{24,8},{28,12},{1,17},{... | collective-permute-start | bytes 393224 | tf_op jit(solution)/shard_map/ppermute | solution.py:284
  17.3 18.0 %copy-start = (s32[8]{0:T(128)S(1)}, s32[8]{0:T(128)}, u32[]{:S(2)}) copy-start(s32[8]{0:T(128)} %count_ref.1) | copy-start | bytes 100
  17.6 5.0 %collective-permute-start.8 = (bf16[128,256]{1,0:T(8,128)(2,1)S(1)}, bf16[128,256]{1,0:T(8,128)(2,1)S(1)}, u32[]{:S(2)}, u32[]{:S(2)}) collective-permute-start(bf16[128,256]{1,0:T(8,128)(2,1)S(1)} %get-tuple-element.35), channel_id=1, source_target_pairs={{0,8},{4,12},{8,0},{12,4},{16,24},{20,28},{24,16},{28,20},{1,9},{5... | collective-permute-start | bytes 196616 | tf_op jit(solution)/shard_map/ppermute | solution.py:284
  19.9 8.5 %collective-permute-start.10 = (bf16[128,256]{1,0:T(8,128)(2,1)S(1)}, bf16[128,256]{1,0:T(8,128)(2,1)S(1)}, u32[]{:S(2)}, u32[]{:S(2)}) collective-permute-start(bf16[128,256]{1,0:T(8,128)(2,1)S(1)} %get-tuple-element.35), channel_id=1, source_target_pairs={{0,24},{4,28},{8,16},{12,20},{16,8},{20,12},{24,0},{28,4},{1,25},{... | collective-permute-start | bytes 196616 | tf_op jit(solution)/shard_map/ppermute | solution.py:284
  21.6 9.0 %collective-permute-start.9 = (bf16[128,256]{1,0:T(8,128)(2,1)S(1)}, bf16[128,256]{1,0:T(8,128)(2,1)S(1)}, u32[]{:S(2)}, u32[]{:S(2)}) collective-permute-start(bf16[128,256]{1,0:T(8,128)(2,1)S(1)} %get-tuple-element.35), channel_id=1, source_target_pairs={{0,16},{4,20},{8,24},{12,28},{16,0},{20,4},{24,8},{28,12},{1,17},{... | collective-permute-start | bytes 196616 | tf_op jit(solution)/shard_map/ppermute | solution.py:284
  22.7 8.0 %collective-permute-start.11 = (bf16[128,1024]{1,0:T(8,128)(2,1)S(1)}, bf16[128,1024]{1,0:T(8,128)(2,1)S(1)}, u32[]{:S(2)}, u32[]{:S(2)}) collective-permute-start(bf16[128,1024]{1,0:T(8,128)(2,1)S(1)} %get-tuple-element.37), channel_id=1, source_target_pairs={{0,4},{4,0},{8,12},{12,8},{16,20},{20,16},{24,28},{28,24},{1,5},{5... | collective-permute-start | bytes 786440 | tf_op jit(solution)/shard_map/ppermute | solution.py:287
  24.1 20.0 %collective-permute-start.16 = (bf16[1024,128]{1,0:T(8,128)(2,1)S(1)}, bf16[1024,128]{1,0:T(8,128)(2,1)S(1)}, u32[]{:S(2)}, u32[]{:S(2)}) collective-permute-start(bf16[1024,128]{1,0:T(8,128)(2,1)S(1)} %collective-permute-done.6), channel_id=1, source_target_pairs={{0,1},{1,0},{2,3},{3,2},{4,5},{5,4},{6,7},{7,6},{8,9},{9,8},{10,11... | collective-permute-start | bytes 786440 | tf_op jit(solution)/shard_map/ppermute | solution.py:290
  28.4 5.0 %collective-permute-start.2 = (bf16[64,1024]{1,0:T(8,128)(2,1)S(1)}, bf16[64,1024]{1,0:T(8,128)(2,1)S(1)}, u32[]{:S(2)}, u32[]{:S(2)}) collective-permute-start(bf16[64,1024]{1,0:T(8,128)(2,1)S(1)} %collective-permute-done.1.refs_2_), channel_id=1, source_target_pairs={{0,8},{4,12},{8,0},{12,4},{16,24},{20,28},{24,16},{28,20},{1,9},{5... | collective-permute-start | bytes 393224 | tf_op jit(solution)/shard_map/ppermute | solution.py:284
  28.4 15.7 %collective-permute-start.17 = (bf16[1024,128]{1,0:T(8,128)(2,1)S(1)}, bf16[1024,128]{1,0:T(8,128)(2,1)S(1)}, u32[]{:S(2)}, u32[]{:S(2)}) collective-permute-start(bf16[1024,128]{1,0:T(8,128)(2,1)S(1)} %collective-permute-done.7), channel_id=1, source_target_pairs={{0,1},{1,0},{2,3},{3,2},{4,5},{5,4},{6,7},{7,6},{8,9},{9,8},{10,11... | collective-permute-start | bytes 786440 | tf_op jit(solution)/shard_map/ppermute | solution.py:290
  30.6 14.7 %collective-permute-start.15 = (bf16[1024,256]{1,0:T(8,128)(2,1)S(1)}, bf16[1024,256]{1,0:T(8,128)(2,1)S(1)}, u32[]{:S(2)}, u32[]{:S(2)}) collective-permute-start(bf16[1024,256]{1,0:T(8,128)(2,1)S(1)} %get-tuple-element.46.refs_4_.refs_2_), channel_id=1, source_target_pairs={{0,1},{1,0},{2,3},{3,2},{4,5},{5,4},{6,7},{7,6},{8,9},{9,8},{10,11... | collective-permute-start | bytes 1572872 | tf_op jit(solution)/shard_map/ppermute | solution.py:290
  30.7 4.6 %collective-permute-start.12 = (bf16[128,256]{1,0:T(8,128)(2,1)S(1)}, bf16[128,256]{1,0:T(8,128)(2,1)S(1)}, u32[]{:S(2)}, u32[]{:S(2)}) collective-permute-start(bf16[128,256]{1,0:T(8,128)(2,1)S(1)} %add_convert_fusion.refs_4_), channel_id=1, source_target_pairs={{0,4},{4,0},{8,12},{12,8},{16,20},{20,16},{24,28},{28,24},{1,5},{5... | collective-permute-start | bytes 196616 | tf_op jit(solution)/shard_map/ppermute | solution.py:287
  38.9 5.1 %collective-permute-start.13 = (bf16[256,256]{1,0:T(8,128)(2,1)S(1)}, bf16[256,256]{1,0:T(8,128)(2,1)S(1)}, u32[]{:S(2)}, u32[]{:S(2)}) collective-permute-start(bf16[256,256]{1,0:T(8,128)(2,1)S(1)} %get-tuple-element.43), channel_id=1, source_target_pairs={{0,4},{4,0},{8,12},{12,8},{16,20},{20,16},{24,28},{28,24},{1,5},{5... | collective-permute-start | bytes 393224 | tf_op jit(solution)/shard_map/ppermute | solution.py:287
  44.0 1.3 %collective-permute-start.14 = (bf16[64,256]{1,0:T(8,128)(2,1)S(1)}, bf16[64,256]{1,0:T(8,128)(2,1)S(1)}, u32[]{:S(2)}, u32[]{:S(2)}) collective-permute-start(bf16[64,256]{1,0:T(8,128)(2,1)S(1)} %get-tuple-element.45), channel_id=1, source_target_pairs={{0,1},{1,0},{2,3},{3,2},{4,5},{5,4},{6,7},{7,6},{8,9},{9,8},{10,11... | collective-permute-start | bytes 98312 | tf_op jit(solution)/shard_map/ppermute | solution.py:290
  46.1 8.8 %collective-permute-start.19 = (bf16[32,2048]{1,0:T(8,128)(2,1)S(1)}, bf16[32,2048]{1,0:T(8,128)(2,1)S(1)}, u32[]{:S(2)}, u32[]{:S(2)}) collective-permute-start(bf16[32,2048]{1,0:T(8,128)(2,1)S(1)} %get-tuple-element.49), channel_id=1, source_target_pairs={{0,8},{1,24},{2,0},{3,16},{4,12},{5,28},{6,4},{7,20},{8,9},{9,25},... | collective-permute-start | bytes 393224 | tf_op jit(solution)/shard_map/ppermute | solution.py:295
  46.6 10.2 %collective-permute-start.18 = (bf16[32,2048]{1,0:T(8,128)(2,1)S(1)}, bf16[32,2048]{1,0:T(8,128)(2,1)S(1)}, u32[]{:S(2)}, u32[]{:S(2)}) collective-permute-start(bf16[32,2048]{1,0:T(8,128)(2,1)S(1)} %get-tuple-element.48), channel_id=1, source_target_pairs={{0,0},{1,16},{2,8},{3,24},{4,4},{5,20},{6,12},{7,28},{8,1},{9,17},... | collective-permute-start | bytes 393224 | tf_op jit(solution)/shard_map/ppermute | solution.py:295

commit v3 on v2

--- a/solution.py
+++ b/solution.py
@@ -60,8 +60,8 @@
     size, inner, half, select_hbm, count_hbm, tokens_ref, q_ref, og_ref, k_ref, v_ref, *rest
 ):
     pairs = size // 2 - 1
-    outs, (qd_ref, w_ref, hot_ref) = rest[: pairs + 2], rest[pairs + 2 : pairs + 5]
-    select_ref, count_ref, buf, sems, side = rest[pairs + 5 :]
+    outs, (qd_ref, w_ref, hot_ref, live_ref, order_ref) = rest[: pairs + 2], rest[pairs + 2 : pairs + 7]
+    select_ref, count_ref, buf, og_buf, sems, side = rest[pairs + 7 :]
     a, b, t = place(inner)
     cap, rows = outs[0].shape[0], tokens_ref.shape[0]
     width = q_ref.shape[1]
@@ -87,7 +87,7 @@
         copies[i].start()
     others = [
         pltpu.make_async_copy(q_ref, qd_ref.at[:, :width], side.at[2]),
-        pltpu.make_async_copy(og_ref, qd_ref.at[:, width:], side.at[3]),
+        pltpu.make_async_copy(og_ref, og_buf, side.at[3]),
         pltpu.make_async_copy(k_ref, w_ref.at[:, : k_ref.shape[1]], side.at[4]),
         pltpu.make_async_copy(v_ref, w_ref.at[:, k_ref.shape[1] :], side.at[5]),
     ]
@@ -103,8 +103,16 @@
         copies[i].wait()
         wide = outs[i].shape[1]
         outs[i][...] = dot(hot, buf[:, 2 * half * i : 2 * half * i + wide], 1, 0).astype(BF16)
+    row = lax.broadcasted_iota(jnp.int32, (cap, HEAD), 0)
+    live_ref[...] = jnp.where(row < count_ref[a * inner + b], 1.0, 0.0)
+    for s in range(inner):
+        for z in range(size):
+            shard = z * inner + (b ^ s)
+            at = jnp.where(row < count_ref[shard], shard * cap + row, HIDDEN)
+            order_ref[(s * size + z) * cap : (s * size + z + 1) * cap, :] = at
     for c in others:
         c.wait()
+    qd_ref[:, width:] = og_buf[...] * live_ref[:, :1].astype(BF16)
 
 
 def project_body(size, inner, half, *refs):
@@ -138,20 +146,18 @@
     part_ref[...] = total.astype(BF16)
 
 
-def attend_body(size, inner, cap, group, count_ref, *refs):
+def attend_body(size, inner, cap, group, live_ref, order_ref, *refs):
     qds, kvs = refs[:size], refs[size : size + inner]
     att_ref, dq_ref, kept_ref, sent_ref, q_all, do_all = refs[size + inner :]
     a, b, t = place(inner)
     width = group * HEAD
     block = group * cap
     scale = 1.0 / math.sqrt(HEAD)
-    slot = lax.broadcasted_iota(jnp.int32, (cap, HEAD), 0)
     far, far_other = qds[2][...], qds[3][...]
     swapped = jnp.concatenate([far_other[cap:], far_other[:cap]], axis=0)
     odd = lax.rem(a, 2) == 1
     far_q, far_do = jnp.where(odd, swapped, far), jnp.where(odd, far, swapped)
     for s in range(size):
-        count = count_ref[(a ^ s) * inner + b]
         if s < 2:
             q_rows, do_rows = qds[s][:, :width], qds[s][:, width:]
         else:
@@ -160,52 +166,46 @@
         for g in range(group):
             to = slice(s * block + g * cap, s * block + (g + 1) * cap)
             q_all[to, :] = q_rows[:, g * HEAD : (g + 1) * HEAD]
-            rows = do_rows[:, g * HEAD : (g + 1) * HEAD]
-            do_all[to, :] = jnp.where(slot < count, rows.astype(F32), 0.0).astype(BF16)
+            do_all[to, :] = do_rows[:, g * HEAD : (g + 1) * HEAD]
     kv = jnp.concatenate([r[...] for r in kvs], axis=0)
     keys, values = kv[:, :HEAD], kv[:, HEAD:]
     keys_t = keys.astype(F32).T.astype(BF16)
     values_t = values.astype(F32).T.astype(BF16)
-    row = lax.broadcasted_iota(jnp.int32, (cap, block), 0)
-    pieces = []
-    for s in range(inner):
-        for z in range(size):
-            shard = z * inner + (b ^ s)
-            pieces.append(jnp.where(row < count_ref[shard], shard * cap + row, HIDDEN))
-    key_at = jnp.concatenate(pieces, axis=0)
-    column = lax.rem(lax.broadcasted_iota(jnp.int32, (1, block), 1), cap)
+    key_at = order_ref[:, :1]
+    step = size if kv.shape[0] <= 512 else 1
     dk = dv = None
-    for s in range(size):
-        shard = (a ^ s) * inner + b
-        live = column < count_ref[shard]
-        q = q_all[s * block : (s + 1) * block, :]
-        do = do_all[s * block : (s + 1) * block, :]
+    for s in range(0, size, step):
+        cols = slice(s * block, (s + step) * block)
+        column = lax.broadcasted_iota(jnp.int32, (1, step * block), 1)
+        shard = ((a ^ (s + column // block)) * inner) + b
+        query_at = shard * cap + lax.rem(column, cap)
+        q, do = q_all[cols, :], do_all[cols, :]
         scores = dot(keys, q, 1, 1) * scale
-        scores = jnp.where(key_at <= shard * cap + column, scores, NEG)
+        scores = jnp.where(key_at <= query_at, scores, NEG)
         terms = jnp.exp(scores - jnp.max(scores, axis=0, keepdims=True))
         probs = terms * (1.0 / jnp.sum(terms, axis=0, keepdims=True))
         weights = probs.astype(BF16)
-        att = jnp.where(live, dot(values_t, weights, 1, 0), 0.0).astype(BF16).astype(F32)
-        do_t = do.astype(F32).T
-        out_dot = jnp.sum(do_t * att, axis=0, keepdims=True)
+        att = dot(values_t, weights, 1, 0).astype(BF16).astype(F32)
+        out_dot = jnp.sum(do.astype(F32).T * att, axis=0, keepdims=True)
         grad_probs = dot(values, do, 1, 1)
         grad_scores = (probs * (grad_probs - out_dot) * scale).astype(BF16)
         k_term, v_term = dot(grad_scores, q, 1, 0), dot(weights, do, 1, 0)
         dk = k_term if dk is None else dk + k_term
         dv = v_term if dv is None else dv + v_term
         if s == 0:
-            att_rows = att.T.astype(BF16)
-            dq_rows = dot(keys_t, grad_scores, 1, 0).T.astype(BF16)
+            att_rows = att[:, :block].T
+            dq_rows = dot(keys_t, grad_scores[:, :block], 1, 0).T.astype(BF16)
             for g in range(group):
-                att_ref[:, g * HEAD : (g + 1) * HEAD] = att_rows[g * cap : (g + 1) * cap, :]
-                dq_ref[:, g * HEAD : (g + 1) * HEAD] = dq_rows[g * cap : (g + 1) * cap, :]
+                rows, to = slice(g * cap, (g + 1) * cap), slice(g * HEAD, (g + 1) * HEAD)
+                att_ref[:, to] = (att_rows[rows, :] * live_ref[...]).astype(BF16)
+                dq_ref[:, to] = dq_rows[rows, :]
     for ref in (kept_ref, sent_ref):
         ref[:, :HEAD] = dk.astype(ref.dtype)
         ref[:, HEAD:] = dv.astype(ref.dtype)
 
 
 def total_body(size, inner, cap, *refs):
-    terms, (grads_ref, keep_ref, send_ref) = refs[:inner], refs[inner:]
+    terms, weights, (grads_ref, keep_ref, send_ref) = refs[:inner], refs[inner : 2 * inner], refs[2 * inner :]
     slots = size * cap
     for s in range(inner):
         total = None
@@ -213,14 +213,21 @@
             term = terms[j][(s ^ j) * slots : ((s ^ j) + 1) * slots, :].astype(F32)
             total = term if total is None else total + term
         grads_ref[s * slots : (s + 1) * slots, :] = total.astype(BF16)
+    a, b, t = place(inner)
     rows = slots // 2
-    core = lax.rem(lax.axis_index("tp"), 2)
-    keep_ref[...] = grads_ref[pl.ds(pl.multiple_of(core * rows, rows), rows), :]
-    send_ref[...] = grads_ref[pl.ds(pl.multiple_of((1 - core) * rows, rows), rows), :]
+    core = lax.rem(t, 2)
+    depth = weights[0].shape[0]
+    for ref, side in ((send_ref, 1 - core), (keep_ref, core)):
+        part = grads_ref[pl.ds(pl.multiple_of(side * rows, rows), rows), :]
+        for j in range(inner):
+            term = dot(part, weights[j][...], 1, 1)
+            ref[:, pl.ds(pl.multiple_of((b ^ j) * depth, 128), depth)] = term.astype(ref.dtype)
 
 
 def weight_body(inner, *refs):
-    cols, (grads_ref, k_ref, v_ref) = refs[:inner], refs[inner:]
+    cols, (grads_ref, att_ref, dq_ref, k_ref, v_ref, att_out, dq_out) = refs[:inner], refs[inner:]
+    att_out[...] = att_ref[...]
+    dq_out[...] = dq_ref[...]
     slots = cols[0].shape[0]
     total = None
     for s in range(inner):
@@ -231,17 +238,11 @@
     v_ref[...] = total[:, width:].astype(BF16)
 
 
-def rows_body(size, inner, cap, *refs):
-    own, pair, weights, outs = refs[0], refs[1], refs[2 : 2 + 2 * inner], refs[2 + 2 * inner :]
-    outs, total_ref = outs[:-1], outs[-1]
-    a, b, t = place(inner)
-    depth = weights[0].shape[0]
-    for j in range(inner):
-        total = dot(own[...], weights[j][...], 1, 1) + dot(pair[...], weights[inner + j][...], 1, 1)
-        total_ref[:, pl.ds(pl.multiple_of((b ^ j) * depth, 128), depth)] = total.astype(BF16)
+def pair_body(cap, keep_ref, got_ref, *outs):
+    t = lax.axis_index("tp")
     for m in range(len(outs)):
-        at = (t // 2) ^ m
-        outs[m][...] = total_ref[pl.ds(pl.multiple_of(at * cap, cap), cap), :]
+        at = pl.ds(pl.multiple_of(((t // 2) ^ m) * cap, cap), cap)
+        outs[m][...] = (keep_ref[at, :] + got_ref[at, :].astype(F32)).astype(BF16)
 
 
 def scatter_body(parts, hot_ref, *refs):
@@ -295,18 +296,20 @@
         return lax.ppermute(x, ("ctx", "tp"), [(flat(*i), flat(*target(*i))) for i in index])
 
     inputs = (select_index, valid_count, tokens, queries, out_grad, key_matrix, value_matrix)
-    *picked, own, qd, weights, hot = call(
+    *picked, own, qd, weights, hot, live, order = call(
         functools.partial(pick_body, size, inner, half),
         [shape((cap, 2 * half), BF16)] * pairs
         + [shape((cap, half), BF16), shape((cap, 2 * half), BF16)]
         + [shape((cap, 2 * width), BF16), shape((depth, 2 * kv_width), BF16)]
-        + [shape((cap, rows), BF16)],
+        + [shape((cap, rows), BF16), shape((cap, HEAD), F32)]
+        + [shape((slots * inner, HEAD), jnp.int32)],
         [HBM] * 7,
-        [VMEM] * (pairs + 5),
+        [VMEM] * (pairs + 7),
         [
             pltpu.SMEM((cap,), jnp.int32),
             pltpu.SMEM((ctx,), jnp.int32),
             pltpu.VMEM((rows, 2 * half * (pairs + 2)), BF16),
+            pltpu.VMEM((cap, width), BF16),
             pltpu.SemaphoreType.DMA((pairs + 2,)),
             pltpu.SemaphoreType.DMA((6,)),
         ],
@@ -316,17 +319,13 @@
     got = [
         move(picked[i], lambda a, b, t, i=i: (a ^ (2 * i + 1 + t % 2), b, t)) for i in range(pairs)
     ] + [a_swap(picked[pairs], size - 1)]
-    k_far = [b_swap(key_matrix, s) for s in range(1, inner)]
-    v_far = [b_swap(value_matrix, s) for s in range(1, inner)]
-    w_own = [weights] + [jnp.concatenate(x, axis=1) for x in zip(k_far, v_far)]
-    k_pair = [t_swap(x, 1) for x in k_far]
+    w_far = [[b_swap(x, s) for x in (key_matrix, value_matrix)] for s in range(1, inner)]
+    w_own = [weights] + [jnp.concatenate(x, axis=1) for x in w_far]
     other = t_swap(jnp.concatenate(got, axis=1), 1)
     near = a_swap(qd, 1)
     both = jnp.concatenate([qd, near], axis=0)
     odd = lax.rem(lax.axis_index("ctx") // inner, 2) == 1
     far = a_swap(jnp.where(odd, both[:, width:], both[:, :width]), 2)
-    far_other = a_swap(far, 1)
-    qds = [qd, near, far, far_other]
 
     part, *cols = call(
         functools.partial(project_body, size, inner, half),
@@ -340,60 +339,57 @@
     )(*got, other, own, *w_own)
     parts = [part] + [a_swap(part, s) for s in range(1, size)]
     first = parts[1]
-    cols = cols[:1] + [b_swap(after(x, first), s + 1) for s, x in enumerate(cols[1:])]
+    cols = cols[:1] + [b_swap(x, s + 1) for s, x in enumerate(cols[1:])]
     while len(parts) > 1:
         parts = [x.astype(F32) + y.astype(F32) for x, y in zip(parts[::2], parts[1::2])]
     kv = parts[0].astype(BF16)
     kvs = [kv] + [b_swap(kv, s) for s in range(1, inner)]
+    far_other = a_swap(after(far, first), 1)
+    qds = [qd, near, far, far_other]
 
     terms = (slots * inner, 2 * kv_width)
     attended, query_gradient, kept, sent = call(
         functools.partial(attend_body, size, inner, cap, group),
         [shape((cap, width), BF16)] * 2 + [shape(terms, F32), shape(terms, BF16)],
-        [SMEM] + [VMEM] * (size + inner),
+        [VMEM] * (2 + size + inner),
         [VMEM] * 4,
         [pltpu.VMEM((slots * group, HEAD), BF16)] * 2,
         cost(12 * slots * group * slots * inner * HEAD, 4 * slots * width),
         "attend",
-    )(valid_count, *qds, after(kvs[0], cols[1]), *kvs[1:])
-
-    piece = shape((size // 2 * cap, 2 * kv_width), BF16)
+    )(live, order, *qds, after(kvs[0], cols[1]), *kvs[1:])
+
+    piece = (size // 2 * cap, 2 * half)
     grads, keep, send = call(
         functools.partial(total_body, size, inner, cap),
-        [shape(terms, BF16), piece, piece],
-        [VMEM] * inner,
+        [shape(terms, BF16), shape(piece, F32), shape(piece, BF16)],
+        [VMEM] * (2 * inner),
         [VMEM] * 3,
         (),
-        cost(slots * inner * kv_width * 4, 16 * slots * inner * kv_width),
-        "grads_total",
-    )(kept, *[b_swap(sent, s) for s in range(1, inner)])
-    pair_grads = t_swap(send, 1)
-    w_pair = [t_swap(after(weights, first), 1)] + [
-        jnp.concatenate([k, t_swap(after(v, first), 1)], axis=1) for k, v in zip(k_pair, v_far)
-    ]
-
+        cost(4 * slots * half * 2 * kv_width, 8 * kv_width * half),
+        "row_terms",
+    )(kept, *[b_swap(sent, s) for s in range(1, inner)], *w_own)
     row_grads = call(
-        functools.partial(rows_body, size, inner, cap),
+        functools.partial(pair_body, cap),
         [shape((cap, 2 * half), BF16)] * (size // 2),
-        [VMEM] * (2 + 2 * inner),
+        [VMEM] * 2,
         [VMEM] * (size // 2),
-        [pltpu.VMEM((size // 2 * cap, 2 * half), BF16)],
-        cost(4 * cap * size * 2 * kv_width * half, 8 * size * kv_width * half),
+        (),
+        cost(2 * slots * half, 8 * slots * half),
         "row_grad",
-    )(keep, pair_grads, *w_own, *w_pair)
+    )(keep, t_swap(send, 1))
     swapped = [
         move(x, lambda a, b, t, m=m: (t % 2 * (size // 2) + (t // 2 ^ m), b, a))
         for m, x in enumerate(row_grads)
     ]
-    key_weight_grad, value_weight_grad = call(
+    key_weight_grad, value_weight_grad, attended, query_gradient = call(
         functools.partial(weight_body, inner),
-        [shape((depth, kv_width), BF16)] * 2,
-        [VMEM] * (inner + 1),
-        [VMEM] * 2,
+        [shape((depth, kv_width), BF16)] * 2 + [shape((cap, width), BF16)] * 2,
+        [VMEM] * (inner + 3),
+        [VMEM] * 4,
         (),
         cost(4 * slots * half * 2 * kv_width, 16 * half * kv_width),
         "weight_grads",
-    )(*cols, after(grads, row_grads[0]))
+    )(*cols, after(grads, row_grads[0]), attended, query_gradient)
 
     chunks = 4
     token_grad = call(

time: 59.4 us -> 57.3 us (0.965)
  the two profiles are of different devices: /device:TPU:4 before, /device:TPU:1 now
where the time goes in v3:
time: 57.3 us; the launch traced here: 57.1 us
  waiting for transfers between devices  26.2 us (46%)
  starting transfers between devices  22.4 us (39%)
  Pallas kernels  7.52 us (13%)
  between operations  0.75 us (1%)
    ppermute x7, waiting for transfers between devices, a_swap(): lax.ppermute(x, 'ctx', [(j, (j // inner ^ s) * inner + j % inner) for j i...  10.2 us
    ppermute x3, waiting for transfers between devices, move(): lax.ppermute(x, ('ctx', 'tp'), [(flat(*i), flat(*target(*i))) for i in in...  9.67 us
    ppermute x7, starting transfers between devices, a_swap(): lax.ppermute(x, 'ctx', [(j, (j // inner ^ s) * inner + j % inner) for j i...  7.16 us
    ppermute x5, starting transfers between devices, b_swap(): lax.ppermute(x, 'ctx', [(j, j // inner * inner + (j % inner ^ s)) for j i...  5.94 us
    ppermute x2, starting transfers between devices, t_swap(): return lax.ppermute(x, 'tp', [(j, j ^ s) for j in range(size)])  5.21 us
    ppermute x5, waiting for transfers between devices, b_swap(): lax.ppermute(x, 'ctx', [(j, j // inner * inner + (j % inner ^ s)) for j i...  4.74 us
    ppermute x3, starting transfers between devices, move(): lax.ppermute(x, ('ctx', 'tp'), [(flat(*i), flat(*target(*i))) for i in in...  4.14 us
    pallas_call x1, Pallas kernels, local(): call(functools.partial(pick_body, size, inner, half), [shape((cap, 2 * ha...  2.33 us
  transfers between devices with their start and end apart: 17, of which 10 were waited for; matrix products, arithmetic and copies ran while one was open for 0% of the time, Pallas kernels for 7%

profile of v3, /device:TPU:1, one launch (start us, length us, event | category | flops | bytes accessed | tf_op | source)
XLA Modules:
  0.0 57.1 jit_solution(2671092356265736657)
XLA Ops:
  0.6 2.1 %collective-permute-start.3 = (bf16[1024,128]{1,0:T(8,128)(2,1)}, bf16[1024,128]{1,0:T(8,128)(2,1)S(1)}, u32[]{:S(2)}, u32[]{:S(2)}) collective-permute-start(bf16[1024,128]{1,0:T(8,128)(2,1)} %k_ref.1), channel_id=1, source_target_pairs={{0,4},{4,0},{8,12},{12,8},{16,20},{20,16},{24,28},{28,24},{1,5},{5... | collective-permute-start | bytes 786440 | tf_op jit(solution)/shard_map/ppermute | solution.py:288
  2.8 2.3 %pick.1 = (bf16[32,2048]{1,0:T(8,128)(2,1)S(1)}, bf16[32,1024]{1,0:T(8,128)(2,1)S(1)}, bf16[32,2048]{1,0:T(8,128)(2,1)S(1)}, bf16[32,2048]{1,0:T(8,128)(2,1)S(1)...) custom-call(s32[32]{0:T(128)} %select_hbm.1, ...), custom_call_target="tpu_custom_call" | custom-call | flops 20000000000 | bytes 2097152 | tf_op jit(solution)/shard_map/pick/pallas_call | solution.py:299
  5.2 3.6 %collective-permute-start.1 = (bf16[32,1024]{1,0:T(8,128)(2,1)S(1)}, bf16[32,1024]{1,0:T(8,128)(2,1)S(1)}, u32[]{:S(2)}, u32[]{:S(2)}) collective-permute-start(bf16[32,1024]{1,0:T(8,128)(2,1)S(1)} %get-tuple-element.33), channel_id=1, source_target_pairs={{0,24},{4,28},{8,16},{12,20},{16,8},{20,12},{24,0},{28,4},{1,25},{... | collective-permute-start | bytes 196616 | tf_op jit(solution)/shard_map/ppermute | solution.py:285
  9.1 1.3 %collective-permute-done.1.refs_1_ = bf16[32,1024]{1,0:T(8,128)(2,1)S(1)} collective-permute-done((bf16[32,1024]{1,0:T(8,128)(2,1)S(1)}, bf16[32,1024]{1,0:T(8,128)(2,1)S(1)}, u32[]{:S(2)}, u32[]{:S(2)}) %collective-permute-start.1) | collective-permute-done | bytes 65568 | tf_op jit(solution)/shard_map/ppermute | solution.py:285
  10.4 4.5 %collective-permute-done.refs_0_ = bf16[32,2048]{1,0:T(8,128)(2,1)S(1)} collective-permute-done((bf16[32,2048]{1,0:T(8,128)(2,1)S(1)}, bf16[32,2048]{1,0:T(8,128)(2,1)S(1)}, u32[]{:S(2)}, u32[]{:S(2)}) %collective-permute-start) | collective-permute-done | bytes 131104 | tf_op jit(solution)/shard_map/ppermute | solution.py:296
  14.9 2.0 %collective-permute-start.2 = (bf16[32,3072]{1,0:T(8,128)(2,1)S(1)}, bf16[32,3072]{1,0:T(8,128)(2,1)S(1)}, u32[]{:S(2)}, u32[]{:S(2)}) collective-permute-start(bf16[32,3072]{1,0:T(8,128)(2,1)S(1)} %pad_maximum_fusion), channel_id=1, source_target_pairs={{0,1},{1,0},{2,3},{3,2},{4,5},{5,4},{6,7},{7,6},{8,9},{9,8},{10,11... | collective-permute-start | bytes 589832 | tf_op jit(solution)/shard_map/ppermute | solution.py:291
  18.2 1.2 %collective-permute-start.8 = (bf16[128,256]{1,0:T(8,128)(2,1)S(1)}, bf16[128,256]{1,0:T(8,128)(2,1)S(1)}, u32[]{:S(2)}, u32[]{:S(2)}) collective-permute-start(bf16[128,256]{1,0:T(8,128)(2,1)S(1)} %get-tuple-element.41), channel_id=1, source_target_pairs={{0,8},{4,12},{8,0},{12,4},{16,24},{20,28},{24,16},{28,20},{1,9},{5... | collective-permute-start | bytes 196616 | tf_op jit(solution)/shard_map/ppermute | solution.py:285
  19.4 1.6 %collective-permute-start.11 = (bf16[128,256]{1,0:T(8,128)(2,1)S(1)}, bf16[128,256]{1,0:T(8,128)(2,1)S(1)}, u32[]{:S(2)}, u32[]{:S(2)}) collective-permute-start(bf16[128,256]{1,0:T(8,128)(2,1)S(1)} %get-tuple-element.41), channel_id=1, source_target_pairs={{0,24},{4,28},{8,16},{12,20},{16,8},{20,12},{24,0},{28,4},{1,25},{... | collective-permute-start | bytes 196616 | tf_op jit(solution)/shard_map/ppermute | solution.py:285
  21.0 1.2 %collective-permute-start.5 = (bf16[128,1024]{1,0:T(8,128)(2,1)S(1)}, bf16[128,1024]{1,0:T(8,128)(2,1)S(1)}, u32[]{:S(2)}, u32[]{:S(2)}) collective-permute-start(bf16[128,1024]{1,0:T(8,128)(2,1)S(1)} %get-tuple-element.37), channel_id=1, source_target_pairs={{0,4},{4,0},{8,12},{12,8},{16,20},{20,16},{24,28},{28,24},{1,5},{5... | collective-permute-start | bytes 786440 | tf_op jit(solution)/shard_map/ppermute | solution.py:288
  22.2 6.1 %collective-permute-done.7.refs_2_ = bf16[64,1024]{1,0:T(8,128)(2,1)S(1)} collective-permute-done((bf16[64,1024]{1,0:T(8,128)(2,1)S(1)}, bf16[64,1024]{1,0:T(8,128)(2,1)S(1)}, u32[]{:S(2)}, u32[]{:S(2)}) %collective-permute-start.7) | collective-permute-done | bytes 131104 | tf_op jit(solution)/shard_map/ppermute | solution.py:285
  28.3 2.8 %collective-permute-done.10 = bf16[128,256]{1,0:T(8,128)(2,1)S(1)} collective-permute-done((bf16[128,256]{1,0:T(8,128)(2,1)S(1)}, bf16[128,256]{1,0:T(8,128)(2,1)S(1)}, u32[]{:S(2)}, u32[]{:S(2)}) %collective-permute-start.10) | collective-permute-done | bytes 65568 | tf_op jit(solution)/shard_map/ppermute | solution.py:285
  31.2 1.3 %collective-permute-start.12 = (bf16[128,256]{1,0:T(8,128)(2,1)S(1)}, bf16[128,256]{1,0:T(8,128)(2,1)S(1)}, u32[]{:S(2)}, u32[]{:S(2)}) collective-permute-start(bf16[128,256]{1,0:T(8,128)(2,1)S(1)} %add_convert_fusion.refs_4_), channel_id=1, source_target_pairs={{0,4},{4,0},{8,12},{12,8},{16,20},{20,16},{24,28},{28,24},{1,5},{5... | collective-permute-start | bytes 196616 | tf_op jit(solution)/shard_map/ppermute | solution.py:288
  32.5 2.1 %collective-permute-done.12.refs_5_ = bf16[128,256]{1,0:T(8,128)(2,1)S(1)} collective-permute-done((bf16[128,256]{1,0:T(8,128)(2,1)S(1)}, bf16[128,256]{1,0:T(8,128)(2,1)S(1)}, u32[]{:S(2)}, u32[]{:S(2)}) %collective-permute-start.12) | collective-permute-done | bytes 65568 | tf_op jit(solution)/shard_map/ppermute | solution.py:288
  34.6 1.3 %attend.1 = (bf16[32,1024]{1,0:T(8,128)(2,1)S(1)}, bf16[32,1024]{1,0:T(8,128)(2,1)S(1)}, f32[256,256]{1,0:T(8,128)S(1)}, bf16[256,256]{1,0:T(8,128)(2,1)S(1)}) custom-call(f32[32,128]{1,0:T(8,128)S(1)} %get-tuple-element.38.live_ref, s32[256,128]{1,0:T(8,128)S(1)} %get-tuple-element.39.order_ref, bf16[32,2048]{1,0:T(8,128)(2,1)S(1)} %get-tuple-element.40.refs_0_, ...), custom_call_target="tpu_custom_call" | custom-call | flops 402653184 | bytes 524288 | tf_op jit(solution)/shard_map/attend/pallas_call | solution.py:351
  35.9 1.3 %collective-permute-start.13 = (bf16[256,256]{1,0:T(8,128)(2,1)S(1)}, bf16[256,256]{1,0:T(8,128)(2,1)S(1)}, u32[]{:S(2)}, u32[]{:S(2)}) collective-permute-start(bf16[256,256]{1,0:T(8,128)(2,1)S(1)} %get-tuple-element.45), channel_id=1, source_target_pairs={{0,4},{4,0},{8,12},{12,8},{16,20},{20,16},{24,28},{28,24},{1,5},{5... | collective-permute-start | bytes 393224 | tf_op jit(solution)/shard_map/ppermute | solution.py:288
  37.2 2.6 %collective-permute-done.13.refs_1_ = bf16[256,256]{1,0:T(8,128)(2,1)S(1)} collective-permute-done((bf16[256,256]{1,0:T(8,128)(2,1)S(1)}, bf16[256,256]{1,0:T(8,128)(2,1)S(1)}, u32[]{:S(2)}, u32[]{:S(2)}) %collective-permute-start.13) | collective-permute-done | bytes 131104 | tf_op jit(solution)/shard_map/ppermute | solution.py:288
  40.6 3.2 %collective-permute-start.14 = (bf16[64,2048]{1,0:T(8,128)(2,1)S(1)}, bf16[64,2048]{1,0:T(8,128)(2,1)S(1)}, u32[]{:S(2)}, u32[]{:S(2)}) collective-permute-start(bf16[64,2048]{1,0:T(8,128)(2,1)S(1)} %get-tuple-element.48), channel_id=1, source_target_pairs={{0,1},{1,0},{2,3},{3,2},{4,5},{5,4},{6,7},{7,6},{8,9},{9,8},{10,11... | collective-permute-start | bytes 786440 | tf_op jit(solution)/shard_map/ppermute | solution.py:291
  43.8 1.2 %collective-permute-done.14.got_ref = bf16[64,2048]{1,0:T(8,128)(2,1)S(1)} collective-permute-done((bf16[64,2048]{1,0:T(8,128)(2,1)S(1)}, bf16[64,2048]{1,0:T(8,128)(2,1)S(1)}, u32[]{:S(2)}, u32[]{:S(2)}) %collective-permute-start.14) | collective-permute-done | bytes 262176 | tf_op jit(solution)/shard_map/ppermute | solution.py:291
  45.0 1.5 %collective-permute-start.16 = (bf16[32,2048]{1,0:T(8,128)(2,1)S(1)}, bf16[32,2048]{1,0:T(8,128)(2,1)S(1)}, u32[]{:S(2)}, u32[]{:S(2)}) collective-permute-start(bf16[32,2048]{1,0:T(8,128)(2,1)S(1)} %get-tuple-element.56), channel_id=1, source_target_pairs={{0,8},{1,24},{2,0},{3,16},{4,12},{5,28},{6,4},{7,20},{8,9},{9,25},... | collective-permute-start | bytes 393224 | tf_op jit(solution)/shard_map/ppermute | solution.py:296
  46.6 2.6 %collective-permute-start.15 = (bf16[32,2048]{1,0:T(8,128)(2,1)S(1)}, bf16[32,2048]{1,0:T(8,128)(2,1)S(1)}, u32[]{:S(2)}, u32[]{:S(2)}) collective-permute-start(bf16[32,2048]{1,0:T(8,128)(2,1)S(1)} %get-tuple-element.49), channel_id=1, source_target_pairs={{0,0},{1,16},{2,8},{3,24},{4,4},{5,20},{6,12},{7,28},{8,1},{9,17},... | collective-permute-start | bytes 393224 | tf_op jit(solution)/shard_map/ppermute | solution.py:296
  49.2 1.3 %weight_grads.1 = (bf16[1024,128]{1,0:T(8,128)(2,1)}, bf16[1024,128]{1,0:T(8,128)(2,1)}, bf16[32,1024]{1,0:T(8,128)(2,1)}, bf16[32,1024]{1,0:T(8,128)(2,1)}) custom-call(bf16[128,1024]{1,0:T(8,128)(2,1)S(1)} %get-tuple-element.36.refs_0_, bf16[128,1024]{1,0:T(8,128)(2,1)S(1)} %collective-permute-done.5.refs_1_, ...), custom_call_target="tpu_custom_call" | custom-call | flops 134217728 | bytes 2097152 | tf_op jit(solution)/shard_map/weight_grads/pallas_call | solution.py:384
  50.4 2.5 %collective-permute-done.16.refs_1_ = bf16[32,2048]{1,0:T(8,128)(2,1)S(1)} collective-permute-done((bf16[32,2048]{1,0:T(8,128)(2,1)S(1)}, bf16[32,2048]{1,0:T(8,128)(2,1)S(1)}, u32[]{:S(2)}, u32[]{:S(2)}) %collective-permute-start.16) | collective-permute-done | bytes 131104 | tf_op jit(solution)/shard_map/ppermute | solution.py:296
  52.9 2.7 %collective-permute-done.15.refs_0_ = bf16[32,2048]{1,0:T(8,128)(2,1)S(1)} collective-permute-done((bf16[32,2048]{1,0:T(8,128)(2,1)S(1)}, bf16[32,2048]{1,0:T(8,128)(2,1)S(1)}, u32[]{:S(2)}, u32[]{:S(2)}) %collective-permute-start.15) | collective-permute-done | bytes 131104 | tf_op jit(solution)/shard_map/ppermute | solution.py:296
  55.6 1.5 %scatter.1 = bf16[256,2048]{1,0:T(8,128)(2,1)} custom-call(bf16[32,256]{1,0:T(8,128)(2,1)S(1)} %get-tuple-element.55.hot_ref, bf16[32,2048]{1,0:T(8,128)(2,1)S(1)} %collective-permute-done.15.refs_0_, bf16[32,2048]{1,0:T(8,128)(2,1)S(1)} %collective-permute-done.16.refs_1_), custom_call_target="tpu_custom_call" | custom-call | flops 33554432 | bytes 1048576 | tf_op jit(solution)/shard_map/scatter/pallas_call | solution.py:395
  (24 shorter events, 2.7 us)
Async XLA Ops:
  0.6 16.7 %collective-permute-start.3 = (bf16[1024,128]{1,0:T(8,128)(2,1)}, bf16[1024,128]{1,0:T(8,128)(2,1)S(1)}, u32[]{:S(2)}, u32[]{:S(2)}) collective-permute-start(bf16[1024,128]{1,0:T(8,128)(2,1)} %k_ref.1), channel_id=1, source_target_pairs={{0,4},{4,0},{8,12},{12,8},{16,20},{20,16},{24,28},{28,24},{1,5},{5... | collective-permute-start | bytes 786440 | tf_op jit(solution)/shard_map/ppermute | solution.py:288
  2.7 14.6 %collective-permute-start.4 = (bf16[1024,128]{1,0:T(8,128)(2,1)}, bf16[1024,128]{1,0:T(8,128)(2,1)S(1)}, u32[]{:S(2)}, u32[]{:S(2)}) collective-permute-start(bf16[1024,128]{1,0:T(8,128)(2,1)} %v_ref.1), channel_id=1, source_target_pairs={{0,4},{4,0},{8,12},{12,8},{16,20},{20,16},{24,28},{28,24},{1,5},{5... | collective-permute-start | bytes 786440 | tf_op jit(solution)/shard_map/ppermute | solution.py:288
  5.2 5.2 %collective-permute-start.1 = (bf16[32,1024]{1,0:T(8,128)(2,1)S(1)}, bf16[32,1024]{1,0:T(8,128)(2,1)S(1)}, u32[]{:S(2)}, u32[]{:S(2)}) collective-permute-start(bf16[32,1024]{1,0:T(8,128)(2,1)S(1)} %get-tuple-element.33), channel_id=1, source_target_pairs={{0,24},{4,28},{8,16},{12,20},{16,8},{20,12},{24,0},{28,4},{1,25},{... | collective-permute-start | bytes 196616 | tf_op jit(solution)/shard_map/ppermute | solution.py:285
  8.7 6.1 %collective-permute-start = (bf16[32,2048]{1,0:T(8,128)(2,1)S(1)}, bf16[32,2048]{1,0:T(8,128)(2,1)S(1)}, u32[]{:S(2)}, u32[]{:S(2)}) collective-permute-start(bf16[32,2048]{1,0:T(8,128)(2,1)S(1)} %get-tuple-element.32), channel_id=1, source_target_pairs={{0,8},{1,17},{2,10},{3,19},{4,12},{5,21},{6,14},{7,23},{8,0},{9,25... | collective-permute-start | bytes 393224 | tf_op jit(solution)/shard_map/ppermute | solution.py:296
  8.7 8.1 %collective-permute-start.6 = (bf16[32,2048]{1,0:T(8,128)(2,1)S(1)}, bf16[32,2048]{1,0:T(8,128)(2,1)S(1)}, u32[]{:S(2)}, u32[]{:S(2)}) collective-permute-start(bf16[32,2048]{1,0:T(8,128)(2,1)S(1)} %get-tuple-element.40.refs_0_), channel_id=1, source_target_pairs={{0,8},{4,12},{8,0},{12,4},{16,24},{20,28},{24,16},{28,20},{1,9},{5... | collective-permute-start | bytes 393224 | tf_op jit(solution)/shard_map/ppermute | solution.py:285
  14.9 3.0 %collective-permute-start.2 = (bf16[32,3072]{1,0:T(8,128)(2,1)S(1)}, bf16[32,3072]{1,0:T(8,128)(2,1)S(1)}, u32[]{:S(2)}, u32[]{:S(2)}) collective-permute-start(bf16[32,3072]{1,0:T(8,128)(2,1)S(1)} %pad_maximum_fusion), channel_id=1, source_target_pairs={{0,1},{1,0},{2,3},{3,2},{4,5},{5,4},{6,7},{7,6},{8,9},{9,8},{10,11... | collective-permute-start | bytes 589832 | tf_op jit(solution)/shard_map/ppermute | solution.py:291
  16.9 11.5 %collective-permute-start.7 = (bf16[64,1024]{1,0:T(8,128)(2,1)S(1)}, bf16[64,1024]{1,0:T(8,128)(2,1)S(1)}, u32[]{:S(2)}, u32[]{:S(2)}) collective-permute-start(bf16[64,1024]{1,0:T(8,128)(2,1)S(1)} %slice_select_fusion), channel_id=1, source_target_pairs={{0,16},{4,20},{8,24},{12,28},{16,0},{20,4},{24,8},{28,12},{1,17},{... | collective-permute-start | bytes 393224 | tf_op jit(solution)/shard_map/ppermute | solution.py:285
  18.2 10.1 %collective-permute-start.8 = (bf16[128,256]{1,0:T(8,128)(2,1)S(1)}, bf16[128,256]{1,0:T(8,128)(2,1)S(1)}, u32[]{:S(2)}, u32[]{:S(2)}) collective-permute-start(bf16[128,256]{1,0:T(8,128)(2,1)S(1)} %get-tuple-element.41), channel_id=1, source_target_pairs={{0,8},{4,12},{8,0},{12,4},{16,24},{20,28},{24,16},{28,20},{1,9},{5... | collective-permute-start | bytes 196616 | tf_op jit(solution)/shard_map/ppermute | solution.py:285
  19.4 8.9 %collective-permute-start.11 = (bf16[128,256]{1,0:T(8,128)(2,1)S(1)}, bf16[128,256]{1,0:T(8,128)(2,1)S(1)}, u32[]{:S(2)}, u32[]{:S(2)}) collective-permute-start(bf16[128,256]{1,0:T(8,128)(2,1)S(1)} %get-tuple-element.41), channel_id=1, source_target_pairs={{0,24},{4,28},{8,16},{12,20},{16,8},{20,12},{24,0},{28,4},{1,25},{... | collective-permute-start | bytes 196616 | tf_op jit(solution)/shard_map/ppermute | solution.py:285
  21.0 10.1 %collective-permute-start.10 = (bf16[128,256]{1,0:T(8,128)(2,1)S(1)}, bf16[128,256]{1,0:T(8,128)(2,1)S(1)}, u32[]{:S(2)}, u32[]{:S(2)}) collective-permute-start(bf16[128,256]{1,0:T(8,128)(2,1)S(1)} %get-tuple-element.41), channel_id=1, source_target_pairs={{0,16},{4,20},{8,24},{12,28},{16,0},{20,4},{24,8},{28,12},{1,17},{... | collective-permute-start | bytes 196616 | tf_op jit(solution)/shard_map/ppermute | solution.py:285
  21.0 11.4 %collective-permute-start.5 = (bf16[128,1024]{1,0:T(8,128)(2,1)S(1)}, bf16[128,1024]{1,0:T(8,128)(2,1)S(1)}, u32[]{:S(2)}, u32[]{:S(2)}) collective-permute-start(bf16[128,1024]{1,0:T(8,128)(2,1)S(1)} %get-tuple-element.37), channel_id=1, source_target_pairs={{0,4},{4,0},{8,12},{12,8},{16,20},{20,16},{24,28},{28,24},{1,5},{5... | collective-permute-start | bytes 786440 | tf_op jit(solution)/shard_map/ppermute | solution.py:288
  28.3 6.2 %collective-permute-start.9 = (bf16[64,1024]{1,0:T(8,128)(2,1)S(1)}, bf16[64,1024]{1,0:T(8,128)(2,1)S(1)}, u32[]{:S(2)}, u32[]{:S(2)}) collective-permute-start(bf16[64,1024]{1,0:T(8,128)(2,1)S(1)} %collective-permute-done.7.refs_2_), channel_id=1, source_target_pairs={{0,8},{4,12},{8,0},{12,4},{16,24},{20,28},{24,16},{28,20},{1,9},{5... | collective-permute-start | bytes 393224 | tf_op jit(solution)/shard_map/ppermute | solution.py:285
  31.2 3.4 %collective-permute-start.12 = (bf16[128,256]{1,0:T(8,128)(2,1)S(1)}, bf16[128,256]{1,0:T(8,128)(2,1)S(1)}, u32[]{:S(2)}, u32[]{:S(2)}) collective-permute-start(bf16[128,256]{1,0:T(8,128)(2,1)S(1)} %add_convert_fusion.refs_4_), channel_id=1, source_target_pairs={{0,4},{4,0},{8,12},{12,8},{16,20},{20,16},{24,28},{28,24},{1,5},{5... | collective-permute-start | bytes 196616 | tf_op jit(solution)/shard_map/ppermute | solution.py:288
  35.9 3.9 %collective-permute-start.13 = (bf16[256,256]{1,0:T(8,128)(2,1)S(1)}, bf16[256,256]{1,0:T(8,128)(2,1)S(1)}, u32[]{:S(2)}, u32[]{:S(2)}) collective-permute-start(bf16[256,256]{1,0:T(8,128)(2,1)S(1)} %get-tuple-element.45), channel_id=1, source_target_pairs={{0,4},{4,0},{8,12},{12,8},{16,20},{20,16},{24,28},{28,24},{1,5},{5... | collective-permute-start | bytes 393224 | tf_op jit(solution)/shard_map/ppermute | solution.py:288
  40.6 4.4 %collective-permute-start.14 = (bf16[64,2048]{1,0:T(8,128)(2,1)S(1)}, bf16[64,2048]{1,0:T(8,128)(2,1)S(1)}, u32[]{:S(2)}, u32[]{:S(2)}) collective-permute-start(bf16[64,2048]{1,0:T(8,128)(2,1)S(1)} %get-tuple-element.48), channel_id=1, source_target_pairs={{0,1},{1,0},{2,3},{3,2},{4,5},{5,4},{6,7},{7,6},{8,9},{9,8},{10,11... | collective-permute-start | bytes 786440 | tf_op jit(solution)/shard_map/ppermute | solution.py:291
  45.0 7.9 %collective-permute-start.16 = (bf16[32,2048]{1,0:T(8,128)(2,1)S(1)}, bf16[32,2048]{1,0:T(8,128)(2,1)S(1)}, u32[]{:S(2)}, u32[]{:S(2)}) collective-permute-start(bf16[32,2048]{1,0:T(8,128)(2,1)S(1)} %get-tuple-element.56), channel_id=1, source_target_pairs={{0,8},{1,24},{2,0},{3,16},{4,12},{5,28},{6,4},{7,20},{8,9},{9,25},... | collective-permute-start | bytes 393224 | tf_op jit(solution)/shard_map/ppermute | solution.py:296
  46.6 9.1 %collective-permute-start.15 = (bf16[32,2048]{1,0:T(8,128)(2,1)S(1)}, bf16[32,2048]{1,0:T(8,128)(2,1)S(1)}, u32[]{:S(2)}, u32[]{:S(2)}) collective-permute-start(bf16[32,2048]{1,0:T(8,128)(2,1)S(1)} %get-tuple-element.49), channel_id=1, source_target_pairs={{0,0},{1,16},{2,8},{3,24},{4,4},{5,20},{6,12},{7,28},{8,1},{9,17},... | collective-permute-start | bytes 393224 | tf_op jit(solution)/shard_map/ppermute | solution.py:296

commit v4 on v3

--- a/solution.py
+++ b/solution.py
@@ -57,14 +57,13 @@
 
 
 def pick_body(
-    size, inner, half, select_hbm, count_hbm, tokens_ref, q_ref, og_ref, k_ref, v_ref, *rest
+    size, inner, half, select_hbm, count_hbm, tokens_ref, k_ref, v_ref, *rest
 ):
     pairs = size // 2 - 1
-    outs, (qd_ref, w_ref, hot_ref, live_ref, order_ref) = rest[: pairs + 2], rest[pairs + 2 : pairs + 7]
-    select_ref, count_ref, buf, og_buf, sems, side = rest[pairs + 7 :]
+    outs, (w_ref, hot_ref, live_ref, order_ref) = rest[: pairs + 2], rest[pairs + 2 : pairs + 6]
+    select_ref, count_ref, buf, sems, side = rest[pairs + 6 :]
     a, b, t = place(inner)
     cap, rows = outs[0].shape[0], tokens_ref.shape[0]
-    width = q_ref.shape[1]
     core = lax.rem(t, 2)
     first = [
         pltpu.make_async_copy(select_hbm, select_ref, side.at[0]),
@@ -86,10 +85,8 @@
         )
         copies[i].start()
     others = [
-        pltpu.make_async_copy(q_ref, qd_ref.at[:, :width], side.at[2]),
-        pltpu.make_async_copy(og_ref, og_buf, side.at[3]),
-        pltpu.make_async_copy(k_ref, w_ref.at[:, : k_ref.shape[1]], side.at[4]),
-        pltpu.make_async_copy(v_ref, w_ref.at[:, k_ref.shape[1] :], side.at[5]),
+        pltpu.make_async_copy(k_ref, w_ref.at[:, : k_ref.shape[1]], side.at[2]),
+        pltpu.make_async_copy(v_ref, w_ref.at[:, k_ref.shape[1] :], side.at[3]),
     ]
     for c in others:
         c.start()
@@ -104,7 +101,9 @@
         wide = outs[i].shape[1]
         outs[i][...] = dot(hot, buf[:, 2 * half * i : 2 * half * i + wide], 1, 0).astype(BF16)
     row = lax.broadcasted_iota(jnp.int32, (cap, HEAD), 0)
-    live_ref[...] = jnp.where(row < count_ref[a * inner + b], 1.0, 0.0)
+    for s in range(size):
+        count = count_ref[(a ^ s) * inner + b]
+        live_ref[s * cap : (s + 1) * cap, :] = jnp.where(row < count, 1.0, 0.0).astype(BF16)
     for s in range(inner):
         for z in range(size):
             shard = z * inner + (b ^ s)
@@ -112,7 +111,6 @@
             order_ref[(s * size + z) * cap : (s * size + z + 1) * cap, :] = at
     for c in others:
         c.wait()
-    qd_ref[:, width:] = og_buf[...] * live_ref[:, :1].astype(BF16)
 
 
 def project_body(size, inner, half, *refs):
@@ -147,22 +145,23 @@
 
 
 def attend_body(size, inner, cap, group, live_ref, order_ref, *refs):
-    qds, kvs = refs[:size], refs[size : size + inner]
-    att_ref, dq_ref, kept_ref, sent_ref, q_all, do_all = refs[size + inner :]
+    qds, kvs = refs[:6], refs[6 : 6 + inner]
+    att_ref, dq_ref, kept_ref, *sent, q_all, do_all = refs[6 + inner :]
     a, b, t = place(inner)
     width = group * HEAD
     block = group * cap
     scale = 1.0 / math.sqrt(HEAD)
-    far, far_other = qds[2][...], qds[3][...]
+    far, far_other = qds[4][...], qds[5][...]
     swapped = jnp.concatenate([far_other[cap:], far_other[:cap]], axis=0)
     odd = lax.rem(a, 2) == 1
     far_q, far_do = jnp.where(odd, swapped, far), jnp.where(odd, far, swapped)
     for s in range(size):
         if s < 2:
-            q_rows, do_rows = qds[s][:, :width], qds[s][:, width:]
+            q_rows, do_rows = qds[2 * s][...], qds[2 * s + 1][...]
         else:
             far_rows = slice((s - 2) * cap, (s - 1) * cap)
             q_rows, do_rows = far_q[far_rows], far_do[far_rows]
+        do_rows = do_rows * live_ref[s * cap : (s + 1) * cap, :1]
         for g in range(group):
             to = slice(s * block + g * cap, s * block + (g + 1) * cap)
             q_all[to, :] = q_rows[:, g * HEAD : (g + 1) * HEAD]
@@ -197,22 +196,21 @@
             dq_rows = dot(keys_t, grad_scores[:, :block], 1, 0).T.astype(BF16)
             for g in range(group):
                 rows, to = slice(g * cap, (g + 1) * cap), slice(g * HEAD, (g + 1) * HEAD)
-                att_ref[:, to] = (att_rows[rows, :] * live_ref[...]).astype(BF16)
+                att_ref[:, to] = (att_rows[rows, :] * live_ref[:cap, :].astype(F32)).astype(BF16)
                 dq_ref[:, to] = dq_rows[rows, :]
-    for ref in (kept_ref, sent_ref):
-        ref[:, :HEAD] = dk.astype(ref.dtype)
-        ref[:, HEAD:] = dv.astype(ref.dtype)
+    rows = size * cap
+    for s, ref in enumerate([kept_ref, *sent]):
+        ref[:, :HEAD] = dk[s * rows : (s + 1) * rows, :].astype(ref.dtype)
+        ref[:, HEAD:] = dv[s * rows : (s + 1) * rows, :].astype(ref.dtype)
 
 
 def total_body(size, inner, cap, *refs):
     terms, weights, (grads_ref, keep_ref, send_ref) = refs[:inner], refs[inner : 2 * inner], refs[2 * inner :]
     slots = size * cap
-    for s in range(inner):
-        total = None
-        for j in range(inner):
-            term = terms[j][(s ^ j) * slots : ((s ^ j) + 1) * slots, :].astype(F32)
-            total = term if total is None else total + term
-        grads_ref[s * slots : (s + 1) * slots, :] = total.astype(BF16)
+    total = terms[0][...]
+    for r in terms[1:]:
+        total = total + r[...].astype(F32)
+    grads_ref[...] = total.astype(BF16)
     a, b, t = place(inner)
     rows = slots // 2
     core = lax.rem(t, 2)
@@ -225,13 +223,13 @@
 
 
 def weight_body(inner, *refs):
-    cols, (grads_ref, att_ref, dq_ref, k_ref, v_ref, att_out, dq_out) = refs[:inner], refs[inner:]
+    cols, grads = refs[:inner], refs[inner : 2 * inner]
+    att_ref, dq_ref, k_ref, v_ref, att_out, dq_out = refs[2 * inner :]
     att_out[...] = att_ref[...]
     dq_out[...] = dq_ref[...]
-    slots = cols[0].shape[0]
     total = None
-    for s in range(inner):
-        term = dot(cols[s][...], grads_ref[s * slots : (s + 1) * slots, :], 0, 0)
+    for c, g in zip(cols, grads):
+        term = dot(c[...], g[...], 0, 0)
         total = term if total is None else total + term
     width = k_ref.shape[1]
     k_ref[...] = total[:, :width].astype(BF16)
@@ -295,23 +293,22 @@
         flat = lambda a, b, t: (a * inner + b) * size + t
         return lax.ppermute(x, ("ctx", "tp"), [(flat(*i), flat(*target(*i))) for i in index])
 
-    inputs = (select_index, valid_count, tokens, queries, out_grad, key_matrix, value_matrix)
-    *picked, own, qd, weights, hot, live, order = call(
+    inputs = (select_index, valid_count, tokens, key_matrix, value_matrix)
+    *picked, own, weights, hot, live, order = call(
         functools.partial(pick_body, size, inner, half),
         [shape((cap, 2 * half), BF16)] * pairs
         + [shape((cap, half), BF16), shape((cap, 2 * half), BF16)]
-        + [shape((cap, 2 * width), BF16), shape((depth, 2 * kv_width), BF16)]
-        + [shape((cap, rows), BF16), shape((cap, HEAD), F32)]
+        + [shape((depth, 2 * kv_width), BF16), shape((cap, rows), BF16)]
+        + [shape((slots, HEAD), BF16)]
         + [shape((slots * inner, HEAD), jnp.int32)],
-        [HBM] * 7,
-        [VMEM] * (pairs + 7),
+        [HBM] * 5,
+        [VMEM] * (pairs + 6),
         [
             pltpu.SMEM((cap,), jnp.int32),
             pltpu.SMEM((ctx,), jnp.int32),
             pltpu.VMEM((rows, 2 * half * (pairs + 2)), BF16),
-            pltpu.VMEM((cap, width), BF16),
             pltpu.SemaphoreType.DMA((pairs + 2,)),
-            pltpu.SemaphoreType.DMA((6,)),
+            pltpu.SemaphoreType.DMA((4,)),
         ],
         cost(HINT, rows * model),
         "pick",
@@ -322,10 +319,10 @@
     w_far = [[b_swap(x, s) for x in (key_matrix, value_matrix)] for s in range(1, inner)]
     w_own = [weights] + [jnp.concatenate(x, axis=1) for x in w_far]
     other = t_swap(jnp.concatenate(got, axis=1), 1)
-    near = a_swap(qd, 1)
-    both = jnp.concatenate([qd, near], axis=0)
+    near_q, near_g = a_swap(queries, 1), a_swap(out_grad, 1)
     odd = lax.rem(lax.axis_index("ctx") // inner, 2) == 1
-    far = a_swap(jnp.where(odd, both[:, width:], both[:, :width]), 2)
+    pair_q, pair_g = [jnp.concatenate(x, axis=0) for x in ((queries, near_q), (out_grad, near_g))]
+    far = a_swap(jnp.where(odd, pair_g, pair_q), 2)
 
     part, *cols = call(
         functools.partial(project_body, size, inner, half),
@@ -345,14 +342,14 @@
     kv = parts[0].astype(BF16)
     kvs = [kv] + [b_swap(kv, s) for s in range(1, inner)]
     far_other = a_swap(after(far, first), 1)
-    qds = [qd, near, far, far_other]
-
-    terms = (slots * inner, 2 * kv_width)
-    attended, query_gradient, kept, sent = call(
+    qds = [queries, out_grad, near_q, near_g, far, far_other]
+
+    terms = (slots, 2 * kv_width)
+    attended, query_gradient, kept, *sent = call(
         functools.partial(attend_body, size, inner, cap, group),
-        [shape((cap, width), BF16)] * 2 + [shape(terms, F32), shape(terms, BF16)],
-        [VMEM] * (2 + size + inner),
-        [VMEM] * 4,
+        [shape((cap, width), BF16)] * 2 + [shape(terms, F32)] + [shape(terms, BF16)] * (inner - 1),
+        [VMEM] * (8 + inner),
+        [VMEM] * (2 + inner),
         [pltpu.VMEM((slots * group, HEAD), BF16)] * 2,
         cost(12 * slots * group * slots * inner * HEAD, 4 * slots * width),
         "attend",
@@ -367,7 +364,7 @@
         (),
         cost(4 * slots * half * 2 * kv_width, 8 * kv_width * half),
         "row_terms",
-    )(kept, *[b_swap(sent, s) for s in range(1, inner)], *w_own)
+    )(kept, *[b_swap(x, s + 1) for s, x in enumerate(sent)], *w_own)
     row_grads = call(
         functools.partial(pair_body, cap),
         [shape((cap, 2 * half), BF16)] * (size // 2),
@@ -381,15 +378,16 @@
         move(x, lambda a, b, t, m=m: (t % 2 * (size // 2) + (t // 2 ^ m), b, a))
         for m, x in enumerate(row_grads)
     ]
+    far_grads = [b_swap(grads, s) for s in range(1, inner)]
     key_weight_grad, value_weight_grad, attended, query_gradient = call(
         functools.partial(weight_body, inner),
         [shape((depth, kv_width), BF16)] * 2 + [shape((cap, width), BF16)] * 2,
-        [VMEM] * (inner + 3),
+        [VMEM] * (2 * inner + 2),
         [VMEM] * 4,
         (),
         cost(4 * slots * half * 2 * kv_width, 16 * half * kv_width),
         "weight_grads",
-    )(*cols, after(grads, row_grads[0]), attended, query_gradient)
+    )(*cols, grads, *far_grads, after(attended, row_grads[0]), query_gradient)
 
     chunks = 4
     token_grad = call(

time: 57.3 us -> 56.6 us (0.988)
  the two profiles are of different devices: /device:TPU:1 before, /device:TPU:4 now
where the time goes in v4:
time: 56.6 us; the launch traced here: 55.5 us
  waiting for transfers between devices  24.3 us (43%)
  starting transfers between devices  22.9 us (40%)
  Pallas kernels  7.38 us (13%)
  between operations  0.77 us (1%)
    ppermute x6, waiting for transfers between devices, b_swap(): lax.ppermute(x, 'ctx', [(j, j // inner * inner + (j % inner ^ s)) for j i...  13.3 us
    ppermute x8, starting transfers between devices, a_swap(): lax.ppermute(x, 'ctx', [(j, (j // inner ^ s) * inner + j % inner) for j i...  10.5 us
    ppermute x6, starting transfers between devices, b_swap(): lax.ppermute(x, 'ctx', [(j, j // inner * inner + (j % inner ^ s)) for j i...  8.15 us
    ppermute x8, waiting for transfers between devices, a_swap(): lax.ppermute(x, 'ctx', [(j, (j // inner ^ s) * inner + j % inner) for j i...  6.9 us
    ppermute x3, starting transfers between devices, move(): lax.ppermute(x, ('ctx', 'tp'), [(flat(*i), flat(*target(*i))) for i in in...  4.11 us
    ppermute x3, waiting for transfers between devices, move(): lax.ppermute(x, ('ctx', 'tp'), [(flat(*i), flat(*target(*i))) for i in in...  2.64 us
    pallas_call x1, Pallas kernels, local(): call(functools.partial(pick_body, size, inner, half), [shape((cap, 2 * ha...  2.19 us
    ppermute x2, waiting for transfers between devices, t_swap(): return lax.ppermute(x, 'tp', [(j, j ^ s) for j in range(size)])  1.52 us
  transfers between devices with their start and end apart: 19, of which 11 were waited for; matrix products, arithmetic and copies ran while one was open for 0% of the time, Pallas kernels for 7%

profile of v4, /device:TPU:4, one launch (start us, length us, event | category | flops | bytes accessed | tf_op | source)
XLA Modules:
  0.0 55.5 jit_solution(12584816175647948967)
XLA Ops:
  0.7 1.6 %collective-permute-start.6 = (bf16[32,1024]{1,0:T(8,128)(2,1)}, bf16[32,1024]{1,0:T(8,128)(2,1)S(1)}, u32[]{:S(2)}, u32[]{:S(2)}) collective-permute-start(bf16[32,1024]{1,0:T(8,128)(2,1)} %refs_0_.1), channel_id=1, source_target_pairs={{0,8},{4,12},{8,0},{12,4},{16,24},{20,28},{24,16},{28,20},{1,9},{5... | collective-permute-start | bytes 196616 | tf_op jit(solution)/shard_map/ppermute | solution.py:283
  2.8 2.2 %pick.1 = (bf16[32,2048]{1,0:T(8,128)(2,1)S(1)}, bf16[32,1024]{1,0:T(8,128)(2,1)S(1)}, bf16[32,2048]{1,0:T(8,128)(2,1)S(1)}, bf16[1024,256]{1,0:T(8,128)(2,1)S(1...) custom-call(s32[32]{0:T(128)} %select_hbm.1, s32[8]{0:T(128)} %count_hbm.1, ...), custom_call_target="tpu_custom_call" | custom-call | flops 20000000000 | bytes 2097152 | tf_op jit(solution)/shard_map/pick/pallas_call | solution.py:297
  5.0 1.6 %collective-permute-start = (bf16[32,2048]{1,0:T(8,128)(2,1)S(1)}, bf16[32,2048]{1,0:T(8,128)(2,1)S(1)}, u32[]{:S(2)}, u32[]{:S(2)}) collective-permute-start(bf16[32,2048]{1,0:T(8,128)(2,1)S(1)} %get-tuple-element.31), channel_id=1, source_target_pairs={{0,8},{1,17},{2,10},{3,19},{4,12},{5,21},{6,14},{7,23},{8,0},{9,25... | collective-permute-start | bytes 393224 | tf_op jit(solution)/shard_map/ppermute | solution.py:294
  6.6 1.5 %collective-permute-start.3 = (bf16[1024,128]{1,0:T(8,128)(2,1)S(1)}, bf16[1024,128]{1,0:T(8,128)(2,1)S(1)}, u32[]{:S(2)}, u32[]{:S(2)}) collective-permute-start(bf16[1024,128]{1,0:T(8,128)(2,1)S(1)} %copy-done.2), channel_id=1, source_target_pairs={{0,4},{4,0},{8,12},{12,8},{16,20},{20,16},{24,28},{28,24},{1,5},{5... | collective-permute-start | bytes 786440 | tf_op jit(solution)/shard_map/ppermute | solution.py:286
  8.6 2.5 %collective-permute-start.1 = (bf16[32,1024]{1,0:T(8,128)(2,1)S(1)}, bf16[32,1024]{1,0:T(8,128)(2,1)S(1)}, u32[]{:S(2)}, u32[]{:S(2)}) collective-permute-start(bf16[32,1024]{1,0:T(8,128)(2,1)S(1)} %get-tuple-element.32), channel_id=1, source_target_pairs={{0,24},{4,28},{8,16},{12,20},{16,8},{20,12},{24,0},{28,4},{1,25},{... | collective-permute-start | bytes 196616 | tf_op jit(solution)/shard_map/ppermute | solution.py:283
  11.4 4.0 %collective-permute-done.1.refs_1_ = bf16[32,1024]{1,0:T(8,128)(2,1)S(1)} collective-permute-done((bf16[32,1024]{1,0:T(8,128)(2,1)S(1)}, bf16[32,1024]{1,0:T(8,128)(2,1)S(1)}, u32[]{:S(2)}, u32[]{:S(2)}) %collective-permute-start.1) | collective-permute-done | bytes 65568 | tf_op jit(solution)/shard_map/ppermute | solution.py:283
  15.8 4.6 %collective-permute-done.4 = bf16[1024,128]{1,0:T(8,128)(2,1)S(1)} collective-permute-done((bf16[1024,128]{1,0:T(8,128)(2,1)S(1)}, bf16[1024,128]{1,0:T(8,128)(2,1)S(1)}, u32[]{:S(2)}, u32[]{:S(2)}) %collective-permute-start.4) | collective-permute-done | bytes 262176 | tf_op jit(solution)/shard_map/ppermute | solution.py:286
  20.9 1.3 %collective-permute-start.9 = (bf16[128,256]{1,0:T(8,128)(2,1)S(1)}, bf16[128,256]{1,0:T(8,128)(2,1)S(1)}, u32[]{:S(2)}, u32[]{:S(2)}) collective-permute-start(bf16[128,256]{1,0:T(8,128)(2,1)S(1)} %get-tuple-element.39), channel_id=1, source_target_pairs={{0,8},{4,12},{8,0},{12,4},{16,24},{20,28},{24,16},{28,20},{1,9},{5... | collective-permute-start | bytes 196616 | tf_op jit(solution)/shard_map/ppermute | solution.py:283
  22.9 1.5 %collective-permute-start.11 = (bf16[128,256]{1,0:T(8,128)(2,1)S(1)}, bf16[128,256]{1,0:T(8,128)(2,1)S(1)}, u32[]{:S(2)}, u32[]{:S(2)}) collective-permute-start(bf16[128,256]{1,0:T(8,128)(2,1)S(1)} %get-tuple-element.39), channel_id=1, source_target_pairs={{0,16},{4,20},{8,24},{12,28},{16,0},{20,4},{24,8},{28,12},{1,17},{... | collective-permute-start | bytes 196616 | tf_op jit(solution)/shard_map/ppermute | solution.py:283
  24.4 1.5 %collective-permute-start.5 = (bf16[128,1024]{1,0:T(8,128)(2,1)S(1)}, bf16[128,1024]{1,0:T(8,128)(2,1)S(1)}, u32[]{:S(2)}, u32[]{:S(2)}) collective-permute-start(bf16[128,1024]{1,0:T(8,128)(2,1)S(1)} %get-tuple-element.36), channel_id=1, source_target_pairs={{0,4},{4,0},{8,12},{12,8},{16,20},{20,16},{24,28},{28,24},{1,5},{5... | collective-permute-start | bytes 786440 | tf_op jit(solution)/shard_map/ppermute | solution.py:286
  25.9 2.1 %collective-permute-start.10 = (bf16[64,1024]{1,0:T(8,128)(2,1)S(1)}, bf16[64,1024]{1,0:T(8,128)(2,1)S(1)}, u32[]{:S(2)}, u32[]{:S(2)}) collective-permute-start(bf16[64,1024]{1,0:T(8,128)(2,1)S(1)} %collective-permute-done.8.refs_4_), channel_id=1, source_target_pairs={{0,8},{4,12},{8,0},{12,4},{16,24},{20,28},{24,16},{28,20},{1,9},{5... | collective-permute-start | bytes 393224 | tf_op jit(solution)/shard_map/ppermute | solution.py:283
  28.8 2.2 %collective-permute-done.11 = bf16[128,256]{1,0:T(8,128)(2,1)S(1)} collective-permute-done((bf16[128,256]{1,0:T(8,128)(2,1)S(1)}, bf16[128,256]{1,0:T(8,128)(2,1)S(1)}, u32[]{:S(2)}, u32[]{:S(2)}) %collective-permute-start.11) | collective-permute-done | bytes 65568 | tf_op jit(solution)/shard_map/ppermute | solution.py:283
  31.0 1.5 %collective-permute-start.13 = (bf16[128,256]{1,0:T(8,128)(2,1)S(1)}, bf16[128,256]{1,0:T(8,128)(2,1)S(1)}, u32[]{:S(2)}, u32[]{:S(2)}) collective-permute-start(bf16[128,256]{1,0:T(8,128)(2,1)S(1)} %add_convert_fusion.refs_6_), channel_id=1, source_target_pairs={{0,4},{4,0},{8,12},{12,8},{16,20},{20,16},{24,28},{28,24},{1,5},{5... | collective-permute-start | bytes 196616 | tf_op jit(solution)/shard_map/ppermute | solution.py:286
  32.5 2.8 %collective-permute-done.13.refs_7_ = bf16[128,256]{1,0:T(8,128)(2,1)S(1)} collective-permute-done((bf16[128,256]{1,0:T(8,128)(2,1)S(1)}, bf16[128,256]{1,0:T(8,128)(2,1)S(1)}, u32[]{:S(2)}, u32[]{:S(2)}) %collective-permute-start.13) | collective-permute-done | bytes 65568 | tf_op jit(solution)/shard_map/ppermute | solution.py:286
  35.3 1.3 %attend.1 = (bf16[32,1024]{1,0:T(8,128)(2,1)S(1)}, bf16[32,1024]{1,0:T(8,128)(2,1)S(1)}, f32[128,256]{1,0:T(8,128)S(1)}, bf16[128,256]{1,0:T(8,128)(2,1)S(1)}) custom-call(bf16[128,128]{1,0:T(8,128)(2,1)S(1)} %get-tuple-element.37.live_ref, s32[256,128]{1,0:T(8,128)S(1)} %get-tuple-element.38.order_ref, bf16[32,1024]{1,0:T(8,128)(2,1)S(1)} %copy-done, ...), custom_call_target="tpu_custom_call" | custom-call | flops 402653184 | bytes 524288 | tf_op jit(solution)/shard_map/attend/pallas_call | solution.py:348
  36.6 1.5 %collective-permute-start.14 = (bf16[128,256]{1,0:T(8,128)(2,1)S(1)}, bf16[128,256]{1,0:T(8,128)(2,1)S(1)}, u32[]{:S(2)}, u32[]{:S(2)}) collective-permute-start(bf16[128,256]{1,0:T(8,128)(2,1)S(1)} %get-tuple-element.43), channel_id=1, source_target_pairs={{0,4},{4,0},{8,12},{12,8},{16,20},{20,16},{24,28},{28,24},{1,5},{5... | collective-permute-start | bytes 196616 | tf_op jit(solution)/shard_map/ppermute | solution.py:286
  38.2 2.8 %collective-permute-done.14.refs_1_ = bf16[128,256]{1,0:T(8,128)(2,1)S(1)} collective-permute-done((bf16[128,256]{1,0:T(8,128)(2,1)S(1)}, bf16[128,256]{1,0:T(8,128)(2,1)S(1)}, u32[]{:S(2)}, u32[]{:S(2)}) %collective-permute-start.14) | collective-permute-done | bytes 65568 | tf_op jit(solution)/shard_map/ppermute | solution.py:286
  41.8 1.5 %collective-permute-done.16.got_ref = bf16[64,2048]{1,0:T(8,128)(2,1)S(1)} collective-permute-done((bf16[64,2048]{1,0:T(8,128)(2,1)S(1)}, bf16[64,2048]{1,0:T(8,128)(2,1)S(1)}, u32[]{:S(2)}, u32[]{:S(2)}) %collective-permute-start.16) | collective-permute-done | bytes 262176 | tf_op jit(solution)/shard_map/ppermute | solution.py:289
  43.9 1.9 %collective-permute-start.17 = (bf16[32,2048]{1,0:T(8,128)(2,1)S(1)}, bf16[32,2048]{1,0:T(8,128)(2,1)S(1)}, u32[]{:S(2)}, u32[]{:S(2)}) collective-permute-start(bf16[32,2048]{1,0:T(8,128)(2,1)S(1)} %get-tuple-element.48), channel_id=1, source_target_pairs={{0,0},{1,16},{2,8},{3,24},{4,4},{5,20},{6,12},{7,28},{8,1},{9,17},... | collective-permute-start | bytes 393224 | tf_op jit(solution)/shard_map/ppermute | solution.py:294
  45.8 1.5 %collective-permute-start.15 = (bf16[128,256]{1,0:T(8,128)(2,1)S(1)}, bf16[128,256]{1,0:T(8,128)(2,1)S(1)}, u32[]{:S(2)}, u32[]{:S(2)}) collective-permute-start(bf16[128,256]{1,0:T(8,128)(2,1)S(1)} %get-tuple-element.44.refs_2_), channel_id=1, source_target_pairs={{0,4},{4,0},{8,12},{12,8},{16,20},{20,16},{24,28},{28,24},{1,5},{5... | collective-permute-start | bytes 196616 | tf_op jit(solution)/shard_map/ppermute | solution.py:286
  47.4 2.8 %collective-permute-done.15.refs_3_ = bf16[128,256]{1,0:T(8,128)(2,1)S(1)} collective-permute-done((bf16[128,256]{1,0:T(8,128)(2,1)S(1)}, bf16[128,256]{1,0:T(8,128)(2,1)S(1)}, u32[]{:S(2)}, u32[]{:S(2)}) %collective-permute-start.15) | collective-permute-done | bytes 65568 | tf_op jit(solution)/shard_map/ppermute | solution.py:286
  50.2 1.3 %weight_grads.1 = (bf16[1024,128]{1,0:T(8,128)(2,1)}, bf16[1024,128]{1,0:T(8,128)(2,1)}, bf16[32,1024]{1,0:T(8,128)(2,1)}, bf16[32,1024]{1,0:T(8,128)(2,1)}) custom-call(bf16[128,1024]{1,0:T(8,128)(2,1)S(1)} %get-tuple-element.35.refs_0_, bf16[128,1024]{1,0:T(8,128)(2,1)S(1)} %collective-permute-done.5.refs_1_, ...), custom_call_target="tpu_custom_call" | custom-call | flops 134217728 | bytes 2097152 | tf_op jit(solution)/shard_map/weight_grads/pallas_call | solution.py:382
  52.1 1.9 %collective-permute-done.17.refs_0_ = bf16[32,2048]{1,0:T(8,128)(2,1)S(1)} collective-permute-done((bf16[32,2048]{1,0:T(8,128)(2,1)S(1)}, bf16[32,2048]{1,0:T(8,128)(2,1)S(1)}, u32[]{:S(2)}, u32[]{:S(2)}) %collective-permute-start.17) | collective-permute-done | bytes 131104 | tf_op jit(solution)/shard_map/ppermute | solution.py:294
  54.1 1.5 %scatter.1 = bf16[256,2048]{1,0:T(8,128)(2,1)} custom-call(bf16[32,256]{1,0:T(8,128)(2,1)S(1)} %get-tuple-element.53.hot_ref, bf16[32,2048]{1,0:T(8,128)(2,1)S(1)} %collective-permute-done.17.refs_0_, bf16[32,2048]{1,0:T(8,128)(2,1)S(1)} %collective-permute-done.18.refs_1_), custom_call_target="tpu_custom_call" | custom-call | flops 33554432 | bytes 1048576 | tf_op jit(solution)/shard_map/scatter/pallas_call | solution.py:393
  (34 shorter events, 5.7 us)
Async XLA Ops:
  0.6 10.5 %copy-start = (bf16[32,1024]{1,0:T(8,128)(2,1)S(1)}, bf16[32,1024]{1,0:T(8,128)(2,1)}, u32[]{:S(2)}) copy-start(bf16[32,1024]{1,0:T(8,128)(2,1)} %refs_0_.1) | copy-start | bytes 196612
  0.6 10.5 %copy-start.1 = (bf16[32,1024]{1,0:T(8,128)(2,1)S(1)}, bf16[32,1024]{1,0:T(8,128)(2,1)}, u32[]{:S(2)}) copy-start(bf16[32,1024]{1,0:T(8,128)(2,1)} %refs_1_.1) | copy-start | bytes 196612
  0.7 7.4 %copy-start.3 = (bf16[1024,128]{1,0:T(8,128)(2,1)S(1)}, bf16[1024,128]{1,0:T(8,128)(2,1)}, u32[]{:S(2)}) copy-start(bf16[1024,128]{1,0:T(8,128)(2,1)} %v_ref.1) | copy-start | bytes 786436
  0.7 5.9 %copy-start.2 = (bf16[1024,128]{1,0:T(8,128)(2,1)S(1)}, bf16[1024,128]{1,0:T(8,128)(2,1)}, u32[]{:S(2)}) copy-start(bf16[1024,128]{1,0:T(8,128)(2,1)} %k_ref.1) | copy-start | bytes 786436
  0.7 8.0 %collective-permute-start.6 = (bf16[32,1024]{1,0:T(8,128)(2,1)}, bf16[32,1024]{1,0:T(8,128)(2,1)S(1)}, u32[]{:S(2)}, u32[]{:S(2)}) collective-permute-start(bf16[32,1024]{1,0:T(8,128)(2,1)} %refs_0_.1), channel_id=1, source_target_pairs={{0,8},{4,12},{8,0},{12,4},{16,24},{20,28},{24,16},{28,20},{1,9},{5... | collective-permute-start | bytes 196616 | tf_op jit(solution)/shard_map/ppermute | solution.py:283
  2.3 8.8 %collective-permute-start.7 = (bf16[32,1024]{1,0:T(8,128)(2,1)}, bf16[32,1024]{1,0:T(8,128)(2,1)S(1)}, u32[]{:S(2)}, u32[]{:S(2)}) collective-permute-start(bf16[32,1024]{1,0:T(8,128)(2,1)} %refs_1_.1), channel_id=1, source_target_pairs={{0,8},{4,12},{8,0},{12,4},{16,24},{20,28},{24,16},{28,20},{1,9},{5... | collective-permute-start | bytes 196616 | tf_op jit(solution)/shard_map/ppermute | solution.py:283
  5.0 10.4 %collective-permute-start = (bf16[32,2048]{1,0:T(8,128)(2,1)S(1)}, bf16[32,2048]{1,0:T(8,128)(2,1)S(1)}, u32[]{:S(2)}, u32[]{:S(2)}) collective-permute-start(bf16[32,2048]{1,0:T(8,128)(2,1)S(1)} %get-tuple-element.31), channel_id=1, source_target_pairs={{0,8},{1,17},{2,10},{3,19},{4,12},{5,21},{6,14},{7,23},{8,0},{9,25... | collective-permute-start | bytes 393224 | tf_op jit(solution)/shard_map/ppermute | solution.py:294
  6.6 9.2 %collective-permute-start.3 = (bf16[1024,128]{1,0:T(8,128)(2,1)S(1)}, bf16[1024,128]{1,0:T(8,128)(2,1)S(1)}, u32[]{:S(2)}, u32[]{:S(2)}) collective-permute-start(bf16[1024,128]{1,0:T(8,128)(2,1)S(1)} %copy-done.2), channel_id=1, source_target_pairs={{0,4},{4,0},{8,12},{12,8},{16,20},{20,16},{24,28},{28,24},{1,5},{5... | collective-permute-start | bytes 786440 | tf_op jit(solution)/shard_map/ppermute | solution.py:286
  8.1 12.3 %collective-permute-start.4 = (bf16[1024,128]{1,0:T(8,128)(2,1)S(1)}, bf16[1024,128]{1,0:T(8,128)(2,1)S(1)}, u32[]{:S(2)}, u32[]{:S(2)}) collective-permute-start(bf16[1024,128]{1,0:T(8,128)(2,1)S(1)} %copy-done.3), channel_id=1, source_target_pairs={{0,4},{4,0},{8,12},{12,8},{16,20},{20,16},{24,28},{28,24},{1,5},{5... | collective-permute-start | bytes 786440 | tf_op jit(solution)/shard_map/ppermute | solution.py:286
  8.6 6.7 %collective-permute-start.1 = (bf16[32,1024]{1,0:T(8,128)(2,1)S(1)}, bf16[32,1024]{1,0:T(8,128)(2,1)S(1)}, u32[]{:S(2)}, u32[]{:S(2)}) collective-permute-start(bf16[32,1024]{1,0:T(8,128)(2,1)S(1)} %get-tuple-element.32), channel_id=1, source_target_pairs={{0,24},{4,28},{8,16},{12,20},{16,8},{20,12},{24,0},{28,4},{1,25},{... | collective-permute-start | bytes 196616 | tf_op jit(solution)/shard_map/ppermute | solution.py:283
  11.2 14.7 %collective-permute-start.8 = (bf16[64,1024]{1,0:T(8,128)(2,1)S(1)}, bf16[64,1024]{1,0:T(8,128)(2,1)S(1)}, u32[]{:S(2)}, u32[]{:S(2)}) collective-permute-start(bf16[64,1024]{1,0:T(8,128)(2,1)S(1)} %maximum_select_fusion), channel_id=1, source_target_pairs={{0,16},{4,20},{8,24},{12,28},{16,0},{20,4},{24,8},{28,12},{1,17},{... | collective-permute-start | bytes 393224 | tf_op jit(solution)/shard_map/ppermute | solution.py:283
  15.4 5.1 %collective-permute-start.2 = (bf16[32,3072]{1,0:T(8,128)(2,1)S(1)}, bf16[32,3072]{1,0:T(8,128)(2,1)S(1)}, u32[]{:S(2)}, u32[]{:S(2)}) collective-permute-start(bf16[32,3072]{1,0:T(8,128)(2,1)S(1)} %pad_maximum_fusion), channel_id=1, source_target_pairs={{0,1},{1,0},{2,3},{3,2},{4,5},{5,4},{6,7},{7,6},{8,9},{9,8},{10,11... | collective-permute-start | bytes 589832 | tf_op jit(solution)/shard_map/ppermute | solution.py:289
  20.9 5.1 %collective-permute-start.9 = (bf16[128,256]{1,0:T(8,128)(2,1)S(1)}, bf16[128,256]{1,0:T(8,128)(2,1)S(1)}, u32[]{:S(2)}, u32[]{:S(2)}) collective-permute-start(bf16[128,256]{1,0:T(8,128)(2,1)S(1)} %get-tuple-element.39), channel_id=1, source_target_pairs={{0,8},{4,12},{8,0},{12,4},{16,24},{20,28},{24,16},{28,20},{1,9},{5... | collective-permute-start | bytes 196616 | tf_op jit(solution)/shard_map/ppermute | solution.py:283
  22.2 6.6 %collective-permute-start.12 = (bf16[128,256]{1,0:T(8,128)(2,1)S(1)}, bf16[128,256]{1,0:T(8,128)(2,1)S(1)}, u32[]{:S(2)}, u32[]{:S(2)}) collective-permute-start(bf16[128,256]{1,0:T(8,128)(2,1)S(1)} %get-tuple-element.39), channel_id=1, source_target_pairs={{0,24},{4,28},{8,16},{12,20},{16,8},{20,12},{24,0},{28,4},{1,25},{... | collective-permute-start | bytes 196616 | tf_op jit(solution)/shard_map/ppermute | solution.py:283
  22.9 8.0 %collective-permute-start.11 = (bf16[128,256]{1,0:T(8,128)(2,1)S(1)}, bf16[128,256]{1,0:T(8,128)(2,1)S(1)}, u32[]{:S(2)}, u32[]{:S(2)}) collective-permute-start(bf16[128,256]{1,0:T(8,128)(2,1)S(1)} %get-tuple-element.39), channel_id=1, source_target_pairs={{0,16},{4,20},{8,24},{12,28},{16,0},{20,4},{24,8},{28,12},{1,17},{... | collective-permute-start | bytes 196616 | tf_op jit(solution)/shard_map/ppermute | solution.py:283
  24.4 8.1 %collective-permute-start.5 = (bf16[128,1024]{1,0:T(8,128)(2,1)S(1)}, bf16[128,1024]{1,0:T(8,128)(2,1)S(1)}, u32[]{:S(2)}, u32[]{:S(2)}) collective-permute-start(bf16[128,1024]{1,0:T(8,128)(2,1)S(1)} %get-tuple-element.36), channel_id=1, source_target_pairs={{0,4},{4,0},{8,12},{12,8},{16,20},{20,16},{24,28},{28,24},{1,5},{5... | collective-permute-start | bytes 786440 | tf_op jit(solution)/shard_map/ppermute | solution.py:286
  25.9 9.4 %collective-permute-start.10 = (bf16[64,1024]{1,0:T(8,128)(2,1)S(1)}, bf16[64,1024]{1,0:T(8,128)(2,1)S(1)}, u32[]{:S(2)}, u32[]{:S(2)}) collective-permute-start(bf16[64,1024]{1,0:T(8,128)(2,1)S(1)} %collective-permute-done.8.refs_4_), channel_id=1, source_target_pairs={{0,8},{4,12},{8,0},{12,4},{16,24},{20,28},{24,16},{28,20},{1,9},{5... | collective-permute-start | bytes 393224 | tf_op jit(solution)/shard_map/ppermute | solution.py:283
  31.0 4.3 %collective-permute-start.13 = (bf16[128,256]{1,0:T(8,128)(2,1)S(1)}, bf16[128,256]{1,0:T(8,128)(2,1)S(1)}, u32[]{:S(2)}, u32[]{:S(2)}) collective-permute-start(bf16[128,256]{1,0:T(8,128)(2,1)S(1)} %add_convert_fusion.refs_6_), channel_id=1, source_target_pairs={{0,4},{4,0},{8,12},{12,8},{16,20},{20,16},{24,28},{28,24},{1,5},{5... | collective-permute-start | bytes 196616 | tf_op jit(solution)/shard_map/ppermute | solution.py:286
  36.6 4.3 %collective-permute-start.14 = (bf16[128,256]{1,0:T(8,128)(2,1)S(1)}, bf16[128,256]{1,0:T(8,128)(2,1)S(1)}, u32[]{:S(2)}, u32[]{:S(2)}) collective-permute-start(bf16[128,256]{1,0:T(8,128)(2,1)S(1)} %get-tuple-element.43), channel_id=1, source_target_pairs={{0,4},{4,0},{8,12},{12,8},{16,20},{20,16},{24,28},{28,24},{1,5},{5... | collective-permute-start | bytes 196616 | tf_op jit(solution)/shard_map/ppermute | solution.py:286
  41.7 1.6 %collective-permute-start.16 = (bf16[64,2048]{1,0:T(8,128)(2,1)S(1)}, bf16[64,2048]{1,0:T(8,128)(2,1)S(1)}, u32[]{:S(2)}, u32[]{:S(2)}) collective-permute-start(bf16[64,2048]{1,0:T(8,128)(2,1)S(1)} %get-tuple-element.47), channel_id=1, source_target_pairs={{0,1},{1,0},{2,3},{3,2},{4,5},{5,4},{6,7},{7,6},{8,9},{9,8},{10,11... | collective-permute-start | bytes 786440 | tf_op jit(solution)/shard_map/ppermute | solution.py:289
  43.4 8.8 %collective-permute-start.18 = (bf16[32,2048]{1,0:T(8,128)(2,1)S(1)}, bf16[32,2048]{1,0:T(8,128)(2,1)S(1)}, u32[]{:S(2)}, u32[]{:S(2)}) collective-permute-start(bf16[32,2048]{1,0:T(8,128)(2,1)S(1)} %get-tuple-element.54), channel_id=1, source_target_pairs={{0,8},{1,24},{2,0},{3,16},{4,12},{5,28},{6,4},{7,20},{8,9},{9,25},... | collective-permute-start | bytes 393224 | tf_op jit(solution)/shard_map/ppermute | solution.py:294
  43.9 10.2 %collective-permute-start.17 = (bf16[32,2048]{1,0:T(8,128)(2,1)S(1)}, bf16[32,2048]{1,0:T(8,128)(2,1)S(1)}, u32[]{:S(2)}, u32[]{:S(2)}) collective-permute-start(bf16[32,2048]{1,0:T(8,128)(2,1)S(1)} %get-tuple-element.48), channel_id=1, source_target_pairs={{0,0},{1,16},{2,8},{3,24},{4,4},{5,20},{6,12},{7,28},{8,1},{9,17},... | collective-permute-start | bytes 393224 | tf_op jit(solution)/shard_map/ppermute | solution.py:294
  45.8 4.3 %collective-permute-start.15 = (bf16[128,256]{1,0:T(8,128)(2,1)S(1)}, bf16[128,256]{1,0:T(8,128)(2,1)S(1)}, u32[]{:S(2)}, u32[]{:S(2)}) collective-permute-start(bf16[128,256]{1,0:T(8,128)(2,1)S(1)} %get-tuple-element.44.refs_2_), channel_id=1, source_target_pairs={{0,4},{4,0},{8,12},{12,8},{16,20},{20,16},{24,28},{28,24},{1,5},{5... | collective-permute-start | bytes 196616 | tf_op jit(solution)/shard_map/ppermute | solution.py:286
